TPU v7x, 256 devices: a whole 4x4x8 slice. The times are simulated.
256 devices in a mesh: pop: 16 (over z, core), mp: 16 (over y, x).
Axes of the slice: x: 4, y: 4, z: 8, core: 2. Of those that a mesh axis runs over, the one named last changes fastest.
Arguments:
- tokens: bfloat16 [16384, 3584], P('pop', 'mp'), may hold values from -6 to 6
- target: bfloat16 [16384, 10240], P('pop', 'mp'), may hold values from -6 to 6
- unit_weight: float32 [10240], P('mp'), may hold values from 0.2 to 5
- gate_weight: bfloat16 [3584, 10240], P(None, 'mp'), may hold values from -0.09375 to 0.09375
- up_weight: bfloat16 [3584, 10240], P(None, 'mp'), may hold values from -0.09375 to 0.09375
- seeds: int32 [256], replicated, may hold values from 0 to 1073741823
Outputs:
- update_gate: float32 [3584, 10240], P('pop', 'mp')
- update_up: float32 [3584, 10240], P('pop', 'mp')
- fitness: float32 [512], P('pop')
Inputs may be any that keep to these rules, and one draw needn't show every extreme that they name: seeds are independent integers, one for each antithetic pair.
All inputs are finite; a program needn't handle non-finite values.
Results may differ from a plain program's by a relative error of at most 0.0003.
Values may be sent and summed in bfloat16 or wider, within the bound.
No kernel may reach another device: no remote copies, remote signals or barrier semaphores. Data moves between devices by JAX's collectives and lax.ppermute only.
A program may use at most 128 MiB of HBM per device.

v0:
```python
import math

import jax
import jax.numpy as jnp
from jax import lax
from jax.sharding import PartitionSpec as P

FF = 10240
ROWS = 64


SIGMA = 0.5
EPSILON = 1e-05


def levels(seed_values, positions, columns, marker):
    mixed = seed_values * 747796405 + (positions * 4 + columns) * 277803737 + marker
    mixed = jnp.bitwise_xor(mixed, jnp.right_shift(mixed, 15))
    mixed = mixed * 1664525 + 1013904223
    mixed = jnp.bitwise_xor(mixed, jnp.right_shift(mixed, 13))
    return (2 * jnp.bitwise_and(mixed, 255) - 255).astype(jnp.float32) / 256.0


def factor_table(seed_list, first_row, row_count, marker):
    positions = (first_row + jnp.arange(row_count, dtype=jnp.int32))[None, :, None]
    corner = jnp.arange(4, dtype=jnp.int32)[None, None, :]
    return levels(seed_list[:, None, None], positions, corner, marker)


def on_device(tokens, target, unit_weight, gate_weight, up_weight, seeds):
    rows_dev = tokens.shape[0]
    pairs_dev = rows_dev // ROWS
    model_width = gate_weight.shape[0]
    hidden_local = gate_weight.shape[1]
    pop_count = lax.axis_size("pop")
    pair_total = seeds.shape[0]
    pop_index = lax.axis_index("pop")
    model_index = lax.axis_index("mp")
    local_seeds = lax.dynamic_slice_in_dim(seeds, pop_index * pairs_dev, pairs_dev)
    hidden_first = model_index * hidden_local
    gate_output = factor_table(local_seeds, hidden_first, hidden_local, 22013)
    up_output = factor_table(local_seeds, hidden_first, hidden_local, 44041)
    portion = lax.all_gather(tokens, "mp", axis=1, tiled=True)
    offset = jnp.int32(0)
    width = portion.shape[1]
    in_both = jnp.concatenate(
        [
            factor_table(local_seeds, offset, width, 11003),
            factor_table(local_seeds, offset, width, 33023),
        ],
        axis=2,
    ).astype(jnp.bfloat16)
    grouped = portion.reshape(pairs_dev, ROWS, width)
    low_rank_portion = jnp.einsum(
        "prk,pkc->prc", grouped, in_both, preferred_element_type=jnp.float32
    )
    base_gate = jnp.dot(portion, gate_weight, preferred_element_type=jnp.float32)
    base_up = jnp.dot(portion, up_weight, preferred_element_type=jnp.float32)
    scale = SIGMA / math.sqrt(model_width)
    side_gate = (
        jnp.einsum(
            "dbw,diw->dbi", low_rank_portion[:, :, :4], gate_output, precision=lax.Precision.HIGHEST
        )
        * scale
    )
    side_up = (
        jnp.einsum(
            "dbw,diw->dbi", low_rank_portion[:, :, 4:], up_output, precision=lax.Precision.HIGHEST
        )
        * scale
    )
    base_gate = base_gate.reshape(pairs_dev, ROWS, hidden_local)
    base_up = base_up.reshape(pairs_dev, ROWS, hidden_local)
    goal = target.reshape(pairs_dev, ROWS, hidden_local).astype(jnp.float32)
    parts_list = []
    for sign in (1.0, -1.0):
        hidden = jax.nn.silu(base_gate + sign * side_gate) * (base_up + sign * side_up)
        parts_list.append(jnp.sum(unit_weight * (hidden - goal) ** 2, axis=(1, 2)))
    parts = jnp.stack(parts_list, axis=1).reshape(-1) / (ROWS * FF)
    summed = lax.psum(parts, "mp")
    errors = lax.all_gather(summed, "pop", axis=0, tiled=True)
    scores = -errors
    center = jnp.mean(scores)
    spread = jnp.mean((scores - center) ** 2)
    fitness = (scores - center) / jnp.sqrt(spread + EPSILON)
    pair_weight = (fitness[0::2] - fitness[1::2]) / 2.0
    factor = pair_weight / math.sqrt(pair_total)
    block_rows = model_width // pop_count
    block_first = pop_index * block_rows
    every_factor = factor[:, None, None]
    left_factor_gate = factor_table(seeds, block_first, block_rows, 11003) * every_factor
    left_factor_up = factor_table(seeds, block_first, block_rows, 33023) * every_factor
    right_gate = factor_table(seeds, hidden_first, hidden_local, 22013)
    right_up = factor_table(seeds, hidden_first, hidden_local, 44041)
    update_gate = jnp.einsum(
        "eiy,ety->it", left_factor_gate, right_gate, precision=lax.Precision.HIGHEST
    )
    update_up = jnp.einsum("eiy,ety->it", left_factor_up, right_up, precision=lax.Precision.HIGHEST)
    local_fitness = lax.dynamic_slice_in_dim(fitness, pop_index * 2 * pairs_dev, 2 * pairs_dev)
    return (update_gate, update_up, local_fitness)


def solution(mesh):
    return jax.shard_map(
        on_device,
        mesh=mesh,
        in_specs=(P("pop", "mp"), P("pop", "mp"), P("mp"), P(None, "mp"), P(None, "mp"), P()),
        out_specs=(P("pop", "mp"), P("pop", "mp"), P("pop")),
        check_vma=False,
    )
```

profile of v0, /device:TPU:1, one launch (start us, length us, event | category | flops | bytes accessed | tf_op | source)
XLA Modules:
  0.0 206.9 jit_solution(6900600368546894270)
XLA Ops:
  7.2 0.0 all-gather.2.cloned.1.call-start
  7.2 0.7 all-gather.2.cloned.1.call-update
  7.9 1.3 dynamic-slice
  9.8 0.8 dynamic-slice_multiply_fusion
  10.6 0.7 broadcast_multiply_fusion
  11.3 0.2 fusion.113
  11.5 0.8 fusion.67
  12.4 0.1 pad_maximum_fusion
  12.5 73.0 %all-gather.2.cloned.1.call-done = bf16[1024,3584]{0,1:T(8,128)(2,1)} async-done(((bf16[1024,224]{0,1:T(8,128)(2,1)}), bf16[1024,3584]{0,1:T(8,128)(2,1)}) %all-gather.2.cloned.1.call-update) | async-done | bytes 7340048 | tf_op jit(solution)/shard_map/all_gather | solution.py:43
  85.4 10.1 %copy.13 = bf16[1024,3584]{1,0:T(8,128)(2,1)} copy(bf16[1024,3584]{0,1:T(8,128)(2,1)} %all-gather.2.cloned.1.call-done) | data formatting | bytes 14680064 | tf_op jit(solution)/shard_map/all_gather | solution.py:43
  95.5 0.0 copy-start
  95.5 5.2 %convolution_bitcast_fusion = f32[16,64,8]{1,2,0:T(8,128)S(1)} fusion(bf16[16,64,3584]{2,1,0:T(8,128)(2,1)} %bitcast.19, bf16[16,3584,8]{1,0,2:T(8,128)(2,1)S(1)} %pad_maximum_fusion), kind=kOutput, calls=%fused_computation.66 | convolution fusion | flops 58720256 | bytes 8290304 | tf_op jit(solution)/shard_map/prk,pkc->prc/dot_general | solution.py:54
  100.7 0.0 slice-start
  100.7 2.7 %fusion.123 = f32[16,64,640]{2,1,0:T(8,128)S(1)} fusion(f32[16,640,4]{1,0,2:T(8,128)S(1)} %get-tuple-element.7, f32[16,64,8]{1,2,0:T(8,128)S(1)} %convolution_bitcast_fusion), kind=kOutput, calls=%fused_computation.143 | convolution fusion | flops 31457280 | bytes 2818048 | tf_op jit(solution)/shard_map/dbw,diw->dbi/dot_general | solution.py:61
  103.4 0.0 copy-done
  103.4 0.0 slice-start.1
  103.4 8.6 %fusion.148 = f32[1024,640]{1,0:T(8,128)S(1)} fusion(bf16[1024,3584]{0,1:T(8,128)(2,1)S(1)} %copy-done, bf16[3584,640]{1,0:T(8,128)(2,1)} %param.9), kind=kOutput, calls=%fused_computation.180 | convolution fusion | flops 4697620480 | bytes 14548992 | tf_op jit(solution)/shard_map/dot_general | solution.py:57
  112.1 0.0 slice-done
  112.1 0.0 slice-done.1
  112.1 0.0 copy-start.1
  112.1 0.0 copy-start.2
  112.1 6.5 %fusion.149 = f32[1024,640]{1,0:T(8,128)S(1)} fusion(bf16[1024,3584]{0,1:T(8,128)(2,1)S(1)} %copy-done, bf16[3584,640]{1,0:T(8,128)(2,1)S(1)} %bitcast.23), kind=kOutput, calls=%fused_computation.181 | convolution fusion | flops 4697620480 | bytes 14548992 | tf_op jit(solution)/shard_map/dot_general | solution.py:58
  118.6 0.0 copy-done.1
  118.6 0.0 copy-done.2
  118.6 5.4 %fusion.2 = (f32[16]{0:T(128)S(1)}, f32[16]{0:T(128)S(1)}) fusion(bf16[16,64,640]{2,1,0:T(8,128)(2,1)S(1)} %bitcast.24, f32[16,64,640]{2,1,0:T(8,128)S(1)} %bitcast.26, f32[16,64,640]{2,1,0:T(8,128)S(1)} %bitcast.25, f32[16,64,640]{2,1,0:T(8,128)S(1)} %fusion.123, f32[640]{0:T(1024)S(1)} %copy-done.2, f32[16,640,4]{1,0,2:T(8,128)S(1)} %get-tuple-element.8, ...), kind=kOutput, calls=%fused_computation.10 | convolution fusion | flops 49151968 | bytes 9375872 | tf_op jit(solution)/shard_map/dbw,diw->dbi/dot_general | solution.py:67
  124.1 0.1 copy.17
  124.2 0.1 div.59
  124.3 31.2 %psum.7 = f32[32]{0:T(128)S(1)} all-reduce(f32[32]{0:T(128)S(1)} %div.59), channel_id=1, replica_groups=mesh['pop'=16,'mp'=16] {'mp'}, use_global_device_ids=true, to_apply=%region_2.3 | all-reduce | flops 32 | bytes 256 | tf_op jit(solution)/shard_map/psum | solution.py:80
  155.5 0.2 dynamic-update-slice
  155.7 31.3 %all-reduce = f32[512]{0:T(512)S(1)} all-reduce(f32[512]{0:T(512)S(1)} %dynamic-update-slice), channel_id=1, replica_groups=mesh['pop'=16,'mp'=16] {'pop'}, use_global_device_ids=true, to_apply=%add | all-reduce | flops 512 | bytes 4096
  186.9 0.6 reduce_sum.38
  188.2 0.6 multiply_reduce_fusion
  189.5 0.2 slice.14
  189.7 0.2 slice.15
  190.0 4.7 %fusion.46 = f32[224,640]{1,0:T(8,128)} fusion(s32[640,4]{0,1:T(4,128)S(1)} %add_multiply_fusion.1, s32[256]{0:T(256)S(1)} %broadcast_multiply_fusion, f32[256]{0:T(256)S(1)} %subtract_multiply_fusion, s32[224,4]{0,1:T(4,128)S(1)} %add_multiply_fusion.3), kind=kOutput, calls=%fused_computation.64 | convolution fusion | flops 1773109248 | bytes 589312 | tf_op jit(solution)/shard_map/eiy,ety->it/dot_general | solution.py:98
  194.7 4.7 %fusion.49 = f32[224,640]{1,0:T(8,128)} fusion(s32[640,4]{0,1:T(4,128)S(1)} %add_multiply_fusion.1, s32[256]{0:T(256)S(1)} %broadcast_multiply_fusion, f32[256]{0:T(256)S(1)} %subtract_multiply_fusion, s32[224,4]{0,1:T(4,128)S(1)} %add_multiply_fusion.3), kind=kOutput, calls=%fused_computation.65 | convolution fusion | flops 1773109248 | bytes 589312 | tf_op jit(solution)/shard_map/eiy,ety->it/dot_general | solution.py:95
  199.4 0.6 dynamic_slice.7
  (11 shorter events, 0.1 us)
Async XLA Ops:
  7.2 78.3 %all-gather.2.cloned.1.call-start = ((), (), s32[]{:S(2)}) async-start(), calls=%async_computation | async-start | bytes 7798784 | tf_op jit(solution)/shard_map/all_gather | solution.py:43
  95.5 7.9 %copy-start = (bf16[1024,3584]{0,1:T(8,128)(2,1)S(1)}, bf16[1024,3584]{0,1:T(8,128)(2,1)}, u32[]{:S(2)}) copy-start(bf16[1024,3584]{0,1:T(8,128)(2,1)} %all-gather.2.cloned.1.call-done) | copy-start | bytes 22020100
  100.7 11.3 %slice-start = ((s8[4587520]{0:T(1024)(128)(4,1)}), s8[4194304]{0:T(1024)(128)(4,1)S(1)}, s32[]{:S(2)}) async-start(s8[4587520]{0:T(1024)(128)(4,1)} %bitcast.22), calls=%async_computation.1 | async-start | bytes 8388608
  103.4 8.7 %slice-start.1 = ((s8[4587520]{0:T(1024)(128)(4,1)}), s8[393216]{0:T(1024)(128)(4,1)S(1)}, s32[]{:S(2)}) async-start(s8[4587520]{0:T(1024)(128)(4,1)} %bitcast.22), calls=%async_computation.2 | async-start | bytes 786432
  112.1 6.5 %copy-start.1 = (bf16[1024,640]{1,0:T(8,128)(2,1)S(1)}, bf16[1024,640]{1,0:T(8,128)(2,1)}, u32[]{:S(2)}) copy-start(bf16[1024,640]{1,0:T(8,128)(2,1)} %param.7) | copy-start | bytes 3932164
  112.1 6.5 %copy-start.2 = (f32[640]{0:T(1024)S(1)}, f32[640]{0:T(1024)}, u32[]{:S(2)}) copy-start(f32[640]{0:T(1024)} %param.8) | copy-start | bytes 7684
Sparse Core Ops, SparseCore 0:
  10.4 74.9 all-gather.1
where the time goes:
time: 207 us
  waiting for transfers between devices  73.6 us (36%)
  blocking collectives  62.5 us (30%)
  matrix products  37.9 us (18%)
  between operations  16.2 us (8%)
  local copies, waits for them, and re-layouts  12.8 us (6%)
  other arithmetic  3.84 us (2%)
    all_gather x1, waiting for transfers between devices, on_device(): portion = lax.all_gather(tokens, 'mp', axis=1, tiled=True)  73 us
    unnamed x1, blocking collectives  31.3 us
    psum x1, blocking collectives, on_device(): summed = lax.psum(parts, 'mp')  31.2 us
    all_gather x1, local copies, waits for them, and re-layouts, on_device(): portion = lax.all_gather(tokens, 'mp', axis=1, tiled=True)  10.1 us
    dot_general x1, matrix products, on_device(): jnp.dot(portion, gate_weight, preferred_element_type=jnp.float32)  8.63 us
    dot_general x1, matrix products, on_device(): base_up = jnp.dot(portion, up_weight, preferred_element_type=jnp.float32)  6.5 us
    dot_general x1, matrix products, on_device(): jnp.einsum('dbw,diw->dbi', low_rank_portion[:, :, 4:], up_output, precisi...  5.42 us
    dot_general x1, matrix products, on_device(): jnp.einsum('prk,pkc->prc', grouped, in_both, preferred_element_type=jnp.f...  5.22 us
  transfers between devices with their start and end apart: 1, of which 1 were waited for; matrix products, arithmetic and copies ran while one was open for 2% of the time, Pallas kernels for 0%

commit v1 on v0

v1 whole, which is shorter than its diff:
```python
import math

import jax
import jax.numpy as jnp
from jax import lax
from jax.experimental import pallas as pl
from jax.experimental.pallas import tpu as pltpu
from jax.sharding import PartitionSpec as P

FF = 10240
ROWS = 64
SIGMA = 0.5
EPSILON = 1e-05
SEED_STEP = 747796405
CELL_STEP = 277803737
VMEM = 48 * 1024 * 1024

WAYS = {"+x": (1, 0), "-x": (3, 0), "+y": (0, 1), "-y": (0, 3)}
STEPS = (
    (((0, 0), "+x"), ((0, 0), "-x"), ((0, 0), "+y"), ((0, 0), "-y")),
    (((0, 1), "+x"), ((0, 3), "-x"), ((3, 0), "+y"), ((1, 0), "-y")),
    (((1, 0), "+x"), ((3, 1), "-x"), ((0, 1), "+y"), ((3, 3), "-y")),
    (((1, 3), "+x"), ((1, 1), "+y"), ((3, 2), "-x")),
)


def moved(place, way):
    return ((place[0] + WAYS[way][0]) % 4, (place[1] + WAYS[way][1]) % 4)


def pairs_of(way):
    dx, dy = WAYS[way]
    return [(y * 4 + x, (y + dy) % 4 * 4 + (x + dx) % 4) for y in range(4) for x in range(4)]


def source_of(place):
    me = lax.axis_index("mp")
    return lax.rem(me // 4 + 4 - place[1], 4) * 4 + lax.rem(lax.rem(me, 4) + 4 - place[0], 4)


def levels_of(mixed):
    mixed = jnp.bitwise_xor(mixed, jnp.right_shift(mixed, 15))
    mixed = mixed * 1664525 + 1013904223
    mixed = jnp.bitwise_xor(mixed, jnp.right_shift(mixed, 13))
    level = (2 * jnp.bitwise_and(mixed, 255) - 255).astype(jnp.float32) * (1.0 / 256.0)
    return level.astype(jnp.bfloat16)


def iota(shape, dim):
    return lax.broadcasted_iota(jnp.int32, shape, dim)


def in_table_kernel(lane_ref, out_ref):
    rows = 64

    @pl.loop(0, out_ref.shape[0] // rows)
    def _(i):
        at = pl.multiple_of(i * rows, rows)
        cell = (iota((rows, 128), 0) + at) * (4 * CELL_STEP)
        out_ref[pl.ds(at, rows), :] = levels_of(lane_ref[...] + cell)


def out_table_kernel(column_ref, gate_ref, up_ref, right_gate_ref, right_up_ref):
    width = right_gate_ref.shape[1]
    first = lax.axis_index("mp") * width
    rows = 16
    cell = (iota((rows, width), 1) + first) * (4 * CELL_STEP)

    @pl.loop(0, right_gate_ref.shape[0] // rows)
    def _(i):
        at = pl.multiple_of(i * rows, rows)
        right_gate_ref[pl.ds(at, rows), :] = levels_of(column_ref[pl.ds(at, rows), 0:1] + cell)
        right_up_ref[pl.ds(at, rows), :] = levels_of(column_ref[pl.ds(at, rows), 1:2] + cell)

    mine = lax.axis_index("pop") * 64
    for half in (0, 128):
        gate_ref[half + 0 : half + 64, :] = right_gate_ref[pl.ds(mine, 64), :]
        gate_ref[half + 64 : half + 128, :] = jnp.zeros((64, width), jnp.bfloat16)
        up_ref[half + 0 : half + 64, :] = jnp.zeros((64, width), jnp.bfloat16)
        up_ref[half + 64 : half + 128, :] = right_up_ref[pl.ds(mine, 64), :]


def left_table_kernel(lane_ref, left_gate_ref, left_up_ref):
    rows = 16
    count, width = left_gate_ref.shape
    first = lax.axis_index("pop") * count

    @pl.loop(0, count // rows)
    def _(i):
        at = pl.multiple_of(i * rows, rows)
        cell = (iota((rows, width), 0) + (at + first)) * (4 * CELL_STEP)
        left_gate_ref[pl.ds(at, rows), :] = levels_of(lane_ref[0:1, :] + cell)
        left_up_ref[pl.ds(at, rows), :] = levels_of(lane_ref[1:2, :] + cell)


def contract(a, b):
    return lax.dot_general(a, b, (((0,), (0,)), ((), ())), preferred_element_type=jnp.float32)


def block_copies(places, blocks, gate_ref, up_ref, table_ref, x_ref, w_ref, sems):
    depth = blocks[0].shape[0]
    width = gate_ref.shape[1]
    copies = []
    for i, (place, block) in enumerate(zip(places, blocks)):
        rows = pl.ds(source_of(place) * depth, depth)
        mine = pl.ds(i * depth, depth)
        copies.append(
            [
                pltpu.make_async_copy(block, x_ref.at[mine, :], sems.at[4 * i]),
                pltpu.make_async_copy(gate_ref.at[rows, :], w_ref.at[mine, pl.ds(0, width)], sems.at[4 * i + 1]),
                pltpu.make_async_copy(up_ref.at[rows, :], w_ref.at[mine, pl.ds(width, width)], sems.at[4 * i + 2]),
                pltpu.make_async_copy(table_ref.at[rows, :], w_ref.at[mine, pl.ds(2 * width, 128)], sems.at[4 * i + 3]),
            ]
        )
    return copies


def first_kernel(places, slabs, *refs):
    n = len(places)
    blocks, (gate_ref, up_ref, table_ref, acc_ref, x_ref, w_ref, sems) = refs[:n], refs[n:]
    depth = blocks[0].shape[0]
    copies = block_copies(places, blocks, gate_ref, up_ref, table_ref, x_ref, w_ref, sems)
    for group in copies:
        for copy in group:
            copy.start()
    done = 0
    for slab in slabs:
        for group in copies[done : done + slab]:
            for copy in group:
                copy.wait()
        low, high = done * depth, (done + slab) * depth

        @pl.loop(0, acc_ref.shape[0] // 256)
        def _(i):
            rows = pl.ds(pl.multiple_of(i * 256, 256), 256)
            part = contract(x_ref[low:high, rows], w_ref[low:high, :])
            if low == 0:
                acc_ref[rows, :] = part
            else:
                acc_ref[rows, :] += part

        done += slab


def last_kernel(places, *refs):
    n = len(places)
    blocks = refs[:n]
    gate_ref, up_ref, table_ref, acc_ref, target_ref, weight_ref, gate_out_ref, up_out_ref = refs[n : n + 8]
    message_ref, x_ref, w_ref, a_ref, t_ref, total_ref, side_ref, parts_ref, sems, a_sems, t_sems = refs[n + 8 :]
    width = gate_ref.shape[1]
    tile = 256
    tiles = acc_ref.shape[0] // tile
    copies = block_copies(places, blocks, gate_ref, up_ref, table_ref, x_ref, w_ref, sems)
    for group in copies:
        for copy in group:
            copy.start()
    for i in range(tiles):
        rows = pl.ds(i * tile, tile)
        pltpu.make_async_copy(acc_ref.at[rows, :], a_ref.at[rows, :], a_sems.at[i]).start()
        pltpu.make_async_copy(target_ref.at[rows, :], t_ref.at[rows, :], t_sems.at[i]).start()
    for group in copies:
        for copy in group:
            copy.wait()
    scale = SIGMA / math.sqrt(16 * blocks[0].shape[0])
    lane_pair = lax.rem(iota((tile, 128), 1), 64) // 4
    row_pair = iota((tile, 128), 0) // ROWS

    @pl.loop(0, tiles)
    def _(i):
        rows = pl.ds(pl.multiple_of(i * tile, tile), tile)
        pltpu.make_async_copy(acc_ref.at[rows, :], a_ref.at[rows, :], a_sems.at[i]).wait()
        pltpu.make_async_copy(target_ref.at[rows, :], t_ref.at[rows, :], t_sems.at[i]).wait()
        part = contract(x_ref[:, rows], w_ref[...]) + a_ref[rows, :]
        total_ref[...] = part[:, : 2 * width]
        low = jnp.where(lane_pair == row_pair + i * (tile // ROWS), part[:, 2 * width :] * scale, 0.0)
        high = low.astype(jnp.bfloat16)
        rest = (low - high.astype(jnp.float32)).astype(jnp.bfloat16)
        low_both = jnp.concatenate([high, rest], axis=1)
        side_ref[:, :width] = jnp.dot(low_both, gate_out_ref[...], preferred_element_type=jnp.float32)
        side_ref[:, width:] = jnp.dot(low_both, up_out_ref[...], preferred_element_type=jnp.float32)

        @pl.loop(0, tile // ROWS)
        def _(p):
            plus = jnp.zeros((8, width), jnp.float32)
            minus = jnp.zeros((8, width), jnp.float32)
            for q in range(ROWS // 16):
                at16 = pl.multiple_of(p * ROWS + q * 16, 16)
                goals = t_ref[pl.ds(pl.multiple_of(i * tile + at16, 16), 16), :].astype(jnp.float32)
                for h in range(2):
                    here = pl.ds(pl.multiple_of(at16 + h * 8, 8), 8)
                    goal = goals[h * 8 : h * 8 + 8, :]
                    gate, up = total_ref[here, :width], total_ref[here, width:]
                    side_gate, side_up = side_ref[here, :width], side_ref[here, width:]
                    half = 0.5 * (gate + side_gate)
                    error = (half * jnp.tanh(half) + half) * (up + side_up) - goal
                    plus += error * error
                    half = 0.5 * (gate - side_gate)
                    error = (half * jnp.tanh(half) + half) * (up - side_up) - goal
                    minus += error * error
            k = i * (tile // ROWS) + p
            parts_ref[0, pl.ds(k, 1), :] = jnp.sum(plus, axis=0, keepdims=True) * weight_ref[...]
            parts_ref[1, pl.ds(k, 1), :] = jnp.sum(minus, axis=0, keepdims=True) * weight_ref[...]

    odd = lax.rem(lax.axis_index("pop"), 2)
    pairs = parts_ref.shape[1]
    lane = iota((pairs, 128), 1)
    keep = lane // 4 == iota((pairs, 128), 0) + odd * 16
    lines = []
    for s in range(2):
        sums = jnp.sum(parts_ref[s], axis=1, keepdims=True) * (1.0 / (ROWS * FF))
        lines.append(jnp.sum(jnp.where(keep, sums, 0.0), axis=0, keepdims=True))
    row = iota((8, 128), 0)
    both = jnp.where(lax.rem(row, 2) == 0, lines[0], lines[1])

    @pl.loop(0, message_ref.shape[0] // 8)
    def _(i):
        message_ref[pl.ds(pl.multiple_of(i * 8, 8), 8), :] = both


def update_kernel(message_ref, left_gate_ref, left_up_ref, right_gate_ref, right_up_ref, out_gate_ref, out_up_ref, fit_ref, f_ref):
    count = message_ref.shape[0]
    pick_row, pick = iota((16, count), 0), iota((16, count), 1)
    chosen = (pick // 64 == lax.rem(pick_row, 8)) & (lax.rem(pick, 2) == pick_row // 8)
    summed = jnp.dot(
        chosen.astype(jnp.float32),
        message_ref[...],
        precision=lax.Precision.HIGHEST,
        preferred_element_type=jnp.float32,
    )
    scores = -summed
    members = 4.0 * 512.0
    center = jnp.sum(scores) / members
    spread = jnp.sum((scores - center) ** 2) / members
    fitness = (scores - center) / jnp.sqrt(jnp.full((16, 128), spread + EPSILON, jnp.float32))
    f_ref[...] = fitness
    factor = (fitness[:8] - fitness[8:]) * (0.5 / 16.0)
    for left_ref, right_ref, out_ref in (
        (left_gate_ref, right_gate_ref, out_gate_ref),
        (left_up_ref, right_up_ref, out_up_ref),
    ):
        highs, rests = [], []
        for q in range(8):
            scaled = left_ref[:, q * 128 : (q + 1) * 128].astype(jnp.float32) * factor[q : q + 1, :]
            high = scaled.astype(jnp.bfloat16)
            highs.append(high)
            rests.append((scaled - high.astype(jnp.float32)).astype(jnp.bfloat16))
        out_ref[...] = jnp.dot(
            jnp.concatenate(highs, axis=1), right_ref[...], preferred_element_type=jnp.float32
        ) + jnp.dot(jnp.concatenate(rests, axis=1), right_ref[...], preferred_element_type=jnp.float32)
    pop = lax.axis_index("pop")
    mine = pop // 2
    lane, member = iota((128, 128), 0), iota((128, 128), 1)
    at = lane == lax.rem(pop, 2) * 64 + member // 2 * 4
    total = jnp.zeros((1, 128), jnp.float32)
    for s in range(2):
        line = jnp.broadcast_to(f_ref[pl.ds(mine + 8 * s, 1), :], (8, 128))
        select = (at & (lax.rem(member, 2) == s)).astype(jnp.float32)
        total += jnp.dot(line, select, precision=lax.Precision.HIGHEST, preferred_element_type=jnp.float32)[:1]
    fit_ref[...] = total[:, : fit_ref.shape[1]]


def params():
    return pltpu.CompilerParams(vmem_limit_bytes=VMEM)


def cost(flops, size):
    return pl.CostEstimate(flops=flops, bytes_accessed=size, transcendentals=0)


def on_device(tokens, target, unit_weight, gate_weight, up_weight, seeds):
    rows_dev, depth = tokens.shape
    model_width, width = gate_weight.shape
    pairs_dev = rows_dev // ROWS
    pair_total = seeds.shape[0]
    device_total = lax.axis_size("pop") * lax.axis_size("mp")
    any_space = pl.BlockSpec(memory_space=pl.ANY)
    in_vmem = pl.BlockSpec(memory_space=pltpu.VMEM)

    mine = tokens.T
    blocks = {(0, 0): mine}
    for step in STEPS:
        for place, way in step:
            blocks[moved(place, way)] = lax.ppermute(blocks[place], "mp", pairs_of(way))
    late = [moved(place, way) for place, way in STEPS[-1]]
    early = [place for place in blocks if place not in late]

    corner = jnp.tile(jnp.arange(4, dtype=jnp.int32) * CELL_STEP, pair_total)
    by_lane = jnp.repeat(seeds * SEED_STEP, 4) + corner
    local_lane = lax.dynamic_slice_in_dim(by_lane, lax.axis_index("pop") * pairs_dev * 4, pairs_dev * 4)
    in_lanes = jnp.concatenate([local_lane + 11003, local_lane + 33023])[None, :]
    left_lanes = jnp.stack([by_lane + 11003, by_lane + 33023])
    out_columns = jnp.stack([by_lane + 22013, by_lane + 44041], axis=1)

    bf16 = jnp.bfloat16
    table = pl.pallas_call(
        in_table_kernel,
        out_shape=jax.ShapeDtypeStruct((model_width, 128), bf16),
        in_specs=[in_vmem],
        out_specs=in_vmem,
        compiler_params=params(),
        cost_estimate=cost(2_000_000_000, 1_000_000),
        name="in_table",
    )(in_lanes)
    gate_out, up_out, right_gate, right_up = pl.pallas_call(
        out_table_kernel,
        out_shape=[jax.ShapeDtypeStruct((256, width), bf16)] * 2 + [jax.ShapeDtypeStruct((pair_total * 4, width), bf16)] * 2,
        in_specs=[in_vmem],
        out_specs=[in_vmem] * 4,
        compiler_params=params(),
        cost_estimate=cost(4_000_000_000, 3_000_000),
        name="out_table",
    )(out_columns)
    left_rows = model_width // lax.axis_size("pop")
    left_gate, left_up = pl.pallas_call(
        left_table_kernel,
        out_shape=[jax.ShapeDtypeStruct((left_rows, pair_total * 4), bf16)] * 2,
        in_specs=[in_vmem],
        out_specs=[in_vmem] * 2,
        compiler_params=params(),
        cost_estimate=cost(2_000_000_000, 1_000_000),
        name="left_table",
    )(left_lanes)

    columns = 2 * width + 128
    n = len(early)
    acc = pl.pallas_call(
        lambda *refs: first_kernel(early, (8, n - 8), *refs),
        out_shape=jax.ShapeDtypeStruct((rows_dev, columns), jnp.float32),
        in_specs=[any_space] * (n + 3),
        out_specs=in_vmem,
        scratch_shapes=[
            pltpu.VMEM((n * depth, rows_dev), bf16),
            pltpu.VMEM((n * depth, columns), bf16),
            pltpu.SemaphoreType.DMA((4 * n,)),
        ],
        compiler_params=params(),
        cost_estimate=cost(2 * rows_dev * n * depth * columns, 20_000_000),
        name="first_blocks",
    )(*[blocks[place] for place in early], gate_weight, up_weight, table)

    n = len(late)
    message = pl.pallas_call(
        lambda *refs: last_kernel(late, *refs),
        out_shape=jax.ShapeDtypeStruct((2 * device_total, 128), jnp.float32),
        in_specs=[any_space] * (n + 5) + [in_vmem] * 3,
        out_specs=in_vmem,
        scratch_shapes=[
            pltpu.VMEM((n * depth, rows_dev), bf16),
            pltpu.VMEM((n * depth, columns), bf16),
            pltpu.VMEM((rows_dev, columns), jnp.float32),
            pltpu.VMEM((rows_dev, width), bf16),
            pltpu.VMEM((256, 2 * width), jnp.float32),
            pltpu.VMEM((256, 2 * width), jnp.float32),
            pltpu.VMEM((2, pairs_dev, width), jnp.float32),
            pltpu.SemaphoreType.DMA((4 * n,)),
            pltpu.SemaphoreType.DMA((rows_dev // 256,)),
            pltpu.SemaphoreType.DMA((rows_dev // 256,)),
        ],
        compiler_params=params(),
        cost_estimate=cost(2 * rows_dev * n * depth * columns, 12_000_000),
        name="last_blocks",
    )(*[blocks[place] for place in late], gate_weight, up_weight, table, acc, target, unit_weight[None, :], gate_out, up_out)

    received = lax.all_to_all(message, ("pop", "mp"), 0, 0, tiled=True)

    update_gate, update_up, fitness = pl.pallas_call(
        update_kernel,
        out_shape=[jax.ShapeDtypeStruct((left_rows, width), jnp.float32)] * 2
        + [jax.ShapeDtypeStruct((1, 2 * pairs_dev), jnp.float32)],
        in_specs=[in_vmem] * 5,
        out_specs=[in_vmem] * 3,
        scratch_shapes=[pltpu.VMEM((16, 128), jnp.float32)],
        compiler_params=params(),
        cost_estimate=cost(1_200_000_000, 5_000_000),
        name="update",
    )(received, left_gate, left_up, right_gate, right_up)
    return (update_gate, update_up, fitness.reshape(2 * pairs_dev))


def solution(mesh):
    return jax.shard_map(
        on_device,
        mesh=mesh,
        in_specs=(P("pop", "mp"), P("pop", "mp"), P("mp"), P(None, "mp"), P(None, "mp"), P()),
        out_specs=(P("pop", "mp"), P("pop", "mp"), P("pop")),
        check_vma=False,
    )
```

time: 207 us -> 112 us (0.54)
  blocking collectives: 62.5 us -> 0 us
  waiting for transfers between devices: 73.6 us -> 29.5 us
  Pallas kernels: 0 us -> 41 us
  matrix products: 37.9 us -> 0 us
  starting transfers between devices: 0.04 us -> 35.6 us
  between operations: 16.2 us -> 0.89 us
  local copies, waits for them, and re-layouts: 12.8 us -> 3.65 us
  other arithmetic: 3.84 us -> 0.97 us
    all_gather x1 -> x0, waiting for transfers between devices: 73 us -> none  [on_device(): portion = lax.all_gather(tokens, 'mp', axis=1, tiled=True)]
    pallas_call x0 -> x6, Pallas kernels: none -> 41 us  [the longest x1 18 us: on_device(): pl.pallas_call(lambda *refs: first_kernel(early, (8, n - 8), *refs), out_...]
    dot_general x7 -> x0, matrix products: 37.9 us -> none  [the longest x1 8.63 us: on_device(): jnp.dot(portion, gate_weight, preferred_element_type=jnp.float32)]
    unnamed x1 -> x0, blocking collectives: 31.3 us -> none
    psum x1 -> x0, blocking collectives: 31.2 us -> none  [on_device(): summed = lax.psum(parts, 'mp')]
    ppermute x0 -> x15, starting transfers between devices: none -> 19.4 us  [on_device(): blocks[moved(place, way)] = lax.ppermute(blocks[place], 'mp', pairs_of(way))]
    all_to_all x0 -> x1, starting transfers between devices: none -> 16.3 us  [on_device(): received = lax.all_to_all(message, ('pop', 'mp'), 0, 0, tiled=True)]
    ppermute x0 -> x15, waiting for transfers between devices: none -> 15.7 us  [on_device(): blocks[moved(place, way)] = lax.ppermute(blocks[place], 'mp', pairs_of(way))]
  transfers between devices with their start and end apart: 1 -> 16, of which waited for: 1 -> 6; matrix products, arithmetic and copies ran while one was open for 2% -> 2% of each run, Pallas kernels for 0% -> 24%
where the time goes in v1:
time: 112 us
  Pallas kernels  41 us (37%)
  starting transfers between devices  35.6 us (32%)
  waiting for transfers between devices  29.5 us (26%)
  local copies, waits for them, and re-layouts  3.65 us (3%)
    ppermute x15, starting transfers between devices, on_device(): blocks[moved(place, way)] = lax.ppermute(blocks[place], 'mp', pairs_of(way))  19.4 us
    pallas_call x1, Pallas kernels, on_device(): pl.pallas_call(lambda *refs: first_kernel(early, (8, n - 8), *refs), out_...  18 us
    all_to_all x1, starting transfers between devices, on_device(): received = lax.all_to_all(message, ('pop', 'mp'), 0, 0, tiled=True)  16.3 us
    ppermute x15, waiting for transfers between devices, on_device(): blocks[moved(place, way)] = lax.ppermute(blocks[place], 'mp', pairs_of(way))  15.7 us
    all_to_all x1, waiting for transfers between devices, on_device(): received = lax.all_to_all(message, ('pop', 'mp'), 0, 0, tiled=True)  13.8 us
    pallas_call x1, Pallas kernels, on_device(): pl.pallas_call(lambda *refs: last_kernel(late, *refs), out_shape=jax.Shap...  10.9 us
    pallas_call x1, Pallas kernels, on_device(): pl.pallas_call(out_table_kernel, out_shape=[jax.ShapeDtypeStruct((256, wi...  6.89 us
    pallas_call x1, Pallas kernels, on_device(): pl.pallas_call(update_kernel, out_shape=[jax.ShapeDtypeStruct((left_rows,...  3 us
  transfers between devices with their start and end apart: 16, of which 6 were waited for; matrix products, arithmetic and copies ran while one was open for 2% of the time, Pallas kernels for 24%

profile of v1, /device:TPU:1, one launch (start us, length us, event | category | flops | bytes accessed | tf_op | source)
XLA Modules:
  0.0 111.5 jit_solution(7762409927666592521)
XLA Ops:
  0.6 0.0 copy-start.10
  0.6 3.6 %collective-permute-start.6 = (bf16[224,1024]{1,0:T(8,128)(2,1)}, bf16[224,1024]{1,0:T(8,128)(2,1)S(1)}, u32[]{:S(2)}, u32[]{:S(2)}) collective-permute-start(bf16[224,1024]{1,0:T(8,128)(2,1)} %bitcast.7), channel_id=1, source_target_pairs={{0,12},{1,13},{2,14},{3,15},{4,0},{5,1},{6,2},{7,3},{8,4},{9,5},{1... | collective-permute-start | bytes 1376264 | tf_op jit(solution)/shard_map/ppermute | solution.py:283
  4.3 1.2 %collective-permute-start = (bf16[224,1024]{1,0:T(8,128)(2,1)}, bf16[224,1024]{1,0:T(8,128)(2,1)S(1)}, u32[]{:S(2)}, u32[]{:S(2)}) collective-permute-start(bf16[224,1024]{1,0:T(8,128)(2,1)} %bitcast.8), channel_id=1, source_target_pairs={{0,1},{1,2},{2,3},{3,0},{4,5},{5,6},{6,7},{7,4},{8,9},{9,10},{10,1... | collective-permute-start | bytes 1376264 | tf_op jit(solution)/shard_map/ppermute | solution.py:283
  5.5 1.5 %collective-permute-start.10 = (bf16[224,1024]{1,0:T(8,128)(2,1)}, bf16[224,1024]{1,0:T(8,128)(2,1)S(1)}, u32[]{:S(2)}, u32[]{:S(2)}) collective-permute-start(bf16[224,1024]{1,0:T(8,128)(2,1)} %bitcast.9), channel_id=1, source_target_pairs={{0,3},{1,0},{2,1},{3,2},{4,7},{5,4},{6,5},{7,6},{8,11},{9,8},{10,9... | collective-permute-start | bytes 1376264 | tf_op jit(solution)/shard_map/ppermute | solution.py:283
  7.0 0.0 collective-permute-start.3
  7.0 0.7 broadcast_multiply_fusion
  7.6 6.1 %collective-permute-done.6.refs_4_ = bf16[224,1024]{1,0:T(8,128)(2,1)S(1)} collective-permute-done((bf16[224,1024]{1,0:T(8,128)(2,1)}, bf16[224,1024]{1,0:T(8,128)(2,1)S(1)}, u32[]{:S(2)}, u32[]{:S(2)}) %collective-permute-start.6) | collective-permute-done | bytes 458784 | tf_op jit(solution)/shard_map/ppermute | solution.py:283
  13.8 2.5 %collective-permute-start.7 = (bf16[224,1024]{1,0:T(8,128)(2,1)S(1)}, bf16[224,1024]{1,0:T(8,128)(2,1)S(1)}, u32[]{:S(2)}, u32[]{:S(2)}) collective-permute-start(bf16[224,1024]{1,0:T(8,128)(2,1)S(1)} %collective-permute-done.6.refs_4_), channel_id=1, source_target_pairs={{0,3},{1,0},{2,1},{3,2},{4,7},{5,4},{6,5},{7,6},{8,11},{9,8},{10,9... | collective-permute-start | bytes 1376264 | tf_op jit(solution)/shard_map/ppermute | solution.py:283
  16.3 0.5 collective-permute-done.refs_1_
  16.8 2.8 %collective-permute-start.1 = (bf16[224,1024]{1,0:T(8,128)(2,1)S(1)}, bf16[224,1024]{1,0:T(8,128)(2,1)S(1)}, u32[]{:S(2)}, u32[]{:S(2)}) collective-permute-start(bf16[224,1024]{1,0:T(8,128)(2,1)S(1)} %collective-permute-done.refs_1_), channel_id=1, source_target_pairs={{0,12},{1,13},{2,14},{3,15},{4,0},{5,1},{6,2},{7,3},{8,4},{9,5},{1... | collective-permute-start | bytes 1376264 | tf_op jit(solution)/shard_map/ppermute | solution.py:283
  19.6 0.0 collective-permute-done.10.refs_2_
  19.6 0.0 collective-permute-start.11
  19.6 0.1 add_add_fusion.1
  19.7 0.1 add.110
  19.8 0.1 add.118
  19.9 0.1 add.121
  20.1 0.1 broadcast_add_fusion.2
  20.1 0.1 add_bitcast_fusion.lane_ref
  20.2 1.2 %in_table.1.refs_15_.refs_5_ = bf16[3584,128]{1,0:T(8,128)(2,1)S(1)} custom-call(s32[1,128]{1,0:T(1,128)S(1)} %add_bitcast_fusion.lane_ref), custom_call_target="tpu_custom_call" | custom-call | flops 2000000000 | bytes 1000000 | tf_op jit(solution)/shard_map/in_table/pallas_call | solution.py:295
  21.5 0.0 copy-start.1
  21.5 1.0 copy-done.1
  22.5 0.0 collective-permute-start.12
  22.5 0.0 collective-permute-done.3.refs_3_
  22.5 0.2 collective-permute-start.4
  22.7 3.8 %collective-permute-done.7.refs_6_ = bf16[224,1024]{1,0:T(8,128)(2,1)S(1)} collective-permute-done((bf16[224,1024]{1,0:T(8,128)(2,1)S(1)}, bf16[224,1024]{1,0:T(8,128)(2,1)S(1)}, u32[]{:S(2)}, u32[]{:S(2)}) %collective-permute-start.7) | collective-permute-done | bytes 458784 | tf_op jit(solution)/shard_map/ppermute | solution.py:283
  26.5 0.0 collective-permute-start.14
  26.5 1.1 collective-permute-done.1.refs_8_
  27.6 3.4 %collective-permute-start.8 = (bf16[224,1024]{1,0:T(8,128)(2,1)S(1)}, bf16[224,1024]{1,0:T(8,128)(2,1)}, u32[]{:S(2)}, u32[]{:S(2)}) collective-permute-start(bf16[224,1024]{1,0:T(8,128)(2,1)S(1)} %collective-permute-done.7.refs_6_), channel_id=1, source_target_pairs={{0,12},{1,13},{2,14},{3,15},{4,0},{5,1},{6,2},{7,3},{8,4},{9,5},{1... | collective-permute-start | bytes 1376264 | tf_op jit(solution)/shard_map/ppermute | solution.py:283
  31.0 0.0 collective-permute-done.11.refs_7_
  31.0 1.2 %collective-permute-start.13 = (bf16[224,1024]{1,0:T(8,128)(2,1)}, bf16[224,1024]{1,0:T(8,128)(2,1)}, u32[]{:S(2)}, u32[]{:S(2)}) collective-permute-start(bf16[224,1024]{1,0:T(8,128)(2,1)} %collective-permute-done.11.refs_7_), channel_id=1, source_target_pairs={{0,3},{1,0},{2,1},{3,2},{4,7},{5,4},{6,5},{7,6},{8,11},{9,8},{10,9... | collective-permute-start | bytes 1376264 | tf_op jit(solution)/shard_map/ppermute | solution.py:283
  32.2 0.2 copy.11.column_ref
  32.4 0.0 copy-done.10
  32.5 0.0 copy-start.3
  32.5 6.9 %out_table.1 = (bf16[256,640]{1,0:T(8,128)(2,1)S(1)}, bf16[256,640]{1,0:T(8,128)(2,1)S(1)}, bf16[1024,640]{1,0:T(8,128)(2,1)S(1)}, bf16[1024,640]{1,0:T(8,128)(2,1)S(1)}) custom-call(s32[1024,2]{1,0:T(8,128)S(1)} %copy.11.column_ref), custom_call_target="tpu_custom_call" | custom-call | flops 4000000000 | bytes 3000000 | tf_op jit(solution)/shard_map/out_table/pallas_call | solution.py:304
  39.4 0.0 copy-start.4
  39.4 0.0 copy-start.6
  39.4 0.0 copy-start
  39.4 0.0 copy-start.2
  39.4 4.1 %collective-permute-done.4.refs_5_ = bf16[224,1024]{1,0:T(8,128)(2,1)} collective-permute-done((bf16[224,1024]{1,0:T(8,128)(2,1)S(1)}, bf16[224,1024]{1,0:T(8,128)(2,1)}, u32[]{:S(2)}, u32[]{:S(2)}) %collective-permute-start.4) | collective-permute-done | bytes 458784 | tf_op jit(solution)/shard_map/ppermute | solution.py:283
  43.5 0.0 collective-permute-start.2
  43.5 0.0 collective-permute-done.12.refs_9_
  43.5 0.0 collective-permute-start.5
  43.5 0.0 collective-permute-done.8.refs_12_
  43.5 2.9 %collective-permute-start.9 = (bf16[224,1024]{1,0:T(8,128)(2,1)}, bf16[224,1024]{1,0:T(8,128)(2,1)S(1)}, u32[]{:S(2)}, u32[]{:S(2)}) collective-permute-start(bf16[224,1024]{1,0:T(8,128)(2,1)} %collective-permute-done.8.refs_12_), channel_id=1, source_target_pairs={{0,3},{1,0},{2,1},{3,2},{4,7},{5,4},{6,5},{7,6},{8,11},{9,8},{10,9... | collective-permute-start | bytes 1376264 | tf_op jit(solution)/shard_map/ppermute | solution.py:283
  46.5 0.0 collective-permute-done.14.refs_11_
  46.5 0.0 collective-permute-done.13.refs_10_
  46.5 0.0 copy-done.3
  46.5 18.0 %first_blocks.1.refs_6_ = f32[1024,1408]{1,0:T(8,128)} custom-call(bf16[224,1024]{1,0:T(8,128)(2,1)S(1)} %bitcast.11, bf16[224,1024]{1,0:T(8,128)(2,1)S(1)} %collective-permute-done.refs_1_, bf16[224,1024]{1,0:T(8,128)(2,1)S(1)} %collective-permute-done.10.refs_2_, bf16[224,1024]{1,0:T(8,128)(2,1)S(1)} %collective-permute-done.3.refs_3_, ...), custom_call_target="tpu_custom_call" | custom-call | flops 8396996608 | bytes 20000000 | tf_op jit(solution)/shard_map/first_blocks/pallas_call | solution.py:326
  64.5 0.0 copy-done.4
  64.5 0.0 copy-done.6
  64.5 0.0 collective-permute-done.2.refs_0_
  64.6 0.0 collective-permute-done.5.refs_1_
  64.6 0.0 collective-permute-done.9.refs_2_
  64.6 0.0 copy-done
  64.6 10.9 %last_blocks.1 = f32[512,128]{1,0:T(8,128)} custom-call(bf16[224,1024]{1,0:T(8,128)(2,1)S(1)} %collective-permute-done.2.refs_0_, bf16[224,1024]{1,0:T(8,128)(2,1)S(1)} %collective-permute-done.5.refs_1_, bf16[224,1024]{1,0:T(8,128)(2,1)S(1)} %collective-permute-done.9.refs_2_, bf16[3584,640]{1,0:T(8,128)(2,1)} %refs_3_.1, bf16[3584,640]{1,0:T(8,128)(2,1)} %refs_4_.1, ...), custom_call_target="tpu_custom_call" | custom-call | flops 1937768448 | bytes 12000000 | tf_op jit(solution)/shard_map/last_blocks/pallas_call | solution.py:342
  75.5 16.3 %all-to-all-start = ((f32[256,2,128]{2,1,0:T(2,128)}), f32[256,2,128]{2,1,0:T(2,128)S(1)}, u32[]{:S(2)}, u32[]{:S(2)}) async-start(f32[256,2,128]{2,1,0:T(2,128)} %bitcast.2), calls=%async_computation | async-start | bytes 524288 | tf_op jit(solution)/shard_map/all_to_all | solution.py:364
  91.8 0.1 add.124
  91.9 0.1 add.127
  92.1 0.9 left_table.1
  93.0 0.0 copy-start.8
  93.0 0.8 copy-done.8
  93.7 13.8 %all-to-all-done = f32[256,2,128]{2,1,0:T(2,128)S(1)} async-done(((f32[256,2,128]{2,1,0:T(2,128)}), f32[256,2,128]{2,1,0:T(2,128)S(1)}, u32[]{:S(2)}, u32[]{:S(2)}) %all-to-all-start) | async-done | bytes 262176 | tf_op jit(solution)/shard_map/all_to_all | solution.py:364
  107.5 1.0 copy-done.9
  108.5 3.0 %update.1 = (f32[224,640]{1,0:T(8,128)}, f32[224,640]{1,0:T(8,128)}, f32[1,32]{1,0:T(1,128)}) custom-call(f32[512,128]{1,0:T(8,128)S(1)} %bitcast.6, bf16[224,1024]{1,0:T(8,128)(2,1)S(1)} %get-tuple-element.14.left_gate_ref, bf16[224,1024]{1,0:T(8,128)(2,1)S(1)} %copy-done.9, bf16[1024,640]{1,0:T(8,128)(2,1)S(1)} %copy-done.5, bf16[1024,640]{1,0:T(8,128)(2,1)S(1)} %copy-done.7), custom_call_target="tpu_custom_call" | custom-call | flops 1200000000 | bytes 5000000 | tf_op jit(solution)/shard_map/update/pallas_call | solution.py:366
  (10 shorter events, 0.0 us)
Async XLA Ops:
  0.6 31.8 %copy-start.10 = (f32[640]{0:T(1024)S(1)}, f32[640]{0:T(1024)}, u32[]{:S(2)}) copy-start(f32[640]{0:T(1024)} %param.8) | copy-start | bytes 7684
  0.6 13.1 %collective-permute-start.6 = (bf16[224,1024]{1,0:T(8,128)(2,1)}, bf16[224,1024]{1,0:T(8,128)(2,1)S(1)}, u32[]{:S(2)}, u32[]{:S(2)}) collective-permute-start(bf16[224,1024]{1,0:T(8,128)(2,1)} %bitcast.7), channel_id=1, source_target_pairs={{0,12},{1,13},{2,14},{3,15},{4,0},{5,1},{6,2},{7,3},{8,4},{9,5},{1... | collective-permute-start | bytes 1376264 | tf_op jit(solution)/shard_map/ppermute | solution.py:283
  4.3 12.5 %collective-permute-start = (bf16[224,1024]{1,0:T(8,128)(2,1)}, bf16[224,1024]{1,0:T(8,128)(2,1)S(1)}, u32[]{:S(2)}, u32[]{:S(2)}) collective-permute-start(bf16[224,1024]{1,0:T(8,128)(2,1)} %bitcast.8), channel_id=1, source_target_pairs={{0,1},{1,2},{2,3},{3,0},{4,5},{5,6},{6,7},{7,4},{8,9},{9,10},{10,1... | collective-permute-start | bytes 1376264 | tf_op jit(solution)/shard_map/ppermute | solution.py:283
  5.5 14.1 %collective-permute-start.10 = (bf16[224,1024]{1,0:T(8,128)(2,1)}, bf16[224,1024]{1,0:T(8,128)(2,1)S(1)}, u32[]{:S(2)}, u32[]{:S(2)}) collective-permute-start(bf16[224,1024]{1,0:T(8,128)(2,1)} %bitcast.9), channel_id=1, source_target_pairs={{0,3},{1,0},{2,1},{3,2},{4,7},{5,4},{6,5},{7,6},{8,11},{9,8},{10,9... | collective-permute-start | bytes 1376264 | tf_op jit(solution)/shard_map/ppermute | solution.py:283
  7.0 15.5 %collective-permute-start.3 = (bf16[224,1024]{1,0:T(8,128)(2,1)}, bf16[224,1024]{1,0:T(8,128)(2,1)S(1)}, u32[]{:S(2)}, u32[]{:S(2)}) collective-permute-start(bf16[224,1024]{1,0:T(8,128)(2,1)} %bitcast.10), channel_id=1, source_target_pairs={{0,4},{1,5},{2,6},{3,7},{4,8},{5,9},{6,10},{7,11},{8,12},{9,13},{1... | collective-permute-start | bytes 1376264 | tf_op jit(solution)/shard_map/ppermute | solution.py:283
  13.8 12.7 %collective-permute-start.7 = (bf16[224,1024]{1,0:T(8,128)(2,1)S(1)}, bf16[224,1024]{1,0:T(8,128)(2,1)S(1)}, u32[]{:S(2)}, u32[]{:S(2)}) collective-permute-start(bf16[224,1024]{1,0:T(8,128)(2,1)S(1)} %collective-permute-done.6.refs_4_), channel_id=1, source_target_pairs={{0,3},{1,0},{2,1},{3,2},{4,7},{5,4},{6,5},{7,6},{8,11},{9,8},{10,9... | collective-permute-start | bytes 1376264 | tf_op jit(solution)/shard_map/ppermute | solution.py:283
  16.8 10.8 %collective-permute-start.1 = (bf16[224,1024]{1,0:T(8,128)(2,1)S(1)}, bf16[224,1024]{1,0:T(8,128)(2,1)S(1)}, u32[]{:S(2)}, u32[]{:S(2)}) collective-permute-start(bf16[224,1024]{1,0:T(8,128)(2,1)S(1)} %collective-permute-done.refs_1_), channel_id=1, source_target_pairs={{0,12},{1,13},{2,14},{3,15},{4,0},{5,1},{6,2},{7,3},{8,4},{9,5},{1... | collective-permute-start | bytes 1376264 | tf_op jit(solution)/shard_map/ppermute | solution.py:283
  19.6 11.4 %collective-permute-start.11 = (bf16[224,1024]{1,0:T(8,128)(2,1)S(1)}, bf16[224,1024]{1,0:T(8,128)(2,1)}, u32[]{:S(2)}, u32[]{:S(2)}) collective-permute-start(bf16[224,1024]{1,0:T(8,128)(2,1)S(1)} %collective-permute-done.10.refs_2_), channel_id=1, source_target_pairs={{0,4},{1,5},{2,6},{3,7},{4,8},{5,9},{6,10},{7,11},{8,12},{9,13},{1... | collective-permute-start | bytes 1376264 | tf_op jit(solution)/shard_map/ppermute | solution.py:283
  21.5 1.0 copy-start.1
  22.5 21.1 %collective-permute-start.12 = (bf16[224,1024]{1,0:T(8,128)(2,1)S(1)}, bf16[224,1024]{1,0:T(8,128)(2,1)}, u32[]{:S(2)}, u32[]{:S(2)}) collective-permute-start(bf16[224,1024]{1,0:T(8,128)(2,1)S(1)} %collective-permute-done.refs_1_), channel_id=1, source_target_pairs={{0,1},{1,2},{2,3},{3,0},{4,5},{5,6},{6,7},{7,4},{8,9},{9,10},{10,1... | collective-permute-start | bytes 1376264 | tf_op jit(solution)/shard_map/ppermute | solution.py:283
  22.5 21.0 %collective-permute-start.4 = (bf16[224,1024]{1,0:T(8,128)(2,1)S(1)}, bf16[224,1024]{1,0:T(8,128)(2,1)}, u32[]{:S(2)}, u32[]{:S(2)}) collective-permute-start(bf16[224,1024]{1,0:T(8,128)(2,1)S(1)} %collective-permute-done.3.refs_3_), channel_id=1, source_target_pairs={{0,1},{1,2},{2,3},{3,0},{4,5},{5,6},{6,7},{7,4},{8,9},{9,10},{10,1... | collective-permute-start | bytes 1376264 | tf_op jit(solution)/shard_map/ppermute | solution.py:283
  26.5 20.0 %collective-permute-start.14 = (bf16[224,1024]{1,0:T(8,128)(2,1)S(1)}, bf16[224,1024]{1,0:T(8,128)(2,1)}, u32[]{:S(2)}, u32[]{:S(2)}) collective-permute-start(bf16[224,1024]{1,0:T(8,128)(2,1)S(1)} %collective-permute-done.3.refs_3_), channel_id=1, source_target_pairs={{0,4},{1,5},{2,6},{3,7},{4,8},{5,9},{6,10},{7,11},{8,12},{9,13},{1... | collective-permute-start | bytes 1376264 | tf_op jit(solution)/shard_map/ppermute | solution.py:283
  27.6 16.0 %collective-permute-start.8 = (bf16[224,1024]{1,0:T(8,128)(2,1)S(1)}, bf16[224,1024]{1,0:T(8,128)(2,1)}, u32[]{:S(2)}, u32[]{:S(2)}) collective-permute-start(bf16[224,1024]{1,0:T(8,128)(2,1)S(1)} %collective-permute-done.7.refs_6_), channel_id=1, source_target_pairs={{0,12},{1,13},{2,14},{3,15},{4,0},{5,1},{6,2},{7,3},{8,4},{9,5},{1... | collective-permute-start | bytes 1376264 | tf_op jit(solution)/shard_map/ppermute | solution.py:283
  31.0 15.5 %collective-permute-start.13 = (bf16[224,1024]{1,0:T(8,128)(2,1)}, bf16[224,1024]{1,0:T(8,128)(2,1)}, u32[]{:S(2)}, u32[]{:S(2)}) collective-permute-start(bf16[224,1024]{1,0:T(8,128)(2,1)} %collective-permute-done.11.refs_7_), channel_id=1, source_target_pairs={{0,3},{1,0},{2,1},{3,2},{4,7},{5,4},{6,5},{7,6},{8,11},{9,8},{10,9... | collective-permute-start | bytes 1376264 | tf_op jit(solution)/shard_map/ppermute | solution.py:283
  32.5 14.0 %copy-start.3 = (bf16[1024,224]{0,1:T(8,128)(2,1)S(1)}, bf16[1024,224]{0,1:T(8,128)(2,1)}, u32[]{:S(2)}) copy-start(bf16[1024,224]{0,1:T(8,128)(2,1)} %param.6) | copy-start | bytes 1376260
  39.4 25.2 %copy-start.4 = (bf16[1024,640]{1,0:T(8,128)(2,1)}, bf16[1024,640]{1,0:T(8,128)(2,1)S(1)}, u32[]{:S(2)}) copy-start(bf16[1024,640]{1,0:T(8,128)(2,1)S(1)} %get-tuple-element.16.right_gate_ref) | copy-start | bytes 3932164
  39.4 25.2 %copy-start.6 = (bf16[1024,640]{1,0:T(8,128)(2,1)}, bf16[1024,640]{1,0:T(8,128)(2,1)S(1)}, u32[]{:S(2)}) copy-start(bf16[1024,640]{1,0:T(8,128)(2,1)S(1)} %get-tuple-element.17.right_up_ref) | copy-start | bytes 3932164
  39.4 25.2 %copy-start = (bf16[1024,640]{1,0:T(8,128)(2,1)S(1)}, bf16[1024,640]{1,0:T(8,128)(2,1)}, u32[]{:S(2)}) copy-start(bf16[1024,640]{1,0:T(8,128)(2,1)} %refs_7_.1) | copy-start | bytes 3932164
  39.4 25.2 %copy-start.2 = (bf16[3584,128]{1,0:T(8,128)(2,1)S(1)}, bf16[3584,128]{1,0:T(8,128)(2,1)}, u32[]{:S(2)}) copy-start(bf16[3584,128]{1,0:T(8,128)(2,1)} %copy-done.1) | copy-start | bytes 2752516
  43.5 21.0 %collective-permute-start.2 = (bf16[224,1024]{1,0:T(8,128)(2,1)S(1)}, bf16[224,1024]{1,0:T(8,128)(2,1)S(1)}, u32[]{:S(2)}, u32[]{:S(2)}) collective-permute-start(bf16[224,1024]{1,0:T(8,128)(2,1)S(1)} %collective-permute-done.1.refs_8_), channel_id=1, source_target_pairs={{0,1},{1,2},{2,3},{3,0},{4,5},{5,6},{6,7},{7,4},{8,9},{9,10},{10,1... | collective-permute-start | bytes 1376264 | tf_op jit(solution)/shard_map/ppermute | solution.py:283
  43.5 21.0 %collective-permute-start.5 = (bf16[224,1024]{1,0:T(8,128)(2,1)}, bf16[224,1024]{1,0:T(8,128)(2,1)S(1)}, u32[]{:S(2)}, u32[]{:S(2)}) collective-permute-start(bf16[224,1024]{1,0:T(8,128)(2,1)} %collective-permute-done.4.refs_5_), channel_id=1, source_target_pairs={{0,4},{1,5},{2,6},{3,7},{4,8},{5,9},{6,10},{7,11},{8,12},{9,13},{1... | collective-permute-start | bytes 1376264 | tf_op jit(solution)/shard_map/ppermute | solution.py:283
  43.5 21.0 %collective-permute-start.9 = (bf16[224,1024]{1,0:T(8,128)(2,1)}, bf16[224,1024]{1,0:T(8,128)(2,1)S(1)}, u32[]{:S(2)}, u32[]{:S(2)}) collective-permute-start(bf16[224,1024]{1,0:T(8,128)(2,1)} %collective-permute-done.8.refs_12_), channel_id=1, source_target_pairs={{0,3},{1,0},{2,1},{3,2},{4,7},{5,4},{6,5},{7,6},{8,11},{9,8},{10,9... | collective-permute-start | bytes 1376264 | tf_op jit(solution)/shard_map/ppermute | solution.py:283
  75.5 32.0 %copy-start.5 = (bf16[1024,640]{1,0:T(8,128)(2,1)S(1)}, bf16[1024,640]{1,0:T(8,128)(2,1)}, u32[]{:S(2)}) copy-start(bf16[1024,640]{1,0:T(8,128)(2,1)} %copy-done.4) | copy-start | bytes 3932164
  75.5 32.0 %copy-start.7 = (bf16[1024,640]{1,0:T(8,128)(2,1)S(1)}, bf16[1024,640]{1,0:T(8,128)(2,1)}, u32[]{:S(2)}) copy-start(bf16[1024,640]{1,0:T(8,128)(2,1)} %copy-done.6) | copy-start | bytes 3932164
  75.5 32.0 %all-to-all-start = ((f32[256,2,128]{2,1,0:T(2,128)}), f32[256,2,128]{2,1,0:T(2,128)S(1)}, u32[]{:S(2)}, u32[]{:S(2)}) async-start(f32[256,2,128]{2,1,0:T(2,128)} %bitcast.2), calls=%async_computation | async-start | bytes 524288 | tf_op jit(solution)/shard_map/all_to_all | solution.py:364
  93.0 0.8 copy-start.8
  107.5 1.0 copy-start.9

commit v2 on v1

v2 whole, which is shorter than its diff:
```python
import math

import jax
import jax.numpy as jnp
from jax import lax
from jax.experimental import pallas as pl
from jax.experimental.pallas import tpu as pltpu
from jax.sharding import PartitionSpec as P

FF = 10240
ROWS = 64
SIGMA = 0.5
EPSILON = 1e-05
SEED_STEP = 747796405
CELL_STEP = 277803737

WAYS = {"+x": (1, 0), "-x": (3, 0), "+y": (0, 1), "-y": (0, 3)}
ROUNDS = (
    (((0, 0), "+x"), ((0, 0), "-y"), ((0, 0), "-x"), ((0, 0), "+y")),
    (((1, 0), "+x"), ((0, 3), "-y"), ((0, 3), "-x"), ((1, 0), "+y")),
    (((0, 3), "+x"), ((2, 0), "-y"), ((0, 1), "-x"), ((2, 0), "+y")),
    (((0, 2), "+x"), ((0, 2), "-x"), ((2, 3), "-y")),
)


def moved(place, way):
    return ((place[0] + WAYS[way][0]) % 4, (place[1] + WAYS[way][1]) % 4)


def pairs_of(way):
    dx, dy = WAYS[way]
    return [(y * 4 + x, (y + dy) % 4 * 4 + (x + dx) % 4) for y in range(4) for x in range(4)]


def source_of(place):
    me = lax.axis_index("mp")
    return lax.rem(me // 4 + 4 - place[1], 4) * 4 + lax.rem(lax.rem(me, 4) + 4 - place[0], 4)


def levels_of(mixed):
    mixed = jnp.bitwise_xor(mixed, jnp.right_shift(mixed, 15))
    mixed = mixed * 1664525 + 1013904223
    mixed = jnp.bitwise_xor(mixed, jnp.right_shift(mixed, 13))
    level = jnp.bitwise_and(mixed, 255).astype(jnp.float32) * (2.0 / 256.0) - 255.0 / 256.0
    return level.astype(jnp.bfloat16)


def iota(shape, dim):
    return lax.broadcasted_iota(jnp.int32, shape, dim)


def in_table_kernel(lane_ref, out_ref):
    rows = 64

    @pl.loop(0, out_ref.shape[0] // rows)
    def _(i):
        at = pl.multiple_of(i * rows, rows)
        cell = (iota((rows, 128), 0) + at) * (4 * CELL_STEP)
        out_ref[pl.ds(at, rows), :] = levels_of(lane_ref[...] + cell)


def side_table_kernel(column_ref, gate_ref, up_ref):
    width = gate_ref.shape[1]
    first = lax.axis_index("mp") * width
    cell = (iota((16, width), 1) + first) * (4 * CELL_STEP)
    nothing = jnp.zeros((64, width), jnp.bfloat16)
    for i in range(4):
        gate = levels_of(column_ref[i * 16 : i * 16 + 16, :] + cell)
        up = levels_of(column_ref[64 + i * 16 : 64 + i * 16 + 16, :] + cell)
        for half in (0, 128):
            gate_ref[half + i * 16 : half + i * 16 + 16, :] = gate
            up_ref[half + 64 + i * 16 : half + 64 + i * 16 + 16, :] = up
    for half in (0, 128):
        gate_ref[half + 64 : half + 128, :] = nothing
        up_ref[half : half + 64, :] = nothing


def factor_kernel(column_ref, lane_ref, left_gate_ref, left_up_ref, right_gate_ref, right_up_ref):
    width = right_gate_ref.shape[1]
    first = lax.axis_index("mp") * width
    rows = 16
    cell = (iota((rows, width), 1) + first) * (4 * CELL_STEP)

    @pl.loop(0, right_gate_ref.shape[0] // rows)
    def _(i):
        at = pl.multiple_of(i * rows, rows)
        right_gate_ref[pl.ds(at, rows), :] = levels_of(column_ref[pl.ds(at, rows), 0:1] + cell)
        right_up_ref[pl.ds(at, rows), :] = levels_of(column_ref[pl.ds(at, rows), 1:2] + cell)

    count, across = left_gate_ref.shape
    left_first = lax.axis_index("pop") * count

    @pl.loop(0, count // rows)
    def _(i):
        at = pl.multiple_of(i * rows, rows)
        step = (iota((rows, across), 0) + (at + left_first)) * (4 * CELL_STEP)
        left_gate_ref[pl.ds(at, rows), :] = levels_of(lane_ref[0:1, :] + step)
        left_up_ref[pl.ds(at, rows), :] = levels_of(lane_ref[1:2, :] + step)


def contract(a, b):
    return lax.dot_general(a, b, (((0,), (0,)), ((), ())), preferred_element_type=jnp.float32)


def block_copies(places, blocks, gate_ref, up_ref, table_ref, x_ref, w_ref, sems):
    depth = blocks[0].shape[0]
    width = gate_ref.shape[1]
    copies = []
    for i, (place, block) in enumerate(zip(places, blocks)):
        rows = pl.ds(source_of(place) * depth, depth)
        mine = pl.ds(i * depth, depth)
        copies.append(
            [
                pltpu.make_async_copy(block, x_ref.at[mine, :], sems.at[4 * i]),
                pltpu.make_async_copy(gate_ref.at[rows, :], w_ref.at[mine, pl.ds(0, width)], sems.at[4 * i + 1]),
                pltpu.make_async_copy(up_ref.at[rows, :], w_ref.at[mine, pl.ds(width, width)], sems.at[4 * i + 2]),
                pltpu.make_async_copy(table_ref.at[rows, :], w_ref.at[mine, pl.ds(2 * width, 128)], sems.at[4 * i + 3]),
            ]
        )
    return copies


def round_kernel(places, fresh, *refs):
    n = len(places)
    blocks, rest = refs[:n], refs[n:]
    gate_ref, up_ref, table_ref = rest[:3]
    acc_ref, x_ref, w_ref, sems = rest[-4:]
    copies = block_copies(places, blocks, gate_ref, up_ref, table_ref, x_ref, w_ref, sems)
    for group in copies:
        for copy in group:
            copy.start()
    for group in copies:
        for copy in group:
            copy.wait()

    @pl.loop(0, acc_ref.shape[0] // 256)
    def _(i):
        rows = pl.ds(pl.multiple_of(i * 256, 256), 256)
        part = contract(x_ref[:, rows], w_ref[...])
        if fresh:
            acc_ref[rows, :] = part
        else:
            acc_ref[rows, :] = rest[3][rows, :] + part


def last_kernel(places, *refs):
    n = len(places)
    blocks = refs[:n]
    gate_ref, up_ref, table_ref, acc_ref, target_ref, weight_ref, gate_out_ref, up_out_ref = refs[n : n + 8]
    message_ref, x_ref, w_ref, t_ref, total_ref, side_ref, parts_ref, sems, t_sems = refs[n + 8 :]
    width = gate_ref.shape[1]
    tile = 256
    tiles = acc_ref.shape[0] // tile
    copies = block_copies(places, blocks, gate_ref, up_ref, table_ref, x_ref, w_ref, sems)
    for group in copies:
        for copy in group:
            copy.start()
    for i in range(tiles):
        rows = pl.ds(i * tile, tile)
        pltpu.make_async_copy(target_ref.at[rows, :], t_ref.at[rows, :], t_sems.at[i]).start()
    for group in copies:
        for copy in group:
            copy.wait()
    scale = SIGMA / math.sqrt(16 * blocks[0].shape[0])
    lane_pair = lax.rem(iota((tile, 128), 1), 64) // 4
    row_pair = iota((tile, 128), 0) // ROWS

    @pl.loop(0, tiles)
    def _(i):
        rows = pl.ds(pl.multiple_of(i * tile, tile), tile)
        pltpu.make_async_copy(target_ref.at[rows, :], t_ref.at[rows, :], t_sems.at[i]).wait()
        part = contract(x_ref[:, rows], w_ref[...]) + acc_ref[rows, :]
        total_ref[...] = part[:, : 2 * width]
        low = jnp.where(lane_pair == row_pair + i * (tile // ROWS), part[:, 2 * width :] * scale, 0.0)
        high = low.astype(jnp.bfloat16)
        rest = (low - high.astype(jnp.float32)).astype(jnp.bfloat16)
        low_both = jnp.concatenate([high, rest], axis=1)
        side_ref[:, :width] = jnp.dot(low_both, gate_out_ref[...], preferred_element_type=jnp.float32)
        side_ref[:, width:] = jnp.dot(low_both, up_out_ref[...], preferred_element_type=jnp.float32)

        @pl.loop(0, tile // ROWS)
        def _(p):
            plus = jnp.zeros((8, width), jnp.float32)
            minus = jnp.zeros((8, width), jnp.float32)
            for q in range(ROWS // 16):
                at16 = pl.multiple_of(p * ROWS + q * 16, 16)
                goals = t_ref[pl.ds(pl.multiple_of(i * tile + at16, 16), 16), :].astype(jnp.float32)
                for h in range(2):
                    here = pl.ds(pl.multiple_of(at16 + h * 8, 8), 8)
                    goal = goals[h * 8 : h * 8 + 8, :]
                    gate, up = total_ref[here, :width], total_ref[here, width:]
                    side_gate, side_up = side_ref[here, :width], side_ref[here, width:]
                    half = 0.5 * (gate + side_gate)
                    error = (half * jnp.tanh(half) + half) * (up + side_up) - goal
                    plus += error * error
                    half = 0.5 * (gate - side_gate)
                    error = (half * jnp.tanh(half) + half) * (up - side_up) - goal
                    minus += error * error
            k = i * (tile // ROWS) + p
            parts_ref[0, pl.ds(k, 1), :] = jnp.sum(plus, axis=0, keepdims=True) * weight_ref[...]
            parts_ref[1, pl.ds(k, 1), :] = jnp.sum(minus, axis=0, keepdims=True) * weight_ref[...]

    pairs = parts_ref.shape[1]
    lane = iota((pairs, 128), 1)
    pair = iota((pairs, 128), 0)
    line = jnp.zeros((1, 128), jnp.float32)
    for s in range(2):
        sums = jnp.sum(parts_ref[s], axis=1, keepdims=True) * (1.0 / (ROWS * FF))
        line += jnp.sum(jnp.where(lane // 4 == pair + 16 * s, sums, 0.0), axis=0, keepdims=True)
    message_ref[...] = jnp.broadcast_to(line, message_ref.shape)


def update_kernel(message_ref, left_gate_ref, left_up_ref, right_gate, right_up, *refs):
    out_gate_ref, out_up_ref, fit_ref, f_ref, right_gate_ref, right_up_ref, sems = refs
    gate_copy = pltpu.make_async_copy(right_gate, right_gate_ref, sems.at[0])
    up_copy = pltpu.make_async_copy(right_up, right_up_ref, sems.at[1])
    gate_copy.start()
    up_copy.start()
    count = message_ref.shape[0]
    pick_row, pick = iota((16, count), 0), iota((16, count), 1)
    chosen = pick // 16 == 2 * lax.rem(pick_row, 8) + pick_row // 8
    by_pop = jnp.dot(
        chosen.astype(jnp.float32),
        message_ref[...],
        precision=lax.Precision.HIGHEST,
        preferred_element_type=jnp.float32,
    )
    even, odd = by_pop[:8], by_pop[8:]
    low_lane = iota((8, 128), 1) < 64
    plus = jnp.where(low_lane, even, pltpu.roll(odd, 64, 1))
    minus = jnp.where(low_lane, pltpu.roll(even, 64, 1), odd)
    summed = jnp.concatenate([plus, minus], axis=0)
    scores = -summed
    members = 4.0 * 512.0
    center = jnp.sum(scores) / members
    spread = jnp.sum((scores - center) ** 2) / members
    fitness = (scores - center) / jnp.sqrt(jnp.full((16, 128), spread + EPSILON, jnp.float32))
    f_ref[...] = fitness
    factor = (fitness[:8] - fitness[8:]) * (0.5 / 16.0)
    for left_ref, right_ref, copy, out_ref in (
        (left_gate_ref, right_gate_ref, gate_copy, out_gate_ref),
        (left_up_ref, right_up_ref, up_copy, out_up_ref),
    ):
        highs, rests = [], []
        for q in range(8):
            scaled = left_ref[:, q * 128 : (q + 1) * 128].astype(jnp.float32) * factor[q : q + 1, :]
            high = scaled.astype(jnp.bfloat16)
            highs.append(high)
            rests.append((scaled - high.astype(jnp.float32)).astype(jnp.bfloat16))
        copy.wait()
        out_ref[...] = jnp.dot(
            jnp.concatenate(highs, axis=1), right_ref[...], preferred_element_type=jnp.float32
        ) + jnp.dot(jnp.concatenate(rests, axis=1), right_ref[...], preferred_element_type=jnp.float32)
    pop = lax.axis_index("pop")
    mine = pop // 2
    lane, member = iota((128, 128), 0), iota((128, 128), 1)
    at = lane == lax.rem(pop, 2) * 64 + member // 2 * 4
    total = jnp.zeros((1, 128), jnp.float32)
    for s in range(2):
        line = jnp.broadcast_to(f_ref[pl.ds(mine + 8 * s, 1), :], (8, 128))
        select = (at & (lax.rem(member, 2) == s)).astype(jnp.float32)
        total += jnp.dot(line, select, precision=lax.Precision.HIGHEST, preferred_element_type=jnp.float32)[:1]
    fit_ref[...] = total[:, : fit_ref.shape[1]]


def params(mib):
    return pltpu.CompilerParams(vmem_limit_bytes=mib * 1024 * 1024)


def cost(flops, size):
    return pl.CostEstimate(flops=flops, bytes_accessed=size, transcendentals=0)


def after(value, *others):
    return lax.optimization_barrier((value, *others))[0]


def on_device(tokens, target, unit_weight, gate_weight, up_weight, seeds):
    rows_dev, depth = tokens.shape
    model_width, width = gate_weight.shape
    pairs_dev = rows_dev // ROWS
    pair_total = seeds.shape[0]
    device_total = lax.axis_size("pop") * lax.axis_size("mp")
    any_space = pl.BlockSpec(memory_space=pl.ANY)
    in_vmem = pl.BlockSpec(memory_space=pltpu.VMEM)
    bf16, f32 = jnp.bfloat16, jnp.float32

    corner = jnp.tile(jnp.arange(4, dtype=jnp.int32) * CELL_STEP, pair_total)
    by_lane = jnp.repeat(seeds * SEED_STEP, 4) + corner
    local_lane = lax.dynamic_slice_in_dim(by_lane, lax.axis_index("pop") * pairs_dev * 4, pairs_dev * 4)
    in_lanes = jnp.concatenate([local_lane + 11003, local_lane + 33023])[None, :]
    side_columns = jnp.concatenate([local_lane + 22013, local_lane + 44041])[:, None]

    left_lanes = jnp.stack([by_lane + 11003, by_lane + 33023])
    right_columns = jnp.stack([by_lane + 22013, by_lane + 44041], axis=1)

    table = pl.pallas_call(
        in_table_kernel,
        out_shape=jax.ShapeDtypeStruct((model_width, 128), bf16),
        in_specs=[in_vmem],
        out_specs=in_vmem,
        compiler_params=params(4),
        cost_estimate=cost(1_000_000_000, 1_000_000),
        name="in_table",
    )(in_lanes)
    gate_out, up_out = pl.pallas_call(
        side_table_kernel,
        out_shape=[jax.ShapeDtypeStruct((256, width), bf16)] * 2,
        in_specs=[in_vmem],
        out_specs=[in_vmem] * 2,
        compiler_params=params(4),
        cost_estimate=cost(500_000_000, 300_000),
        name="side_table",
    )(side_columns)

    columns = 2 * width + 128

    def multiply(places, acc):
        n = len(places)
        given = [blocks[place] for place in places] + [gate_weight, up_weight, table]
        specs = [any_space] * (n + 3)
        if acc is not None:
            given.append(acc)
            specs.append(in_vmem)
        return pl.pallas_call(
            lambda *refs: round_kernel(places, acc is None, *refs),
            out_shape=jax.ShapeDtypeStruct((rows_dev, columns), f32),
            in_specs=specs,
            out_specs=in_vmem,
            scratch_shapes=[
                pltpu.VMEM((n * depth, rows_dev), bf16),
                pltpu.VMEM((n * depth, columns), bf16),
                pltpu.SemaphoreType.DMA((4 * n,)),
            ],
            input_output_aliases={} if acc is None else {n + 3: 0},
            compiler_params=params(20),
            cost_estimate=cost(2 * rows_dev * n * depth * columns, 4_000_000),
            name="round_of_%d" % n,
        )(*given)

    blocks = {(0, 0): tokens.T}
    acc = None
    held = [(0, 0)]
    for number, sends in enumerate(ROUNDS):
        fresh = {}
        for place, way in sends:
            fresh[moved(place, way)] = lax.ppermute({**blocks, **fresh}[place], "mp", pairs_of(way))
        if number > 0:
            acc = multiply(held, acc)
            held = []
        held += list(fresh)
        blocks.update(fresh)

    n = len(held)
    message = pl.pallas_call(
        lambda *refs: last_kernel(held, *refs),
        out_shape=jax.ShapeDtypeStruct((device_total, 128), f32),
        in_specs=[any_space] * (n + 3) + [in_vmem, any_space] + [in_vmem] * 3,
        out_specs=in_vmem,
        scratch_shapes=[
            pltpu.VMEM((n * depth, rows_dev), bf16),
            pltpu.VMEM((n * depth, columns), bf16),
            pltpu.VMEM((rows_dev, width), bf16),
            pltpu.VMEM((256, 2 * width), f32),
            pltpu.VMEM((256, 2 * width), f32),
            pltpu.VMEM((2, pairs_dev, width), f32),
            pltpu.SemaphoreType.DMA((4 * n,)),
            pltpu.SemaphoreType.DMA((rows_dev // 256,)),
        ],
        compiler_params=params(24),
        cost_estimate=cost(2 * rows_dev * n * depth * columns, 12_000_000),
        name="last_round",
    )(*[blocks[place] for place in held], gate_weight, up_weight, table, acc, target, unit_weight[None, :], gate_out, up_out)

    received = lax.all_to_all(message, ("pop", "mp"), 0, 0, tiled=True)

    left_rows = model_width // lax.axis_size("pop")
    left_gate, left_up, right_gate, right_up = pl.pallas_call(
        factor_kernel,
        out_shape=[jax.ShapeDtypeStruct((left_rows, pair_total * 4), bf16)] * 2
        + [jax.ShapeDtypeStruct((pair_total * 4, width), bf16)] * 2,
        in_specs=[in_vmem] * 2,
        out_specs=[in_vmem] * 4,
        compiler_params=params(8),
        cost_estimate=cost(3_000_000_000, 4_000_000),
        name="factor_tables",
    )(after(right_columns, message), left_lanes)
    update_gate, update_up, fitness = pl.pallas_call(
        update_kernel,
        out_shape=[jax.ShapeDtypeStruct((left_rows, width), f32)] * 2
        + [jax.ShapeDtypeStruct((1, 2 * pairs_dev), f32)],
        in_specs=[in_vmem] * 3 + [any_space] * 2,
        out_specs=[in_vmem] * 3,
        scratch_shapes=[
            pltpu.VMEM((16, 128), f32),
            pltpu.VMEM((pair_total * 4, width), bf16),
            pltpu.VMEM((pair_total * 4, width), bf16),
            pltpu.SemaphoreType.DMA((2,)),
        ],
        compiler_params=params(16),
        cost_estimate=cost(1_200_000_000, 5_000_000),
        name="update",
    )(received, left_gate, left_up, right_gate, right_up)
    return (update_gate, update_up, fitness.reshape(2 * pairs_dev))


def solution(mesh):
    return jax.shard_map(
        on_device,
        mesh=mesh,
        in_specs=(P("pop", "mp"), P("pop", "mp"), P("mp"), P(None, "mp"), P(None, "mp"), P()),
        out_specs=(P("pop", "mp"), P("pop", "mp"), P("pop")),
        check_vma=False,
    )
```

time: 112 us -> 102 us (0.911)
  waiting for transfers between devices: 29.5 us -> 17.7 us
  local copies, waits for them, and re-layouts: 3.65 us -> 6.36 us
    all_to_all x1, waiting for transfers between devices: 13.8 us -> 4.5 us  [on_device(): received = lax.all_to_all(message, ('pop', 'mp'), 0, 0, tiled=True)]
    ppermute x15, waiting for transfers between devices: 15.7 us -> 13.2 us  [on_device(): lax.ppermute({**blocks, **fresh}[place], 'mp', pairs_of(way))]
    unnamed x22 -> x16, local copies, waits for them, and re-layouts: 2.81 us -> 4.71 us
    pallas_call x4 -> x6, Pallas kernels: 36.7 us -> 35.5 us  [the longest x3 18.4 us: multiply(): pl.pallas_call(lambda *refs: round_kernel(places, acc is None, *refs), ou...]
  transfers between devices with their start and end apart: 16 -> 16, of which waited for: 6 -> 3; matrix products, arithmetic and copies ran while one was open for 2% -> 2% of each run, Pallas kernels for 24% -> 27%
where the time goes in v2:
time: 102 us; the launch traced here: 101 us
  Pallas kernels  40.3 us (40%)
  starting transfers between devices  34.9 us (34%)
  waiting for transfers between devices  17.7 us (17%)
  local copies, waits for them, and re-layouts  6.36 us (6%)
  between operations  1.06 us (1%)
  other arithmetic  1.05 us (1%)
    ppermute x15, starting transfers between devices, on_device(): lax.ppermute({**blocks, **fresh}[place], 'mp', pairs_of(way))  18.7 us
    pallas_call x3, Pallas kernels, multiply(): pl.pallas_call(lambda *refs: round_kernel(places, acc is None, *refs), ou...  18.4 us
    all_to_all x1, starting transfers between devices, on_device(): received = lax.all_to_all(message, ('pop', 'mp'), 0, 0, tiled=True)  16.2 us
    ppermute x15, waiting for transfers between devices, on_device(): lax.ppermute({**blocks, **fresh}[place], 'mp', pairs_of(way))  13.2 us
    pallas_call x1, Pallas kernels, on_device(): pl.pallas_call(lambda *refs: last_kernel(held, *refs), out_shape=jax.Shap...  9.47 us
    pallas_call x1, Pallas kernels, on_device(): pl.pallas_call(factor_kernel, out_shape=[jax.ShapeDtypeStruct((left_rows,...  7.41 us
    unnamed x16, local copies, waits for them, and re-layouts  4.71 us
    all_to_all x1, waiting for transfers between devices, on_device(): received = lax.all_to_all(message, ('pop', 'mp'), 0, 0, tiled=True)  4.5 us
  transfers between devices with their start and end apart: 16, of which 3 were waited for; matrix products, arithmetic and copies ran while one was open for 2% of the time, Pallas kernels for 27%

profile of v2, /device:TPU:1, one launch (start us, length us, event | category | flops | bytes accessed | tf_op | source)
XLA Modules:
  0.0 101.4 jit_solution(18028450805002175762)
XLA Ops:
  0.6 0.0 copy-start.3
  0.6 3.6 %collective-permute-start = (bf16[224,1024]{1,0:T(8,128)(2,1)}, bf16[224,1024]{1,0:T(8,128)(2,1)S(1)}, u32[]{:S(2)}, u32[]{:S(2)}) collective-permute-start(bf16[224,1024]{1,0:T(8,128)(2,1)} %bitcast.12), channel_id=1, source_target_pairs={{0,12},{1,13},{2,14},{3,15},{4,0},{5,1},{6,2},{7,3},{8,4},{9,5},{1... | collective-permute-start | bytes 1376264 | tf_op jit(solution)/shard_map/ppermute | solution.py:347
  4.3 1.2 %collective-permute-start.4 = (bf16[224,1024]{1,0:T(8,128)(2,1)}, bf16[224,1024]{1,0:T(8,128)(2,1)S(1)}, u32[]{:S(2)}, u32[]{:S(2)}) collective-permute-start(bf16[224,1024]{1,0:T(8,128)(2,1)} %bitcast.13), channel_id=1, source_target_pairs={{0,1},{1,2},{2,3},{3,0},{4,5},{5,6},{6,7},{7,4},{8,9},{9,10},{10,1... | collective-permute-start | bytes 1376264 | tf_op jit(solution)/shard_map/ppermute | solution.py:347
  5.5 0.0 collective-permute-start.9
  5.5 1.5 %collective-permute-start.14 = (bf16[224,1024]{1,0:T(8,128)(2,1)}, bf16[224,1024]{1,0:T(8,128)(2,1)S(1)}, u32[]{:S(2)}, u32[]{:S(2)}) collective-permute-start(bf16[224,1024]{1,0:T(8,128)(2,1)} %bitcast.15), channel_id=1, source_target_pairs={{0,3},{1,0},{2,1},{3,2},{4,7},{5,4},{6,5},{7,6},{8,11},{9,8},{10,9... | collective-permute-start | bytes 1376264 | tf_op jit(solution)/shard_map/ppermute | solution.py:347
  7.0 0.7 broadcast_multiply_fusion
  7.6 0.1 add_add_fusion.1
  7.8 0.1 add.122
  7.9 0.1 broadcast_add_fusion.2
  8.0 8.8 %collective-permute-done.4.refs_1_ = bf16[224,1024]{1,0:T(8,128)(2,1)S(1)} collective-permute-done((bf16[224,1024]{1,0:T(8,128)(2,1)}, bf16[224,1024]{1,0:T(8,128)(2,1)S(1)}, u32[]{:S(2)}, u32[]{:S(2)}) %collective-permute-start.4) | collective-permute-done | bytes 458784 | tf_op jit(solution)/shard_map/ppermute | solution.py:347
  16.8 0.0 collective-permute-start.5
  16.8 0.1 add_bitcast_fusion.1
  16.9 0.1 copy.15.column_ref
  17.0 0.7 broadcast_in_dim.14.refs_8_
  17.7 0.1 add.134
  17.8 0.1 add.137
  17.9 0.1 add.140
  18.0 0.1 add.143
  18.2 0.0 collective-permute-done.refs_2_
  18.2 0.5 collective-permute-start.1
  18.7 2.7 %collective-permute-start.12 = (bf16[224,1024]{1,0:T(8,128)(2,1)S(1)}, bf16[224,1024]{1,0:T(8,128)(2,1)S(1)}, u32[]{:S(2)}, u32[]{:S(2)}) collective-permute-start(bf16[224,1024]{1,0:T(8,128)(2,1)S(1)} %collective-permute-done.refs_2_), channel_id=1, source_target_pairs={{0,3},{1,0},{2,1},{3,2},{4,7},{5,4},{6,5},{7,6},{8,11},{9,8},{10,9... | collective-permute-start | bytes 1376264 | tf_op jit(solution)/shard_map/ppermute | solution.py:347
  21.4 0.1 add_bitcast_fusion.lane_ref
  21.5 1.2 %in_table.1.refs_7_.refs_6_.refs_5_ = bf16[3584,128]{1,0:T(8,128)(2,1)S(1)} custom-call(s32[1,128]{1,0:T(1,128)S(1)} %add_bitcast_fusion.lane_ref), custom_call_target="tpu_custom_call" | custom-call | flops 1000000000 | bytes 1000000 | tf_op jit(solution)/shard_map/in_table/pallas_call | solution.py:297
  22.7 0.0 collective-permute-done.9.refs_4_
  22.7 1.1 %collective-permute-start.13 = (bf16[224,1024]{1,0:T(8,128)(2,1)S(1)}, bf16[224,1024]{1,0:T(8,128)(2,1)S(1)}, u32[]{:S(2)}, u32[]{:S(2)}) collective-permute-start(bf16[224,1024]{1,0:T(8,128)(2,1)S(1)} %collective-permute-done.4.refs_1_), channel_id=1, source_target_pairs={{0,4},{1,5},{2,6},{3,7},{4,8},{5,9},{6,10},{7,11},{8,12},{9,13},{1... | collective-permute-start | bytes 1376264 | tf_op jit(solution)/shard_map/ppermute | solution.py:347
  23.8 0.0 collective-permute-done.14.refs_3_
  23.8 0.0 collective-permute-start.8
  23.8 4.4 %collective-permute-done.5.refs_0_ = bf16[224,1024]{1,0:T(8,128)(2,1)S(1)} collective-permute-done((bf16[224,1024]{1,0:T(8,128)(2,1)S(1)}, bf16[224,1024]{1,0:T(8,128)(2,1)S(1)}, u32[]{:S(2)}, u32[]{:S(2)}) %collective-permute-start.5) | collective-permute-done | bytes 458784 | tf_op jit(solution)/shard_map/ppermute | solution.py:347
  28.1 0.5 collective-permute-start.6
  28.6 0.2 side_table.1
  28.8 0.0 collective-permute-done.1.refs_1_
  28.8 2.0 %collective-permute-start.10 = (bf16[224,1024]{1,0:T(8,128)(2,1)S(1)}, bf16[224,1024]{1,0:T(8,128)(2,1)S(1)}, u32[]{:S(2)}, u32[]{:S(2)}) collective-permute-start(bf16[224,1024]{1,0:T(8,128)(2,1)S(1)} %collective-permute-done.9.refs_4_), channel_id=1, source_target_pairs={{0,3},{1,0},{2,1},{3,2},{4,7},{5,4},{6,5},{7,6},{8,11},{9,8},{10,9... | collective-permute-start | bytes 1376264 | tf_op jit(solution)/shard_map/ppermute | solution.py:347
  30.8 0.0 collective-permute-done.12.refs_2_
  30.8 0.0 collective-permute-start.11
  30.8 0.0 copy-done.3
  30.8 0.0 copy-done
  30.8 0.0 copy-start.1
  30.8 2.3 %copy-done.1 = bf16[3584,640]{1,0:T(8,128)(2,1)S(1)} copy-done((bf16[3584,640]{1,0:T(8,128)(2,1)S(1)}, bf16[3584,640]{1,0:T(8,128)(2,1)}, u32[]{:S(2)}) %copy-start.1) | copy-done | bytes 4587544
  33.1 6.7 %round_of_5.1.refs_7_ = f32[1024,1408]{1,0:T(8,128)S(1)} custom-call(bf16[224,1024]{1,0:T(8,128)(2,1)S(1)} %bitcast.16, bf16[224,1024]{1,0:T(8,128)(2,1)S(1)} %collective-permute-done.4.refs_1_, bf16[224,1024]{1,0:T(8,128)(2,1)S(1)} %collective-permute-done.refs_2_, bf16[224,1024]{1,0:T(8,128)(2,1)S(1)} %collective-permute-done.14.refs_3_, ...), custom_call_target="tpu_custom_call" | custom-call | flops 3229614080 | bytes 4000000 | tf_op jit(solution)/shard_map/round_of_5/pallas_call | solution.py:325
  39.9 0.0 collective-permute-done.13.refs_3_
  39.9 0.8 collective-permute-start.2
  40.7 0.0 collective-permute-done.8.refs_0_
  40.7 2.1 %collective-permute-start.3 = (bf16[224,1024]{1,0:T(8,128)(2,1)S(1)}, bf16[224,1024]{1,0:T(8,128)(2,1)S(1)}, u32[]{:S(2)}, u32[]{:S(2)}) collective-permute-start(bf16[224,1024]{1,0:T(8,128)(2,1)S(1)} %collective-permute-done.1.refs_1_), channel_id=1, source_target_pairs={{0,3},{1,0},{2,1},{3,2},{4,7},{5,4},{6,5},{7,6},{8,11},{9,8},{10,9... | collective-permute-start | bytes 1376264 | tf_op jit(solution)/shard_map/ppermute | solution.py:347
  42.8 0.0 collective-permute-done.6.refs_1_
  42.8 2.7 %collective-permute-start.7 = (bf16[224,1024]{1,0:T(8,128)(2,1)S(1)}, bf16[224,1024]{1,0:T(8,128)(2,1)S(1)}, u32[]{:S(2)}, u32[]{:S(2)}) collective-permute-start(bf16[224,1024]{1,0:T(8,128)(2,1)S(1)} %collective-permute-done.6.refs_1_), channel_id=1, source_target_pairs={{0,12},{1,13},{2,14},{3,15},{4,0},{5,1},{6,2},{7,3},{8,4},{9,5},{1... | collective-permute-start | bytes 1376264 | tf_op jit(solution)/shard_map/ppermute | solution.py:347
  45.5 5.8 %round_of_4.2.refs_7_ = f32[1024,1408]{1,0:T(8,128)S(1)} custom-call(bf16[224,1024]{1,0:T(8,128)(2,1)S(1)} %collective-permute-done.5.refs_0_, bf16[224,1024]{1,0:T(8,128)(2,1)S(1)} %collective-permute-done.1.refs_1_, bf16[224,1024]{1,0:T(8,128)(2,1)S(1)} %collective-permute-done.12.refs_2_, ...), custom_call_target="tpu_custom_call", output_to_operand_aliasing={{}: (7, {})} | custom-call | flops 2583691264 | bytes 4000000 | tf_op jit(solution)/shard_map/round_of_4/pallas_call | solution.py:325
  51.3 0.0 slice-start.1
  51.3 0.0 copy-start.2
  51.4 0.0 collective-permute-done.10.refs_2_
  51.4 0.0 collective-permute-done.11.refs_3_
  51.4 5.8 %round_of_4.3.refs_6_ = f32[1024,1408]{1,0:T(8,128)S(1)} custom-call(bf16[224,1024]{1,0:T(8,128)(2,1)S(1)} %collective-permute-done.8.refs_0_, bf16[224,1024]{1,0:T(8,128)(2,1)S(1)} %collective-permute-done.6.refs_1_, bf16[224,1024]{1,0:T(8,128)(2,1)S(1)} %collective-permute-done.10.refs_2_, ...), custom_call_target="tpu_custom_call", output_to_operand_aliasing={{}: (7, {})} | custom-call | flops 2583691264 | bytes 4000000 | tf_op jit(solution)/shard_map/round_of_4/pallas_call | solution.py:325
  57.2 0.0 collective-permute-done.2.refs_0_
  57.2 0.0 collective-permute-done.3.refs_1_
  57.2 0.0 collective-permute-done.7.refs_2_
  57.3 0.0 slice-done
  57.3 0.0 slice-done.1
  57.3 9.5 %last_round.1 = f32[256,128]{1,0:T(8,128)} custom-call(bf16[224,1024]{1,0:T(8,128)(2,1)S(1)} %collective-permute-done.2.refs_0_, bf16[224,1024]{1,0:T(8,128)(2,1)S(1)} %collective-permute-done.3.refs_1_, bf16[224,1024]{1,0:T(8,128)(2,1)S(1)} %collective-permute-done.7.refs_2_, bf16[3584,640]{1,0:T(8,128)(2,1)S(1)} %copy-done, ...), custom_call_target="tpu_custom_call" | custom-call | flops 1937768448 | bytes 12000000 | tf_op jit(solution)/shard_map/last_round/pallas_call | solution.py:355
  66.8 0.2 copy.17.column_ref
  67.0 16.2 %all-to-all-start = ((f32[256,1,128]{2,1,0:T(1,128)}), f32[256,1,128]{2,1,0:T(1,128)S(1)}, u32[]{:S(2)}, u32[]{:S(2)}) async-start(f32[256,1,128]{2,1,0:T(1,128)} %bitcast.4), calls=%async_computation | async-start | bytes 262144 | tf_op jit(solution)/shard_map/all_to_all | solution.py:375
  83.2 7.4 %factor_tables.1 = (bf16[224,1024]{1,0:T(8,128)(2,1)S(1)}, bf16[224,1024]{1,0:T(8,128)(2,1)S(1)}, bf16[1024,640]{1,0:T(8,128)(2,1)S(1)}, bf16[1024,640]{1,0:T(8,128)(2,1)S(1)}) custom-call(s32[1024,2]{1,0:T(8,128)S(1)} %copy.17.column_ref, s32[2,1024]{1,0:T(2,128)S(1)} %pad_add_fusion.1.lane_ref), custom_call_target="tpu_custom_call" | custom-call | flops 3000000000 | bytes 4000000 | tf_op jit(solution)/shard_map/factor_tables/pallas_call | solution.py:378
  90.7 1.1 %copy-done.4 = bf16[1024,640]{1,0:T(8,128)(2,1)} copy-done((bf16[1024,640]{1,0:T(8,128)(2,1)}, bf16[1024,640]{1,0:T(8,128)(2,1)S(1)}, u32[]{:S(2)}) %copy-start.4) | copy-done | bytes 1310744
  91.7 4.5 %all-to-all-done = f32[256,1,128]{2,1,0:T(1,128)S(1)} async-done(((f32[256,1,128]{2,1,0:T(1,128)}), f32[256,1,128]{2,1,0:T(1,128)S(1)}, u32[]{:S(2)}, u32[]{:S(2)}) %all-to-all-start) | async-done | bytes 131104 | tf_op jit(solution)/shard_map/all_to_all | solution.py:375
  96.2 1.3 %copy-done.5 = bf16[1024,640]{1,0:T(8,128)(2,1)S(1)} copy-done((bf16[1024,640]{1,0:T(8,128)(2,1)S(1)}, bf16[1024,640]{1,0:T(8,128)(2,1)}, u32[]{:S(2)}) %copy-start.5) | copy-done | bytes 1310744
  97.5 3.6 %update.1 = (f32[224,640]{1,0:T(8,128)}, f32[224,640]{1,0:T(8,128)}, f32[1,32]{1,0:T(1,128)}) custom-call(f32[256,128]{1,0:T(8,128)S(1)} %bitcast.17, bf16[224,1024]{1,0:T(8,128)(2,1)S(1)} %get-tuple-element.16.left_gate_ref, bf16[224,1024]{1,0:T(8,128)(2,1)S(1)} %get-tuple-element.17.left_up_ref, bf16[1024,640]{1,0:T(8,128)(2,1)S(1)} %get-tuple-element.18.right_gate, ...), custom_call_target="tpu_custom_call" | custom-call | flops 1200000000 | bytes 5000000 | tf_op jit(solution)/shard_map/update/pallas_call | solution.py:388
  (10 shorter events, 0.0 us)
Async XLA Ops:
  0.6 30.2 %copy-start.3 = (bf16[1024,224]{0,1:T(8,128)(2,1)S(1)}, bf16[1024,224]{0,1:T(8,128)(2,1)}, u32[]{:S(2)}) copy-start(bf16[1024,224]{0,1:T(8,128)(2,1)} %param.6) | copy-start | bytes 1376260
  0.6 17.5 %collective-permute-start = (bf16[224,1024]{1,0:T(8,128)(2,1)}, bf16[224,1024]{1,0:T(8,128)(2,1)S(1)}, u32[]{:S(2)}, u32[]{:S(2)}) collective-permute-start(bf16[224,1024]{1,0:T(8,128)(2,1)} %bitcast.12), channel_id=1, source_target_pairs={{0,12},{1,13},{2,14},{3,15},{4,0},{5,1},{6,2},{7,3},{8,4},{9,5},{1... | collective-permute-start | bytes 1376264 | tf_op jit(solution)/shard_map/ppermute | solution.py:347
  4.3 12.5 %collective-permute-start.4 = (bf16[224,1024]{1,0:T(8,128)(2,1)}, bf16[224,1024]{1,0:T(8,128)(2,1)S(1)}, u32[]{:S(2)}, u32[]{:S(2)}) collective-permute-start(bf16[224,1024]{1,0:T(8,128)(2,1)} %bitcast.13), channel_id=1, source_target_pairs={{0,1},{1,2},{2,3},{3,0},{4,5},{5,6},{6,7},{7,4},{8,9},{9,10},{10,1... | collective-permute-start | bytes 1376264 | tf_op jit(solution)/shard_map/ppermute | solution.py:347
  5.5 17.2 %collective-permute-start.9 = (bf16[224,1024]{1,0:T(8,128)(2,1)}, bf16[224,1024]{1,0:T(8,128)(2,1)S(1)}, u32[]{:S(2)}, u32[]{:S(2)}) collective-permute-start(bf16[224,1024]{1,0:T(8,128)(2,1)} %bitcast.14), channel_id=1, source_target_pairs={{0,4},{1,5},{2,6},{3,7},{4,8},{5,9},{6,10},{7,11},{8,12},{9,13},{1... | collective-permute-start | bytes 1376264 | tf_op jit(solution)/shard_map/ppermute | solution.py:347
  5.5 18.3 %collective-permute-start.14 = (bf16[224,1024]{1,0:T(8,128)(2,1)}, bf16[224,1024]{1,0:T(8,128)(2,1)S(1)}, u32[]{:S(2)}, u32[]{:S(2)}) collective-permute-start(bf16[224,1024]{1,0:T(8,128)(2,1)} %bitcast.15), channel_id=1, source_target_pairs={{0,3},{1,0},{2,1},{3,2},{4,7},{5,4},{6,5},{7,6},{8,11},{9,8},{10,9... | collective-permute-start | bytes 1376264 | tf_op jit(solution)/shard_map/ppermute | solution.py:347
  16.8 11.4 %collective-permute-start.5 = (bf16[224,1024]{1,0:T(8,128)(2,1)S(1)}, bf16[224,1024]{1,0:T(8,128)(2,1)S(1)}, u32[]{:S(2)}, u32[]{:S(2)}) collective-permute-start(bf16[224,1024]{1,0:T(8,128)(2,1)S(1)} %collective-permute-done.4.refs_1_), channel_id=1, source_target_pairs={{0,1},{1,2},{2,3},{3,0},{4,5},{5,6},{6,7},{7,4},{8,9},{9,10},{10,1... | collective-permute-start | bytes 1376264 | tf_op jit(solution)/shard_map/ppermute | solution.py:347
  18.2 12.7 %copy-start = (bf16[3584,640]{1,0:T(8,128)(2,1)S(1)}, bf16[3584,640]{1,0:T(8,128)(2,1)}, u32[]{:S(2)}) copy-start(bf16[3584,640]{1,0:T(8,128)(2,1)} %refs_3_.1) | copy-start | bytes 13762564
  18.2 10.6 %collective-permute-start.1 = (bf16[224,1024]{1,0:T(8,128)(2,1)S(1)}, bf16[224,1024]{1,0:T(8,128)(2,1)S(1)}, u32[]{:S(2)}, u32[]{:S(2)}) collective-permute-start(bf16[224,1024]{1,0:T(8,128)(2,1)S(1)} %collective-permute-done.refs_2_), channel_id=1, source_target_pairs={{0,12},{1,13},{2,14},{3,15},{4,0},{5,1},{6,2},{7,3},{8,4},{9,5},{1... | collective-permute-start | bytes 1376264 | tf_op jit(solution)/shard_map/ppermute | solution.py:347
  18.7 12.1 %collective-permute-start.12 = (bf16[224,1024]{1,0:T(8,128)(2,1)S(1)}, bf16[224,1024]{1,0:T(8,128)(2,1)S(1)}, u32[]{:S(2)}, u32[]{:S(2)}) collective-permute-start(bf16[224,1024]{1,0:T(8,128)(2,1)S(1)} %collective-permute-done.refs_2_), channel_id=1, source_target_pairs={{0,3},{1,0},{2,1},{3,2},{4,7},{5,4},{6,5},{7,6},{8,11},{9,8},{10,9... | collective-permute-start | bytes 1376264 | tf_op jit(solution)/shard_map/ppermute | solution.py:347
  22.7 17.2 %collective-permute-start.13 = (bf16[224,1024]{1,0:T(8,128)(2,1)S(1)}, bf16[224,1024]{1,0:T(8,128)(2,1)S(1)}, u32[]{:S(2)}, u32[]{:S(2)}) collective-permute-start(bf16[224,1024]{1,0:T(8,128)(2,1)S(1)} %collective-permute-done.4.refs_1_), channel_id=1, source_target_pairs={{0,4},{1,5},{2,6},{3,7},{4,8},{5,9},{6,10},{7,11},{8,12},{9,13},{1... | collective-permute-start | bytes 1376264 | tf_op jit(solution)/shard_map/ppermute | solution.py:347
  23.8 16.9 %collective-permute-start.8 = (bf16[224,1024]{1,0:T(8,128)(2,1)S(1)}, bf16[224,1024]{1,0:T(8,128)(2,1)S(1)}, u32[]{:S(2)}, u32[]{:S(2)}) collective-permute-start(bf16[224,1024]{1,0:T(8,128)(2,1)S(1)} %collective-permute-done.refs_2_), channel_id=1, source_target_pairs={{0,1},{1,2},{2,3},{3,0},{4,5},{5,6},{6,7},{7,4},{8,9},{9,10},{10,1... | collective-permute-start | bytes 1376264 | tf_op jit(solution)/shard_map/ppermute | solution.py:347
  28.1 14.7 %collective-permute-start.6 = (bf16[224,1024]{1,0:T(8,128)(2,1)S(1)}, bf16[224,1024]{1,0:T(8,128)(2,1)S(1)}, u32[]{:S(2)}, u32[]{:S(2)}) collective-permute-start(bf16[224,1024]{1,0:T(8,128)(2,1)S(1)} %collective-permute-done.5.refs_0_), channel_id=1, source_target_pairs={{0,12},{1,13},{2,14},{3,15},{4,0},{5,1},{6,2},{7,3},{8,4},{9,5},{1... | collective-permute-start | bytes 1376264 | tf_op jit(solution)/shard_map/ppermute | solution.py:347
  28.8 22.5 %collective-permute-start.10 = (bf16[224,1024]{1,0:T(8,128)(2,1)S(1)}, bf16[224,1024]{1,0:T(8,128)(2,1)S(1)}, u32[]{:S(2)}, u32[]{:S(2)}) collective-permute-start(bf16[224,1024]{1,0:T(8,128)(2,1)S(1)} %collective-permute-done.9.refs_4_), channel_id=1, source_target_pairs={{0,3},{1,0},{2,1},{3,2},{4,7},{5,4},{6,5},{7,6},{8,11},{9,8},{10,9... | collective-permute-start | bytes 1376264 | tf_op jit(solution)/shard_map/ppermute | solution.py:347
  30.8 20.6 %collective-permute-start.11 = (bf16[224,1024]{1,0:T(8,128)(2,1)S(1)}, bf16[224,1024]{1,0:T(8,128)(2,1)S(1)}, u32[]{:S(2)}, u32[]{:S(2)}) collective-permute-start(bf16[224,1024]{1,0:T(8,128)(2,1)S(1)} %collective-permute-done.5.refs_0_), channel_id=1, source_target_pairs={{0,4},{1,5},{2,6},{3,7},{4,8},{5,9},{6,10},{7,11},{8,12},{9,13},{1... | collective-permute-start | bytes 1376264 | tf_op jit(solution)/shard_map/ppermute | solution.py:347
  30.8 2.3 %copy-start.1 = (bf16[3584,640]{1,0:T(8,128)(2,1)S(1)}, bf16[3584,640]{1,0:T(8,128)(2,1)}, u32[]{:S(2)}) copy-start(bf16[3584,640]{1,0:T(8,128)(2,1)} %refs_4_.5) | copy-start | bytes 13762564
  39.9 17.3 %collective-permute-start.2 = (bf16[224,1024]{1,0:T(8,128)(2,1)S(1)}, bf16[224,1024]{1,0:T(8,128)(2,1)S(1)}, u32[]{:S(2)}, u32[]{:S(2)}) collective-permute-start(bf16[224,1024]{1,0:T(8,128)(2,1)S(1)} %collective-permute-done.1.refs_1_), channel_id=1, source_target_pairs={{0,1},{1,2},{2,3},{3,0},{4,5},{5,6},{6,7},{7,4},{8,9},{9,10},{10,1... | collective-permute-start | bytes 1376264 | tf_op jit(solution)/shard_map/ppermute | solution.py:347
  40.7 16.5 %collective-permute-start.3 = (bf16[224,1024]{1,0:T(8,128)(2,1)S(1)}, bf16[224,1024]{1,0:T(8,128)(2,1)S(1)}, u32[]{:S(2)}, u32[]{:S(2)}) collective-permute-start(bf16[224,1024]{1,0:T(8,128)(2,1)S(1)} %collective-permute-done.1.refs_1_), channel_id=1, source_target_pairs={{0,3},{1,0},{2,1},{3,2},{4,7},{5,4},{6,5},{7,6},{8,11},{9,8},{10,9... | collective-permute-start | bytes 1376264 | tf_op jit(solution)/shard_map/ppermute | solution.py:347
  42.8 14.4 %collective-permute-start.7 = (bf16[224,1024]{1,0:T(8,128)(2,1)S(1)}, bf16[224,1024]{1,0:T(8,128)(2,1)S(1)}, u32[]{:S(2)}, u32[]{:S(2)}) collective-permute-start(bf16[224,1024]{1,0:T(8,128)(2,1)S(1)} %collective-permute-done.6.refs_1_), channel_id=1, source_target_pairs={{0,12},{1,13},{2,14},{3,15},{4,0},{5,1},{6,2},{7,3},{8,4},{9,5},{1... | collective-permute-start | bytes 1376264 | tf_op jit(solution)/shard_map/ppermute | solution.py:347
  45.5 11.8 %slice-start = ((s8[4587520]{0:T(1024)(128)(4,1)}), s8[4194304]{0:T(1024)(128)(4,1)S(1)}, s32[]{:S(2)}) async-start(s8[4587520]{0:T(1024)(128)(4,1)} %bitcast.10), calls=%async_computation.1 | async-start | bytes 8388608
  51.3 5.9 %slice-start.1 = ((s8[4587520]{0:T(1024)(128)(4,1)}), s8[393216]{0:T(1024)(128)(4,1)S(1)}, s32[]{:S(2)}) async-start(s8[4587520]{0:T(1024)(128)(4,1)} %bitcast.10), calls=%async_computation.2 | async-start | bytes 786432
  51.3 5.9 %copy-start.2 = (bf16[1024,640]{1,0:T(8,128)(2,1)S(1)}, bf16[1024,640]{1,0:T(8,128)(2,1)}, u32[]{:S(2)}) copy-start(bf16[1024,640]{1,0:T(8,128)(2,1)} %refs_7_.1) | copy-start | bytes 3932164
  67.0 29.2 %all-to-all-start = ((f32[256,1,128]{2,1,0:T(1,128)}), f32[256,1,128]{2,1,0:T(1,128)S(1)}, u32[]{:S(2)}, u32[]{:S(2)}) async-start(f32[256,1,128]{2,1,0:T(1,128)} %bitcast.4), calls=%async_computation | async-start | bytes 262144 | tf_op jit(solution)/shard_map/all_to_all | solution.py:375
  90.6 1.1 %copy-start.4 = (bf16[1024,640]{1,0:T(8,128)(2,1)}, bf16[1024,640]{1,0:T(8,128)(2,1)S(1)}, u32[]{:S(2)}) copy-start(bf16[1024,640]{1,0:T(8,128)(2,1)S(1)} %get-tuple-element.19.right_up) | copy-start | bytes 3932164
  96.2 1.3 %copy-start.5 = (bf16[1024,640]{1,0:T(8,128)(2,1)S(1)}, bf16[1024,640]{1,0:T(8,128)(2,1)}, u32[]{:S(2)}) copy-start(bf16[1024,640]{1,0:T(8,128)(2,1)} %copy-done.4) | copy-start | bytes 3932164

commit v3 on v2

v3 whole, which is shorter than its diff:
```python
import math

import jax
import jax.numpy as jnp
from jax import lax
from jax.experimental import pallas as pl
from jax.experimental.pallas import tpu as pltpu
from jax.sharding import PartitionSpec as P

FF = 10240
ROWS = 64
SIGMA = 0.5
EPSILON = 1e-05
SEED_STEP = 747796405
CELL_STEP = 277803737

WAYS = {"+x": (1, 0), "-x": (3, 0), "+y": (0, 1), "-y": (0, 3)}
ROUNDS = (
    (((0, 0), "+x"), ((0, 0), "-y"), ((0, 0), "-x"), ((0, 0), "+y")),
    (((1, 0), "+x"), ((0, 3), "-y"), ((0, 3), "-x"), ((1, 0), "+y")),
    (((0, 3), "+x"), ((2, 0), "-y"), ((0, 1), "-x"), ((2, 0), "+y")),
    (((0, 2), "+x"), ((0, 2), "-x"), ((2, 3), "-y")),
)


def moved(place, way):
    return ((place[0] + WAYS[way][0]) % 4, (place[1] + WAYS[way][1]) % 4)


def pairs_of(way):
    dx, dy = WAYS[way]
    return [(y * 4 + x, (y + dy) % 4 * 4 + (x + dx) % 4) for y in range(4) for x in range(4)]


def source_of(place):
    me = lax.axis_index("mp")
    return lax.rem(me // 4 + 4 - place[1], 4) * 4 + lax.rem(lax.rem(me, 4) + 4 - place[0], 4)


def levels_of(mixed):
    mixed = jnp.bitwise_xor(mixed, jnp.right_shift(mixed, 15))
    mixed = mixed * 1664525 + 1013904223
    mixed = jnp.bitwise_xor(mixed, jnp.right_shift(mixed, 13))
    level = jnp.bitwise_and(mixed, 255).astype(jnp.float32) * (2.0 / 256.0) - 255.0 / 256.0
    return level.astype(jnp.bfloat16)


def iota(shape, dim):
    return lax.broadcasted_iota(jnp.int32, shape, dim)


def by_pair(shape, dim, pairs, seed_ref, first_pair):
    at = iota(shape, dim)
    mixed = lax.rem(at, 4) * CELL_STEP
    for p in range(pairs):
        mixed += jnp.where(at // 4 == p, seed_ref[first_pair + p] * SEED_STEP, 0)
    return mixed


def prepare_kernel(seed_ref, table_ref, gate_ref, up_ref):
    width = gate_ref.shape[1]
    first_pair = lax.axis_index("pop") * 16
    lane = iota((1, 128), 1)
    half = lax.rem(lane, 4) * CELL_STEP + jnp.where(lane >= 64, 33023, 11003)
    for p in range(16):
        half += jnp.where(lax.rem(lane, 64) // 4 == p, seed_ref[first_pair + p] * SEED_STEP, 0)

    @pl.loop(0, table_ref.shape[0] // 32)
    def _(r):
        at = pl.multiple_of(r * 32, 32)
        cell = (iota((32, 128), 0) + at) * (4 * CELL_STEP)
        table_ref[pl.ds(at, 32), :] = levels_of(half + cell)

    first_unit = lax.axis_index("mp") * width
    cell = (iota((16, width), 1) + first_unit) * (4 * CELL_STEP)
    nothing = jnp.zeros((64, width), jnp.bfloat16)
    for i in range(4):
        column = by_pair((16, width), 0, 4, seed_ref, first_pair + 4 * i)
        gate = levels_of(column + cell + 22013)
        up = levels_of(column + cell + 44041)
        for part in (0, 128):
            gate_ref[part + i * 16 : part + i * 16 + 16, :] = gate
            up_ref[part + 64 + i * 16 : part + 64 + i * 16 + 16, :] = up
    for part in (0, 128):
        gate_ref[part + 64 : part + 128, :] = nothing
        up_ref[part : part + 64, :] = nothing


def factor_kernel(seed_ref, message_ref, table_ref, lane_ref):
    pairs = seed_ref.shape[0]
    width = table_ref.shape[1] // 2
    count = (table_ref.shape[0] - 4 * pairs) // 2
    first = lax.axis_index("mp") * width
    rows = 16
    cell = (iota((rows, width), 1) + first) * (4 * CELL_STEP)

    @pl.loop(0, 4 * pairs // rows)
    def _(i):
        at = pl.multiple_of(i * rows, rows)
        column = by_pair((rows, 128), 0, 4, seed_ref, i * 4)
        mixed = jnp.concatenate([column] * (width // 128), axis=1) + cell
        table_ref[pl.ds(at, rows), :width] = levels_of(mixed + 22013)
        table_ref[pl.ds(at, rows), width:] = levels_of(mixed + 44041)

    left_first = lax.axis_index("pop") * count

    @pl.loop(0, 4 * pairs // 128)
    def _(q):
        lane_ref[...] = jnp.broadcast_to(by_pair((1, 128), 1, 32, seed_ref, q * 32), lane_ref.shape)
        columns = pl.ds(pl.multiple_of(q * 128, 128), 128)

        @pl.loop(0, count // 32)
        def _(i):
            at = pl.multiple_of(i * 32, 32)
            mixed = (iota((32, 128), 0) + (at + left_first)) * (4 * CELL_STEP) + lane_ref[0:1, :]
            table_ref[pl.ds(4 * pairs + at, 32), columns] = levels_of(mixed + 11003)
            table_ref[pl.ds(4 * pairs + count + at, 32), columns] = levels_of(mixed + 33023)


def contract(a, b):
    return lax.dot_general(a, b, (((0,), (0,)), ((), ())), preferred_element_type=jnp.float32)


def product_of(places, blocks, rows, gate_ref, up_ref, table_ref):
    depth = blocks[0].shape[0]
    tokens = jnp.concatenate([block[:, rows] for block in blocks], axis=0)
    weights = []
    for place in places:
        at = pl.ds(pl.multiple_of(source_of(place) * depth, 32), depth)
        weights.append(jnp.concatenate([gate_ref[at, :], up_ref[at, :], table_ref[at, :]], axis=1))
    return contract(tokens, jnp.concatenate(weights, axis=0))


def round_kernel(places, fresh, *refs):
    n = len(places)
    acc_ref, mark_ref = refs[-2:]
    mark_ref[...] = jnp.zeros_like(mark_ref)

    @pl.loop(0, acc_ref.shape[0] // 256)
    def _(i):
        rows = pl.ds(pl.multiple_of(i * 256, 256), 256)
        part = product_of(places, refs[:n], rows, *refs[n : n + 3])
        if fresh:
            acc_ref[rows, :] = part
        else:
            acc_ref[rows, :] = refs[n + 3][rows, :] + part


def last_kernel(places, *refs):
    n = len(places)
    blocks, weight_refs = refs[:n], refs[n : n + 3]
    acc_ref, target_ref, weight_ref, gate_out_ref, up_out_ref, message_ref = refs[n + 3 : n + 9]
    total_refs, side_refs, parts_ref = refs[n + 9 : n + 11], refs[n + 11 : n + 13], refs[n + 13]
    depth = blocks[0].shape[0]
    width = target_ref.shape[1]
    tile = 256
    tiles = acc_ref.shape[0] // tile
    scale = SIGMA / math.sqrt(16 * depth)
    lane_pair = lax.rem(iota((tile, 128), 1), 64) // 4
    row_pair = iota((tile, 128), 0) // ROWS

    def product(i):
        rows = pl.ds(i * tile, tile)
        part = product_of(places, blocks, rows, *weight_refs) + acc_ref[rows, :]
        total_refs[i % 2][...] = part[:, : 2 * width]
        low = jnp.where(lane_pair == row_pair + i * (tile // ROWS), part[:, 2 * width :] * scale, 0.0)
        high = low.astype(jnp.bfloat16)
        rest = (low - high.astype(jnp.float32)).astype(jnp.bfloat16)
        low_both = jnp.concatenate([high, rest], axis=1)
        side_refs[i % 2][:, :width] = jnp.dot(low_both, gate_out_ref[...], preferred_element_type=jnp.float32)
        side_refs[i % 2][:, width:] = jnp.dot(low_both, up_out_ref[...], preferred_element_type=jnp.float32)

    def errors(i):
        total_ref, side_ref = total_refs[i % 2], side_refs[i % 2]
        for p in range(tile // ROWS):
            k = i * (tile // ROWS) + p
            plus = jnp.zeros((8, width), jnp.float32)
            minus = jnp.zeros((8, width), jnp.float32)
            for q in range(ROWS // 16):
                at = p * ROWS + q * 16
                goals = target_ref[i * tile + at : i * tile + at + 16, :].astype(jnp.float32)
                for h in range(2):
                    here = slice(at + h * 8, at + h * 8 + 8)
                    goal = goals[h * 8 : h * 8 + 8, :]
                    gate, up = total_ref[here, :width], total_ref[here, width:]
                    side_gate, side_up = side_ref[here, :width], side_ref[here, width:]
                    half = 0.5 * (gate + side_gate)
                    error = (half * jnp.tanh(half) + half) * (up + side_up) - goal
                    plus += error * error
                    half = 0.5 * (gate - side_gate)
                    error = (half * jnp.tanh(half) + half) * (up - side_up) - goal
                    minus += error * error
            parts_ref[0, k : k + 1, :] = jnp.sum(plus, axis=0, keepdims=True) * weight_ref[...][None, :]
            parts_ref[1, k : k + 1, :] = jnp.sum(minus, axis=0, keepdims=True) * weight_ref[...][None, :]

    product(0)
    for i in range(tiles):
        if i + 1 < tiles:
            product(i + 1)
        errors(i)

    pairs = parts_ref.shape[1]
    lane = iota((pairs, 128), 1)
    pair = iota((pairs, 128), 0)
    line = jnp.zeros((1, 128), jnp.float32)
    for s in range(2):
        sums = jnp.sum(parts_ref[s], axis=1, keepdims=True) * (1.0 / (ROWS * FF))
        line += jnp.sum(jnp.where(lane // 4 == pair + 16 * s, sums, 0.0), axis=0, keepdims=True)
    message_ref[...] = jnp.broadcast_to(line, message_ref.shape)


def update_kernel(message_ref, table_hbm, out_gate_ref, out_up_ref, fit_ref, f_ref, table_ref, sems):
    rows, width = out_gate_ref.shape
    depth = table_ref.shape[0] - 2 * rows
    parts = []
    for k in range(2):
        left, right = pl.ds(depth + k * rows, rows), (pl.ds(0, depth), pl.ds(k * width, width))
        parts.append(pltpu.make_async_copy(table_hbm.at[left, :], table_ref.at[left, :], sems.at[2 * k]))
        parts.append(pltpu.make_async_copy(table_hbm.at[right], table_ref.at[right], sems.at[2 * k + 1]))
    for copy in parts:
        copy.start()
    count = message_ref.shape[0]
    pick_row, pick = iota((16, count), 0), iota((16, count), 1)
    chosen = pick // 16 == 2 * lax.rem(pick_row, 8) + pick_row // 8
    by_pop = jnp.dot(
        chosen.astype(jnp.float32),
        message_ref[...],
        precision=lax.Precision.HIGHEST,
        preferred_element_type=jnp.float32,
    )
    even, odd = by_pop[:8], by_pop[8:]
    low_lane = iota((8, 128), 1) < 64
    plus = jnp.where(low_lane, even, pltpu.roll(odd, 64, 1))
    minus = jnp.where(low_lane, pltpu.roll(even, 64, 1), odd)
    summed = jnp.concatenate([plus, minus], axis=0)
    scores = -summed
    members = 4.0 * 512.0
    center = jnp.sum(scores) / members
    spread = jnp.sum((scores - center) ** 2) / members
    fitness = (scores - center) / jnp.sqrt(jnp.full((16, 128), spread + EPSILON, jnp.float32))
    f_ref[...] = fitness
    factor = (fitness[:8] - fitness[8:]) * (0.5 / 16.0)
    for k, out_ref in enumerate((out_gate_ref, out_up_ref)):
        parts[2 * k].wait()
        highs, rests = [], []
        for q in range(8):
            left = table_ref[depth + k * rows : depth + (k + 1) * rows, q * 128 : (q + 1) * 128]
            scaled = left.astype(jnp.float32) * factor[q : q + 1, :]
            high = scaled.astype(jnp.bfloat16)
            highs.append(high)
            rests.append((scaled - high.astype(jnp.float32)).astype(jnp.bfloat16))
        both = jnp.concatenate([jnp.concatenate(highs, axis=1), jnp.concatenate(rests, axis=1)], axis=0)
        parts[2 * k + 1].wait()
        right = table_ref[:depth, k * width : (k + 1) * width]
        product = jnp.dot(both, right, preferred_element_type=jnp.float32)
        out_ref[...] = product[:rows] + product[rows:]
    pop = lax.axis_index("pop")
    mine = pop // 2
    lane, member = iota((128, 128), 0), iota((128, 128), 1)
    at = lane == lax.rem(pop, 2) * 64 + member // 2 * 4
    total = jnp.zeros((1, 128), jnp.float32)
    for s in range(2):
        line = jnp.broadcast_to(f_ref[pl.ds(mine + 8 * s, 1), :], (8, 128))
        select = (at & (lax.rem(member, 2) == s)).astype(jnp.float32)
        total += jnp.dot(line, select, precision=lax.Precision.HIGHEST, preferred_element_type=jnp.float32)[:1]
    fit_ref[...] = total[:, : fit_ref.shape[1]]


def params(mib):
    return pltpu.CompilerParams(vmem_limit_bytes=mib * 1024 * 1024)


def cost(flops, size):
    return pl.CostEstimate(flops=flops, bytes_accessed=size, transcendentals=0)


def after(value, other):
    return lax.optimization_barrier((value, other))[0]


def on_device(tokens, target, unit_weight, gate_weight, up_weight, seeds):
    rows_dev, depth = tokens.shape
    model_width, width = gate_weight.shape
    pairs_dev = rows_dev // ROWS
    pair_total = seeds.shape[0]
    device_total = lax.axis_size("pop") * lax.axis_size("mp")
    any_space = pl.BlockSpec(memory_space=pl.ANY)
    in_vmem = pl.BlockSpec(memory_space=pltpu.VMEM)
    bf16, f32 = jnp.bfloat16, jnp.float32

    in_smem = pl.BlockSpec(memory_space=pltpu.SMEM)
    columns = 2 * width + 128

    table, gate_out, up_out = pl.pallas_call(
        prepare_kernel,
        out_shape=[jax.ShapeDtypeStruct((model_width, 128), bf16)] + [jax.ShapeDtypeStruct((256, width), bf16)] * 2,
        in_specs=[in_smem],
        out_specs=[in_vmem] * 3,
        compiler_params=params(6),
        cost_estimate=cost(2_000_000_000, 2_000_000),
        name="prepare",
    )(seeds)
    weights = [gate_weight, up_weight, table]

    def multiply(places, acc):
        given = [blocks[place] for place in places] + weights + ([] if acc is None else [acc])
        return pl.pallas_call(
            lambda *refs: round_kernel(places, acc is None, *refs),
            out_shape=[jax.ShapeDtypeStruct((rows_dev, columns), f32), jax.ShapeDtypeStruct((8, 128), f32)],
            in_specs=[in_vmem] * len(given),
            out_specs=[in_vmem] * 2,
            input_output_aliases={} if acc is None else {len(given) - 1: 0},
            compiler_params=params(12),
            cost_estimate=cost(2 * rows_dev * len(places) * depth * columns, 4_000_000),
            name="round_of_%d" % len(places),
        )(*given)

    blocks = {(0, 0): tokens.T}
    acc, mark = None, gate_out
    held = [(0, 0)]
    for number, sends in enumerate(ROUNDS):
        fresh = {}
        for place, way in sends:
            block = blocks[place]
            if number > 0:
                block = after(block, mark)
            fresh[moved(place, way)] = lax.ppermute(block, "mp", pairs_of(way))
        if number > 0:
            acc, mark = multiply(held, acc)
            held = []
        held += list(fresh)
        blocks.update(fresh)

    message = pl.pallas_call(
        lambda *refs: last_kernel(held, *refs),
        out_shape=jax.ShapeDtypeStruct((device_total, 128), f32),
        in_specs=[in_vmem] * (len(held) + 8),
        out_specs=in_vmem,
        scratch_shapes=[pltpu.VMEM((256, 2 * width), f32)] * 4 + [pltpu.VMEM((2, pairs_dev, width), f32)],
        compiler_params=params(16),
        cost_estimate=cost(2 * rows_dev * len(held) * depth * columns, 12_000_000),
        name="last_round",
    )(*[blocks[place] for place in held], *weights, acc, target, unit_weight, gate_out, up_out)

    received = lax.all_to_all(message, ("pop", "mp"), 0, 0, tiled=True)

    left_rows = model_width // lax.axis_size("pop")
    factors = pl.pallas_call(
        factor_kernel,
        out_shape=jax.ShapeDtypeStruct((4 * pair_total + 2 * left_rows, 2 * width), bf16),
        in_specs=[in_smem, any_space],
        out_specs=in_vmem,
        scratch_shapes=[pltpu.VMEM((8, 128), jnp.int32)],
        compiler_params=params(8),
        cost_estimate=cost(3_000_000_000, 4_000_000),
        name="factor_tables",
    )(seeds, message)
    update_gate, update_up, fitness = pl.pallas_call(
        update_kernel,
        out_shape=[jax.ShapeDtypeStruct((left_rows, width), f32)] * 2
        + [jax.ShapeDtypeStruct((1, 2 * pairs_dev), f32)],
        in_specs=[in_vmem, any_space],
        out_specs=[in_vmem] * 3,
        scratch_shapes=[
            pltpu.VMEM((16, 128), f32),
            pltpu.VMEM(factors.shape, bf16),
            pltpu.SemaphoreType.DMA((4,)),
        ],
        compiler_params=params(58),
        cost_estimate=cost(1_200_000_000, 5_000_000),
        name="update",
    )(received, factors)
    return (update_gate, update_up, fitness.reshape(2 * pairs_dev))


def solution(mesh):
    return jax.shard_map(
        on_device,
        mesh=mesh,
        in_specs=(P("pop", "mp"), P("pop", "mp"), P("mp"), P(None, "mp"), P(None, "mp"), P()),
        out_specs=(P("pop", "mp"), P("pop", "mp"), P("pop")),
        check_vma=False,
    )
```

time: 102 us -> 92.7 us (0.909)
  Pallas kernels: 40.3 us -> 35.6 us
  waiting for transfers between devices: 17.7 us -> 14.6 us
  other arithmetic: 1.05 us -> 0.01 us
    ppermute x15, waiting for transfers between devices: 13.2 us -> 8.58 us  [on_device(): fresh[moved(place, way)] = lax.ppermute(block, 'mp', pairs_of(way))]
    pallas_call x3, Pallas kernels: 18.4 us -> 14.8 us  [multiply(): pl.pallas_call(lambda *refs: round_kernel(places, acc is None, *refs), ou...]
    ppermute x15, starting transfers between devices: 18.7 us -> 21.5 us  [on_device(): fresh[moved(place, way)] = lax.ppermute(block, 'mp', pairs_of(way))]
    pallas_call x1, Pallas kernels: 9.47 us -> 7.16 us  [on_device(): pl.pallas_call(lambda *refs: last_kernel(held, *refs), out_shape=jax.Shap...]
    pallas_call x1, Pallas kernels: 3.65 us -> 5.71 us  [on_device(): pl.pallas_call(update_kernel, out_shape=[jax.ShapeDtypeStruct((left_rows,...]
    all_to_all x1, starting transfers between devices: 16.2 us -> 14.4 us  [on_device(): received = lax.all_to_all(message, ('pop', 'mp'), 0, 0, tiled=True)]
    all_to_all x1, waiting for transfers between devices: 4.5 us -> 5.97 us  [on_device(): received = lax.all_to_all(message, ('pop', 'mp'), 0, 0, tiled=True)]
    pallas_call x3 -> x2, Pallas kernels: 8.79 us -> 8 us  [the longest x1 5.2 us: on_device(): pl.pallas_call(factor_kernel, out_shape=jax.ShapeDtypeStruct((4 * pair_to...]
  transfers between devices with their start and end apart: 16 -> 16, of which waited for: 3 -> 7; matrix products, arithmetic and copies ran while one was open for 2% -> 0% of each run, Pallas kernels for 27% -> 25%
where the time goes in v3:
time: 92.7 us; the launch traced here: 92.5 us
  starting transfers between devices  35.9 us (39%)
  Pallas kernels  35.6 us (38%)
  waiting for transfers between devices  14.6 us (16%)
  local copies, waits for them, and re-layouts  5.45 us (6%)
  between operations  0.94 us (1%)
    ppermute x15, starting transfers between devices, on_device(): fresh[moved(place, way)] = lax.ppermute(block, 'mp', pairs_of(way))  21.5 us
    pallas_call x3, Pallas kernels, multiply(): pl.pallas_call(lambda *refs: round_kernel(places, acc is None, *refs), ou...  14.8 us
    all_to_all x1, starting transfers between devices, on_device(): received = lax.all_to_all(message, ('pop', 'mp'), 0, 0, tiled=True)  14.4 us
    ppermute x15, waiting for transfers between devices, on_device(): fresh[moved(place, way)] = lax.ppermute(block, 'mp', pairs_of(way))  8.58 us
    pallas_call x1, Pallas kernels, on_device(): pl.pallas_call(lambda *refs: last_kernel(held, *refs), out_shape=jax.Shap...  7.16 us
    all_to_all x1, waiting for transfers between devices, on_device(): received = lax.all_to_all(message, ('pop', 'mp'), 0, 0, tiled=True)  5.97 us
    pallas_call x1, Pallas kernels, on_device(): pl.pallas_call(update_kernel, out_shape=[jax.ShapeDtypeStruct((left_rows,...  5.71 us
    unnamed x22, local copies, waits for them, and re-layouts  5.45 us
  transfers between devices with their start and end apart: 16, of which 7 were waited for; matrix products, arithmetic and copies ran while one was open for 0% of the time, Pallas kernels for 25%

profile of v3, /device:TPU:1, one launch (start us, length us, event | category | flops | bytes accessed | tf_op | source)
XLA Modules:
  0.0 92.5 jit_solution(4569595471077097069)
XLA Ops:
  0.6 0.0 copy-start.3
  0.6 0.0 copy-start
  0.6 2.1 %collective-permute-start.2 = (bf16[224,1024]{1,0:T(8,128)(2,1)}, bf16[224,1024]{1,0:T(8,128)(2,1)S(1)}, u32[]{:S(2)}, u32[]{:S(2)}) collective-permute-start(bf16[224,1024]{1,0:T(8,128)(2,1)} %bitcast.8), channel_id=1, source_target_pairs={{0,1},{1,2},{2,3},{3,0},{4,5},{5,6},{6,7},{7,4},{8,9},{9,10},{10,1... | collective-permute-start | bytes 1376264 | tf_op jit(solution)/shard_map/ppermute | solution.py:327
  2.8 2.7 %collective-permute-start = (bf16[224,1024]{1,0:T(8,128)(2,1)}, bf16[224,1024]{1,0:T(8,128)(2,1)S(1)}, u32[]{:S(2)}, u32[]{:S(2)}) collective-permute-start(bf16[224,1024]{1,0:T(8,128)(2,1)} %bitcast.9), channel_id=1, source_target_pairs={{0,12},{1,13},{2,14},{3,15},{4,0},{5,1},{6,2},{7,3},{8,4},{9,5},{1... | collective-permute-start | bytes 1376264 | tf_op jit(solution)/shard_map/ppermute | solution.py:327
  5.5 0.0 collective-permute-start.7
  5.5 1.5 %collective-permute-start.6 = (bf16[224,1024]{1,0:T(8,128)(2,1)}, bf16[224,1024]{1,0:T(8,128)(2,1)S(1)}, u32[]{:S(2)}, u32[]{:S(2)}) collective-permute-start(bf16[224,1024]{1,0:T(8,128)(2,1)} %bitcast.11), channel_id=1, source_target_pairs={{0,3},{1,0},{2,1},{3,2},{4,7},{5,4},{6,5},{7,6},{8,11},{9,8},{10,9... | collective-permute-start | bytes 1376264 | tf_op jit(solution)/shard_map/ppermute | solution.py:327
  7.0 0.0 copy-start.5
  7.0 0.7 copy-done.5
  7.7 2.8 %prepare.1 = (bf16[3584,128]{1,0:T(8,128)(2,1)S(1)}, bf16[256,640]{1,0:T(8,128)(2,1)S(1)}, bf16[256,640]{1,0:T(8,128)(2,1)S(1)}) custom-call(s32[256]{0:T(256)S(1)} %copy-done.5), custom_call_target="tpu_custom_call" | custom-call | flops 2000000000 | bytes 2000000 | tf_op jit(solution)/shard_map/prepare/pallas_call | solution.py:294
  10.5 1.7 %collective-permute-done.2.refs_1_ = bf16[224,1024]{1,0:T(8,128)(2,1)S(1)} collective-permute-done((bf16[224,1024]{1,0:T(8,128)(2,1)}, bf16[224,1024]{1,0:T(8,128)(2,1)S(1)}, u32[]{:S(2)}, u32[]{:S(2)}) %collective-permute-start.2) | collective-permute-done | bytes 458784 | tf_op jit(solution)/shard_map/ppermute | solution.py:327
  12.2 1.9 %collective-permute-start.3 = (bf16[224,1024]{1,0:T(8,128)(2,1)S(1)}, bf16[224,1024]{1,0:T(8,128)(2,1)S(1)}, u32[]{:S(2)}, u32[]{:S(2)}) collective-permute-start(bf16[224,1024]{1,0:T(8,128)(2,1)S(1)} %collective-permute-done.2.refs_1_), channel_id=1, source_target_pairs={{0,1},{1,2},{2,3},{3,0},{4,5},{5,6},{6,7},{7,4},{8,9},{9,10},{10,1... | collective-permute-start | bytes 1376264 | tf_op jit(solution)/shard_map/ppermute | solution.py:327
  14.1 0.6 collective-permute-done.refs_2_
  14.7 1.5 %collective-permute-start.4 = (bf16[224,1024]{1,0:T(8,128)(2,1)S(1)}, bf16[224,1024]{1,0:T(8,128)(2,1)S(1)}, u32[]{:S(2)}, u32[]{:S(2)}) collective-permute-start(bf16[224,1024]{1,0:T(8,128)(2,1)S(1)} %collective-permute-done.refs_2_), channel_id=1, source_target_pairs={{0,3},{1,0},{2,1},{3,2},{4,7},{5,4},{6,5},{7,6},{8,11},{9,8},{10,9... | collective-permute-start | bytes 1376264 | tf_op jit(solution)/shard_map/ppermute | solution.py:327
  16.2 3.6 %collective-permute-start.1 = (bf16[224,1024]{1,0:T(8,128)(2,1)S(1)}, bf16[224,1024]{1,0:T(8,128)(2,1)S(1)}, u32[]{:S(2)}, u32[]{:S(2)}) collective-permute-start(bf16[224,1024]{1,0:T(8,128)(2,1)S(1)} %collective-permute-done.refs_2_), channel_id=1, source_target_pairs={{0,12},{1,13},{2,14},{3,15},{4,0},{5,1},{6,2},{7,3},{8,4},{9,5},{1... | collective-permute-start | bytes 1376264 | tf_op jit(solution)/shard_map/ppermute | solution.py:327
  19.8 0.0 collective-permute-done.7.refs_4_
  19.8 0.0 collective-permute-start.5
  19.8 0.0 collective-permute-done.6.refs_3_
  19.8 0.0 copy-done.3
  19.8 0.0 copy-done
  19.8 0.0 copy-start.1
  19.8 2.3 %copy-done.1 = bf16[3584,640]{1,0:T(8,128)(2,1)S(1)} copy-done((bf16[3584,640]{1,0:T(8,128)(2,1)S(1)}, bf16[3584,640]{1,0:T(8,128)(2,1)}, u32[]{:S(2)}) %copy-start.1) | copy-done | bytes 4587544
  22.1 5.1 %round_of_5.1 = (f32[1024,1408]{1,0:T(8,128)S(1)}, f32[8,128]{1,0:T(8,128)}) custom-call(bf16[224,1024]{1,0:T(8,128)(2,1)S(1)} %bitcast.12, bf16[224,1024]{1,0:T(8,128)(2,1)S(1)} %collective-permute-done.2.refs_1_, bf16[224,1024]{1,0:T(8,128)(2,1)S(1)} %collective-permute-done.refs_2_, bf16[224,1024]{1,0:T(8,128)(2,1)S(1)} %collective-permute-done.6.refs_3_, ...), custom_call_target="tpu_custom_call" | custom-call | flops 3229614080 | bytes 4000000 | tf_op jit(solution)/shard_map/round_of_5/pallas_call | solution.py:307
  27.2 0.0 collective-permute-done.3.refs_0_
  27.2 2.7 %collective-permute-start.10 = (bf16[224,1024]{1,0:T(8,128)(2,1)S(1)}, bf16[224,1024]{1,0:T(8,128)(2,1)S(1)}, u32[]{:S(2)}, u32[]{:S(2)}) collective-permute-start(bf16[224,1024]{1,0:T(8,128)(2,1)S(1)} %collective-permute-done.3.refs_0_), channel_id=1, source_target_pairs={{0,12},{1,13},{2,14},{3,15},{4,0},{5,1},{6,2},{7,3},{8,4},{9,5},{1... | collective-permute-start | bytes 1376264 | tf_op jit(solution)/shard_map/ppermute | solution.py:327
  29.9 0.0 collective-permute-start.12
  29.9 0.0 collective-permute-done.4.refs_2_
  29.9 2.7 %collective-permute-start.13 = (bf16[224,1024]{1,0:T(8,128)(2,1)S(1)}, bf16[224,1024]{1,0:T(8,128)(2,1)S(1)}, u32[]{:S(2)}, u32[]{:S(2)}) collective-permute-start(bf16[224,1024]{1,0:T(8,128)(2,1)S(1)} %collective-permute-done.7.refs_4_), channel_id=1, source_target_pairs={{0,3},{1,0},{2,1},{3,2},{4,7},{5,4},{6,5},{7,6},{8,11},{9,8},{10,9... | collective-permute-start | bytes 1376264 | tf_op jit(solution)/shard_map/ppermute | solution.py:327
  32.6 0.0 collective-permute-done.1.refs_1_
  32.6 0.0 collective-permute-start.14
  32.6 0.0 collective-permute-done.5.refs_3_
  32.6 0.0 slice-start
  32.6 4.8 %round_of_4.2 = (f32[1024,1408]{1,0:T(8,128)S(1)}, f32[8,128]{1,0:T(8,128)}) custom-call(bf16[224,1024]{1,0:T(8,128)(2,1)S(1)} %collective-permute-done.3.refs_0_, bf16[224,1024]{1,0:T(8,128)(2,1)S(1)} %collective-permute-done.1.refs_1_, bf16[224,1024]{1,0:T(8,128)(2,1)S(1)} %collective-permute-done.4.refs_2_, ...), custom_call_target="tpu_custom_call", output_to_operand_aliasing={{0}: (7, {})} | custom-call | flops 2583691264 | bytes 4000000 | tf_op jit(solution)/shard_map/round_of_4/pallas_call | solution.py:307
  37.4 0.1 collective-permute-start.9
  37.5 0.0 collective-permute-done.10.refs_1_
  37.5 1.4 %collective-permute-start.8 = (bf16[224,1024]{1,0:T(8,128)(2,1)S(1)}, bf16[224,1024]{1,0:T(8,128)(2,1)S(1)}, u32[]{:S(2)}, u32[]{:S(2)}) collective-permute-start(bf16[224,1024]{1,0:T(8,128)(2,1)S(1)} %collective-permute-done.1.refs_1_), channel_id=1, source_target_pairs={{0,1},{1,2},{2,3},{3,0},{4,5},{5,6},{6,7},{7,4},{8,9},{9,10},{10,1... | collective-permute-start | bytes 1376264 | tf_op jit(solution)/shard_map/ppermute | solution.py:327
  38.9 1.3 %collective-permute-done.12.refs_0_ = bf16[224,1024]{1,0:T(8,128)(2,1)S(1)} collective-permute-done((bf16[224,1024]{1,0:T(8,128)(2,1)S(1)}, bf16[224,1024]{1,0:T(8,128)(2,1)S(1)}, u32[]{:S(2)}, u32[]{:S(2)}) %collective-permute-start.12) | collective-permute-done | bytes 458784 | tf_op jit(solution)/shard_map/ppermute | solution.py:327
  40.2 1.4 %collective-permute-start.11 = (bf16[224,1024]{1,0:T(8,128)(2,1)S(1)}, bf16[224,1024]{1,0:T(8,128)(2,1)S(1)}, u32[]{:S(2)}, u32[]{:S(2)}) collective-permute-start(bf16[224,1024]{1,0:T(8,128)(2,1)S(1)} %collective-permute-done.10.refs_1_), channel_id=1, source_target_pairs={{0,12},{1,13},{2,14},{3,15},{4,0},{5,1},{6,2},{7,3},{8,4},{9,5},{1... | collective-permute-start | bytes 1376264 | tf_op jit(solution)/shard_map/ppermute | solution.py:327
  41.5 0.0 collective-permute-done.13.refs_2_
  41.6 0.8 collective-permute-done.14.refs_3_
  42.3 0.0 slice-start.1
  42.3 0.0 copy-start.2
  42.3 0.0 copy-start.4
  42.3 4.8 %round_of_4.3 = (f32[1024,1408]{1,0:T(8,128)S(1)}, f32[8,128]{1,0:T(8,128)}) custom-call(bf16[224,1024]{1,0:T(8,128)(2,1)S(1)} %collective-permute-done.12.refs_0_, bf16[224,1024]{1,0:T(8,128)(2,1)S(1)} %collective-permute-done.10.refs_1_, bf16[224,1024]{1,0:T(8,128)(2,1)S(1)} %collective-permute-done.13.refs_2_, ...), custom_call_target="tpu_custom_call", output_to_operand_aliasing={{0}: (7, {})} | custom-call | flops 2583691264 | bytes 4000000 | tf_op jit(solution)/shard_map/round_of_4/pallas_call | solution.py:307
  47.2 2.9 %collective-permute-done.9.refs_1_ = bf16[224,1024]{1,0:T(8,128)(2,1)S(1)} collective-permute-done((bf16[224,1024]{1,0:T(8,128)(2,1)S(1)}, bf16[224,1024]{1,0:T(8,128)(2,1)S(1)}, u32[]{:S(2)}, u32[]{:S(2)}) %collective-permute-start.9) | collective-permute-done | bytes 458784 | tf_op jit(solution)/shard_map/ppermute | solution.py:327
  50.0 1.3 %collective-permute-done.8.refs_0_ = bf16[224,1024]{1,0:T(8,128)(2,1)S(1)} collective-permute-done((bf16[224,1024]{1,0:T(8,128)(2,1)S(1)}, bf16[224,1024]{1,0:T(8,128)(2,1)S(1)}, u32[]{:S(2)}, u32[]{:S(2)}) %collective-permute-start.8) | collective-permute-done | bytes 458784 | tf_op jit(solution)/shard_map/ppermute | solution.py:327
  51.3 0.0 collective-permute-done.11.refs_2_
  51.3 0.0 slice-done
  51.3 0.0 slice-done.1
  51.3 0.0 copy-done.2
  51.4 0.0 copy-done.4
  51.4 0.0 copy-start.6
  51.4 7.2 %last_round.1.message_ref = f32[256,128]{1,0:T(8,128)} custom-call(bf16[224,1024]{1,0:T(8,128)(2,1)S(1)} %collective-permute-done.8.refs_0_, bf16[224,1024]{1,0:T(8,128)(2,1)S(1)} %collective-permute-done.9.refs_1_, bf16[224,1024]{1,0:T(8,128)(2,1)S(1)} %collective-permute-done.11.refs_2_, bf16[3584,640]{1,0:T(8,128)(2,1)S(1)} %copy-done, ...), custom_call_target="tpu_custom_call" | custom-call | flops 1937768448 | bytes 12000000 | tf_op jit(solution)/shard_map/last_round/pallas_call | solution.py:334
  58.5 14.4 %all-to-all-start = ((f32[256,1,128]{2,1,0:T(1,128)}), f32[256,1,128]{2,1,0:T(1,128)S(1)}, u32[]{:S(2)}, u32[]{:S(2)}) async-start(f32[256,1,128]{2,1,0:T(1,128)} %bitcast.2), calls=%async_computation | async-start | bytes 262144 | tf_op jit(solution)/shard_map/all_to_all | solution.py:345
  73.0 0.0 copy-done.6
  73.0 5.2 %factor_tables.1.table_hbm = bf16[1472,1280]{1,0:T(8,128)(2,1)S(1)} custom-call(s32[256]{0:T(256)S(1)} %copy-done.6, f32[256,128]{1,0:T(8,128)} %last_round.1.message_ref), custom_call_target="tpu_custom_call" | custom-call | flops 3000000000 | bytes 4000000 | tf_op jit(solution)/shard_map/factor_tables/pallas_call | solution.py:348
  78.2 0.0 copy-start.7
  78.2 1.8 %copy-done.7 = bf16[1472,1280]{1,0:T(8,128)(2,1)} copy-done((bf16[1472,1280]{1,0:T(8,128)(2,1)}, bf16[1472,1280]{1,0:T(8,128)(2,1)S(1)}, u32[]{:S(2)}) %copy-start.7) | copy-done | bytes 3768344
  80.0 6.0 %all-to-all-done = f32[256,1,128]{2,1,0:T(1,128)S(1)} async-done(((f32[256,1,128]{2,1,0:T(1,128)}), f32[256,1,128]{2,1,0:T(1,128)S(1)}, u32[]{:S(2)}, u32[]{:S(2)}) %all-to-all-start) | async-done | bytes 131104 | tf_op jit(solution)/shard_map/all_to_all | solution.py:345
  86.0 0.0 copy-start.8
  86.0 0.6 copy-done.8
  86.6 5.7 %update.1 = (f32[224,640]{1,0:T(8,128)}, f32[224,640]{1,0:T(8,128)}, f32[1,32]{1,0:T(1,128)}) custom-call(f32[256,128]{1,0:T(8,128)} %bitcast.13, bf16[1472,1280]{1,0:T(8,128)(2,1)} %copy-done.7), custom_call_target="tpu_custom_call" | custom-call | flops 1200000000 | bytes 5000000 | tf_op jit(solution)/shard_map/update/pallas_call | solution.py:358
  (1 shorter events, 0.0 us)
Async XLA Ops:
  0.6 19.2 %copy-start.3 = (bf16[1024,224]{0,1:T(8,128)(2,1)S(1)}, bf16[1024,224]{0,1:T(8,128)(2,1)}, u32[]{:S(2)}) copy-start(bf16[1024,224]{0,1:T(8,128)(2,1)} %param.6) | copy-start | bytes 1376260
  0.6 19.2 %copy-start = (bf16[3584,640]{1,0:T(8,128)(2,1)S(1)}, bf16[3584,640]{1,0:T(8,128)(2,1)}, u32[]{:S(2)}) copy-start(bf16[3584,640]{1,0:T(8,128)(2,1)} %refs_3_.1) | copy-start | bytes 13762564
  0.6 11.5 %collective-permute-start.2 = (bf16[224,1024]{1,0:T(8,128)(2,1)}, bf16[224,1024]{1,0:T(8,128)(2,1)S(1)}, u32[]{:S(2)}, u32[]{:S(2)}) collective-permute-start(bf16[224,1024]{1,0:T(8,128)(2,1)} %bitcast.8), channel_id=1, source_target_pairs={{0,1},{1,2},{2,3},{3,0},{4,5},{5,6},{6,7},{7,4},{8,9},{9,10},{10,1... | collective-permute-start | bytes 1376264 | tf_op jit(solution)/shard_map/ppermute | solution.py:327
  2.8 11.9 %collective-permute-start = (bf16[224,1024]{1,0:T(8,128)(2,1)}, bf16[224,1024]{1,0:T(8,128)(2,1)S(1)}, u32[]{:S(2)}, u32[]{:S(2)}) collective-permute-start(bf16[224,1024]{1,0:T(8,128)(2,1)} %bitcast.9), channel_id=1, source_target_pairs={{0,12},{1,13},{2,14},{3,15},{4,0},{5,1},{6,2},{7,3},{8,4},{9,5},{1... | collective-permute-start | bytes 1376264 | tf_op jit(solution)/shard_map/ppermute | solution.py:327
  5.5 14.3 %collective-permute-start.7 = (bf16[224,1024]{1,0:T(8,128)(2,1)}, bf16[224,1024]{1,0:T(8,128)(2,1)S(1)}, u32[]{:S(2)}, u32[]{:S(2)}) collective-permute-start(bf16[224,1024]{1,0:T(8,128)(2,1)} %bitcast.10), channel_id=1, source_target_pairs={{0,4},{1,5},{2,6},{3,7},{4,8},{5,9},{6,10},{7,11},{8,12},{9,13},{1... | collective-permute-start | bytes 1376264 | tf_op jit(solution)/shard_map/ppermute | solution.py:327
  5.5 14.3 %collective-permute-start.6 = (bf16[224,1024]{1,0:T(8,128)(2,1)}, bf16[224,1024]{1,0:T(8,128)(2,1)S(1)}, u32[]{:S(2)}, u32[]{:S(2)}) collective-permute-start(bf16[224,1024]{1,0:T(8,128)(2,1)} %bitcast.11), channel_id=1, source_target_pairs={{0,3},{1,0},{2,1},{3,2},{4,7},{5,4},{6,5},{7,6},{8,11},{9,8},{10,9... | collective-permute-start | bytes 1376264 | tf_op jit(solution)/shard_map/ppermute | solution.py:327
  7.0 0.7 copy-start.5
  12.2 15.1 %collective-permute-start.3 = (bf16[224,1024]{1,0:T(8,128)(2,1)S(1)}, bf16[224,1024]{1,0:T(8,128)(2,1)S(1)}, u32[]{:S(2)}, u32[]{:S(2)}) collective-permute-start(bf16[224,1024]{1,0:T(8,128)(2,1)S(1)} %collective-permute-done.2.refs_1_), channel_id=1, source_target_pairs={{0,1},{1,2},{2,3},{3,0},{4,5},{5,6},{6,7},{7,4},{8,9},{9,10},{10,1... | collective-permute-start | bytes 1376264 | tf_op jit(solution)/shard_map/ppermute | solution.py:327
  14.7 15.2 %collective-permute-start.4 = (bf16[224,1024]{1,0:T(8,128)(2,1)S(1)}, bf16[224,1024]{1,0:T(8,128)(2,1)S(1)}, u32[]{:S(2)}, u32[]{:S(2)}) collective-permute-start(bf16[224,1024]{1,0:T(8,128)(2,1)S(1)} %collective-permute-done.refs_2_), channel_id=1, source_target_pairs={{0,3},{1,0},{2,1},{3,2},{4,7},{5,4},{6,5},{7,6},{8,11},{9,8},{10,9... | collective-permute-start | bytes 1376264 | tf_op jit(solution)/shard_map/ppermute | solution.py:327
  16.2 16.4 %collective-permute-start.1 = (bf16[224,1024]{1,0:T(8,128)(2,1)S(1)}, bf16[224,1024]{1,0:T(8,128)(2,1)S(1)}, u32[]{:S(2)}, u32[]{:S(2)}) collective-permute-start(bf16[224,1024]{1,0:T(8,128)(2,1)S(1)} %collective-permute-done.refs_2_), channel_id=1, source_target_pairs={{0,12},{1,13},{2,14},{3,15},{4,0},{5,1},{6,2},{7,3},{8,4},{9,5},{1... | collective-permute-start | bytes 1376264 | tf_op jit(solution)/shard_map/ppermute | solution.py:327
  19.8 12.8 %collective-permute-start.5 = (bf16[224,1024]{1,0:T(8,128)(2,1)S(1)}, bf16[224,1024]{1,0:T(8,128)(2,1)S(1)}, u32[]{:S(2)}, u32[]{:S(2)}) collective-permute-start(bf16[224,1024]{1,0:T(8,128)(2,1)S(1)} %collective-permute-done.2.refs_1_), channel_id=1, source_target_pairs={{0,4},{1,5},{2,6},{3,7},{4,8},{5,9},{6,10},{7,11},{8,12},{9,13},{1... | collective-permute-start | bytes 1376264 | tf_op jit(solution)/shard_map/ppermute | solution.py:327
  19.8 2.3 %copy-start.1 = (bf16[3584,640]{1,0:T(8,128)(2,1)S(1)}, bf16[3584,640]{1,0:T(8,128)(2,1)}, u32[]{:S(2)}) copy-start(bf16[3584,640]{1,0:T(8,128)(2,1)} %refs_4_.5) | copy-start | bytes 13762564
  27.2 10.3 %collective-permute-start.10 = (bf16[224,1024]{1,0:T(8,128)(2,1)S(1)}, bf16[224,1024]{1,0:T(8,128)(2,1)S(1)}, u32[]{:S(2)}, u32[]{:S(2)}) collective-permute-start(bf16[224,1024]{1,0:T(8,128)(2,1)S(1)} %collective-permute-done.3.refs_0_), channel_id=1, source_target_pairs={{0,12},{1,13},{2,14},{3,15},{4,0},{5,1},{6,2},{7,3},{8,4},{9,5},{1... | collective-permute-start | bytes 1376264 | tf_op jit(solution)/shard_map/ppermute | solution.py:327
  29.9 10.3 %collective-permute-start.12 = (bf16[224,1024]{1,0:T(8,128)(2,1)S(1)}, bf16[224,1024]{1,0:T(8,128)(2,1)S(1)}, u32[]{:S(2)}, u32[]{:S(2)}) collective-permute-start(bf16[224,1024]{1,0:T(8,128)(2,1)S(1)} %collective-permute-done.refs_2_), channel_id=1, source_target_pairs={{0,1},{1,2},{2,3},{3,0},{4,5},{5,6},{6,7},{7,4},{8,9},{9,10},{10,1... | collective-permute-start | bytes 1376264 | tf_op jit(solution)/shard_map/ppermute | solution.py:327
  29.9 11.6 %collective-permute-start.13 = (bf16[224,1024]{1,0:T(8,128)(2,1)S(1)}, bf16[224,1024]{1,0:T(8,128)(2,1)S(1)}, u32[]{:S(2)}, u32[]{:S(2)}) collective-permute-start(bf16[224,1024]{1,0:T(8,128)(2,1)S(1)} %collective-permute-done.7.refs_4_), channel_id=1, source_target_pairs={{0,3},{1,0},{2,1},{3,2},{4,7},{5,4},{6,5},{7,6},{8,11},{9,8},{10,9... | collective-permute-start | bytes 1376264 | tf_op jit(solution)/shard_map/ppermute | solution.py:327
  32.6 9.7 %collective-permute-start.14 = (bf16[224,1024]{1,0:T(8,128)(2,1)S(1)}, bf16[224,1024]{1,0:T(8,128)(2,1)S(1)}, u32[]{:S(2)}, u32[]{:S(2)}) collective-permute-start(bf16[224,1024]{1,0:T(8,128)(2,1)S(1)} %collective-permute-done.3.refs_0_), channel_id=1, source_target_pairs={{0,4},{1,5},{2,6},{3,7},{4,8},{5,9},{6,10},{7,11},{8,12},{9,13},{1... | collective-permute-start | bytes 1376264 | tf_op jit(solution)/shard_map/ppermute | solution.py:327
  32.6 18.7 %slice-start = ((s8[4587520]{0:T(1024)(128)(4,1)}), s8[4194304]{0:T(1024)(128)(4,1)S(1)}, s32[]{:S(2)}) async-start(s8[4587520]{0:T(1024)(128)(4,1)} %bitcast.6), calls=%async_computation.1 | async-start | bytes 8388608
  37.4 12.6 %collective-permute-start.9 = (bf16[224,1024]{1,0:T(8,128)(2,1)S(1)}, bf16[224,1024]{1,0:T(8,128)(2,1)S(1)}, u32[]{:S(2)}, u32[]{:S(2)}) collective-permute-start(bf16[224,1024]{1,0:T(8,128)(2,1)S(1)} %collective-permute-done.1.refs_1_), channel_id=1, source_target_pairs={{0,3},{1,0},{2,1},{3,2},{4,7},{5,4},{6,5},{7,6},{8,11},{9,8},{10,9... | collective-permute-start | bytes 1376264 | tf_op jit(solution)/shard_map/ppermute | solution.py:327
  37.5 13.8 %collective-permute-start.8 = (bf16[224,1024]{1,0:T(8,128)(2,1)S(1)}, bf16[224,1024]{1,0:T(8,128)(2,1)S(1)}, u32[]{:S(2)}, u32[]{:S(2)}) collective-permute-start(bf16[224,1024]{1,0:T(8,128)(2,1)S(1)} %collective-permute-done.1.refs_1_), channel_id=1, source_target_pairs={{0,1},{1,2},{2,3},{3,0},{4,5},{5,6},{6,7},{7,4},{8,9},{9,10},{10,1... | collective-permute-start | bytes 1376264 | tf_op jit(solution)/shard_map/ppermute | solution.py:327
  40.2 11.1 %collective-permute-start.11 = (bf16[224,1024]{1,0:T(8,128)(2,1)S(1)}, bf16[224,1024]{1,0:T(8,128)(2,1)S(1)}, u32[]{:S(2)}, u32[]{:S(2)}) collective-permute-start(bf16[224,1024]{1,0:T(8,128)(2,1)S(1)} %collective-permute-done.10.refs_1_), channel_id=1, source_target_pairs={{0,12},{1,13},{2,14},{3,15},{4,0},{5,1},{6,2},{7,3},{8,4},{9,5},{1... | collective-permute-start | bytes 1376264 | tf_op jit(solution)/shard_map/ppermute | solution.py:327
  42.3 9.0 %slice-start.1 = ((s8[4587520]{0:T(1024)(128)(4,1)}), s8[393216]{0:T(1024)(128)(4,1)S(1)}, s32[]{:S(2)}) async-start(s8[4587520]{0:T(1024)(128)(4,1)} %bitcast.6), calls=%async_computation.2 | async-start | bytes 786432
  42.3 9.0 %copy-start.2 = (bf16[1024,640]{1,0:T(8,128)(2,1)S(1)}, bf16[1024,640]{1,0:T(8,128)(2,1)}, u32[]{:S(2)}) copy-start(bf16[1024,640]{1,0:T(8,128)(2,1)} %refs_7_.1) | copy-start | bytes 3932164
  42.3 9.0 %copy-start.4 = (f32[640]{0:T(1024)S(1)}, f32[640]{0:T(1024)}, u32[]{:S(2)}) copy-start(f32[640]{0:T(1024)} %refs_8_.1) | copy-start | bytes 7684
  51.4 21.6 %copy-start.6 = (s32[256]{0:T(256)S(1)}, s32[256]{0:T(256)}, u32[]{:S(2)}) copy-start(s32[256]{0:T(256)} %seed_ref.3) | copy-start | bytes 3076
  58.5 27.4 %all-to-all-start = ((f32[256,1,128]{2,1,0:T(1,128)}), f32[256,1,128]{2,1,0:T(1,128)S(1)}, u32[]{:S(2)}, u32[]{:S(2)}) async-start(f32[256,1,128]{2,1,0:T(1,128)} %bitcast.2), calls=%async_computation | async-start | bytes 262144 | tf_op jit(solution)/shard_map/all_to_all | solution.py:345
  78.2 1.8 %copy-start.7 = (bf16[1472,1280]{1,0:T(8,128)(2,1)}, bf16[1472,1280]{1,0:T(8,128)(2,1)S(1)}, u32[]{:S(2)}) copy-start(bf16[1472,1280]{1,0:T(8,128)(2,1)S(1)} %factor_tables.1.table_hbm) | copy-start | bytes 11304964
  86.0 0.6 copy-start.8

commit v4 on v3

--- a/solution.py
+++ b/solution.py
@@ -19,8 +19,9 @@
     (((0, 0), "+x"), ((0, 0), "-y"), ((0, 0), "-x"), ((0, 0), "+y")),
     (((1, 0), "+x"), ((0, 3), "-y"), ((0, 3), "-x"), ((1, 0), "+y")),
     (((0, 3), "+x"), ((2, 0), "-y"), ((0, 1), "-x"), ((2, 0), "+y")),
-    (((0, 2), "+x"), ((0, 2), "-x"), ((2, 3), "-y")),
+    (((0, 2), "+x"), ((0, 2), "-x")),
 )
+HALVES = (((2, 3), "-y"), ((2, 1), "+y"))
 
 
 def moved(place, way):
@@ -37,11 +38,15 @@
     return lax.rem(me // 4 + 4 - place[1], 4) * 4 + lax.rem(lax.rem(me, 4) + 4 - place[0], 4)
 
 
-def levels_of(mixed):
+def bytes_of(mixed):
     mixed = jnp.bitwise_xor(mixed, jnp.right_shift(mixed, 15))
     mixed = mixed * 1664525 + 1013904223
     mixed = jnp.bitwise_xor(mixed, jnp.right_shift(mixed, 13))
-    level = jnp.bitwise_and(mixed, 255).astype(jnp.float32) * (2.0 / 256.0) - 255.0 / 256.0
+    return jnp.bitwise_and(mixed, 255)
+
+
+def levels_of(mixed):
+    level = bytes_of(mixed).astype(jnp.float32) * (2.0 / 256.0) - 255.0 / 256.0
     return level.astype(jnp.bfloat16)
 
 
@@ -86,10 +91,10 @@
         up_ref[part : part + 64, :] = nothing
 
 
-def factor_kernel(seed_ref, message_ref, table_ref, lane_ref):
+def factor_kernel(seed_ref, message_ref, left_ref, table_ref, lane_ref):
     pairs = seed_ref.shape[0]
     width = table_ref.shape[1] // 2
-    count = (table_ref.shape[0] - 4 * pairs) // 2
+    count = left_ref.shape[0] // 2
     first = lax.axis_index("mp") * width
     rows = 16
     cell = (iota((rows, width), 1) + first) * (4 * CELL_STEP)
@@ -113,8 +118,8 @@
         def _(i):
             at = pl.multiple_of(i * 32, 32)
             mixed = (iota((32, 128), 0) + (at + left_first)) * (4 * CELL_STEP) + lane_ref[0:1, :]
-            table_ref[pl.ds(4 * pairs + at, 32), columns] = levels_of(mixed + 11003)
-            table_ref[pl.ds(4 * pairs + count + at, 32), columns] = levels_of(mixed + 33023)
+            left_ref[pl.ds(at, 32), columns] = (bytes_of(mixed + 11003) - 128).astype(jnp.int8)
+            left_ref[pl.ds(pl.multiple_of(count + at, 32), 32), columns] = (bytes_of(mixed + 33023) - 128).astype(jnp.int8)
 
 
 def contract(a, b):
@@ -146,37 +151,73 @@
             acc_ref[rows, :] = refs[n + 3][rows, :] + part
 
 
-def last_kernel(places, *refs):
-    n = len(places)
+def last_kernel(pieces, *refs):
+    n = len(pieces)
     blocks, weight_refs = refs[:n], refs[n : n + 3]
     acc_ref, target_ref, weight_ref, gate_out_ref, up_out_ref, message_ref = refs[n + 3 : n + 9]
-    total_refs, side_refs, parts_ref = refs[n + 9 : n + 11], refs[n + 11 : n + 13], refs[n + 13]
+    total_refs, side_refs, (parts_ref, turned_ref, low_ref) = refs[n + 9 : n + 11], refs[n + 11 : n + 13], refs[n + 13 :]
     depth = blocks[0].shape[0]
     width = target_ref.shape[1]
     tile = 256
     tiles = acc_ref.shape[0] // tile
     scale = SIGMA / math.sqrt(16 * depth)
+    features = [
+        pl.ds(pl.multiple_of(source_of(place) * depth + offset, 16), block.shape[0])
+        for (place, offset), block in zip(pieces, blocks)
+    ]
     lane_pair = lax.rem(iota((tile, 128), 1), 64) // 4
     row_pair = iota((tile, 128), 0) // ROWS
 
-    def product(i):
+    def weight_columns(low, high):
+        gate_ref, up_ref = weight_refs[:2]
+        cut = []
+        for at in features:
+            sides = []
+            if low < width:
+                sides.append(gate_ref[at, low : min(high, width)])
+            if high > width:
+                sides.append(up_ref[at, max(low, width) - width : high - width])
+            cut.append(sides[0] if len(sides) == 1 else jnp.concatenate(sides, axis=1))
+        return jnp.concatenate(cut, axis=0)
+
+    def products(i):
         rows = pl.ds(i * tile, tile)
-        part = product_of(places, blocks, rows, *weight_refs) + acc_ref[rows, :]
-        total_refs[i % 2][...] = part[:, : 2 * width]
-        low = jnp.where(lane_pair == row_pair + i * (tile // ROWS), part[:, 2 * width :] * scale, 0.0)
-        high = low.astype(jnp.bfloat16)
-        rest = (low - high.astype(jnp.float32)).astype(jnp.bfloat16)
-        low_both = jnp.concatenate([high, rest], axis=1)
-        side_refs[i % 2][:, :width] = jnp.dot(low_both, gate_out_ref[...], preferred_element_type=jnp.float32)
-        side_refs[i % 2][:, width:] = jnp.dot(low_both, up_out_ref[...], preferred_element_type=jnp.float32)
+        total_ref, side_ref = total_refs[i % 2], side_refs[i % 2]
+
+        def turn():
+            turned_ref[...] = jnp.concatenate([block[:, rows] for block in blocks], axis=0).T
+            table = jnp.concatenate([weight_refs[2][at, :] for at in features], axis=0)
+            low = jnp.dot(turned_ref[...], table, preferred_element_type=jnp.float32) + acc_ref[rows, 2 * width :]
+            low = jnp.where(lane_pair == row_pair + i * (tile // ROWS), low * scale, 0.0)
+            high = low.astype(jnp.bfloat16)
+            low_ref[:, :128] = high
+            low_ref[:, 128:] = (low - high.astype(jnp.float32)).astype(jnp.bfloat16)
+
+        def side(out_ref, first):
+            def step():
+                side_ref[:, first : first + width] = jnp.dot(low_ref[...], out_ref[...], preferred_element_type=jnp.float32)
+
+            return step
+
+        def total(low, high):
+            def step():
+                part = jnp.dot(turned_ref[...], weight_columns(low, high), preferred_element_type=jnp.float32)
+                total_ref[:, low:high] = part + acc_ref[rows, low:high]
+
+            return step
+
+        return [turn, side(gate_out_ref, 0), side(up_out_ref, width)] + [
+            total(low, low + 256) for low in range(0, 2 * width, 256)
+        ]
 
     def errors(i):
         total_ref, side_ref = total_refs[i % 2], side_refs[i % 2]
-        for p in range(tile // ROWS):
+
+        def of_pair(p, kept):
             k = i * (tile // ROWS) + p
-            plus = jnp.zeros((8, width), jnp.float32)
-            minus = jnp.zeros((8, width), jnp.float32)
-            for q in range(ROWS // 16):
+
+            def of_rows(q):
+                plus, minus = kept.get(p) or (jnp.zeros((8, width), jnp.float32), jnp.zeros((8, width), jnp.float32))
                 at = p * ROWS + q * 16
                 goals = target_ref[i * tile + at : i * tile + at + 16, :].astype(jnp.float32)
                 for h in range(2):
@@ -190,14 +231,25 @@
                     half = 0.5 * (gate - side_gate)
                     error = (half * jnp.tanh(half) + half) * (up - side_up) - goal
                     minus += error * error
-            parts_ref[0, k : k + 1, :] = jnp.sum(plus, axis=0, keepdims=True) * weight_ref[...][None, :]
-            parts_ref[1, k : k + 1, :] = jnp.sum(minus, axis=0, keepdims=True) * weight_ref[...][None, :]
-
-    product(0)
+                kept[p] = (plus, minus)
+                if q == ROWS // 16 - 1:
+                    parts_ref[0, k : k + 1, :] = jnp.sum(plus, axis=0, keepdims=True) * weight_ref[...][None, :]
+                    parts_ref[1, k : k + 1, :] = jnp.sum(minus, axis=0, keepdims=True) * weight_ref[...][None, :]
+
+            return [lambda q=q: of_rows(q) for q in range(ROWS // 16)]
+
+        kept = {}
+        return [step for p in range(tile // ROWS) for step in of_pair(p, kept)]
+
+    for step in products(0):
+        step()
     for i in range(tiles):
-        if i + 1 < tiles:
-            product(i + 1)
-        errors(i)
+        ahead = products(i + 1) if i + 1 < tiles else []
+        behind = errors(i)
+        for at, step in enumerate(behind):
+            for other in ahead[at * len(ahead) // len(behind) : (at + 1) * len(ahead) // len(behind)]:
+                other()
+            step()
 
     pairs = parts_ref.shape[1]
     lane = iota((pairs, 128), 1)
@@ -209,16 +261,8 @@
     message_ref[...] = jnp.broadcast_to(line, message_ref.shape)
 
 
-def update_kernel(message_ref, table_hbm, out_gate_ref, out_up_ref, fit_ref, f_ref, table_ref, sems):
+def update_kernel(message_ref, left_ref, table_ref, out_gate, out_up, fit_ref, f_ref, out_gate_ref, out_up_ref, sems):
     rows, width = out_gate_ref.shape
-    depth = table_ref.shape[0] - 2 * rows
-    parts = []
-    for k in range(2):
-        left, right = pl.ds(depth + k * rows, rows), (pl.ds(0, depth), pl.ds(k * width, width))
-        parts.append(pltpu.make_async_copy(table_hbm.at[left, :], table_ref.at[left, :], sems.at[2 * k]))
-        parts.append(pltpu.make_async_copy(table_hbm.at[right], table_ref.at[right], sems.at[2 * k + 1]))
-    for copy in parts:
-        copy.start()
     count = message_ref.shape[0]
     pick_row, pick = iota((16, count), 0), iota((16, count), 1)
     chosen = pick // 16 == 2 * lax.rem(pick_row, 8) + pick_row // 8
@@ -240,20 +284,22 @@
     fitness = (scores - center) / jnp.sqrt(jnp.full((16, 128), spread + EPSILON, jnp.float32))
     f_ref[...] = fitness
     factor = (fitness[:8] - fitness[8:]) * (0.5 / 16.0)
-    for k, out_ref in enumerate((out_gate_ref, out_up_ref)):
-        parts[2 * k].wait()
+    copies = []
+    for k, (out_ref, out) in enumerate(((out_gate_ref, out_gate), (out_up_ref, out_up))):
         highs, rests = [], []
         for q in range(8):
-            left = table_ref[depth + k * rows : depth + (k + 1) * rows, q * 128 : (q + 1) * 128]
-            scaled = left.astype(jnp.float32) * factor[q : q + 1, :]
+            left = left_ref[k * rows : (k + 1) * rows, q * 128 : (q + 1) * 128]
+            level = left.astype(jnp.int32).astype(jnp.float32) * (2.0 / 256.0) + 1.0 / 256.0
+            scaled = level * factor[q : q + 1, :]
             high = scaled.astype(jnp.bfloat16)
             highs.append(high)
             rests.append((scaled - high.astype(jnp.float32)).astype(jnp.bfloat16))
-        both = jnp.concatenate([jnp.concatenate(highs, axis=1), jnp.concatenate(rests, axis=1)], axis=0)
-        parts[2 * k + 1].wait()
-        right = table_ref[:depth, k * width : (k + 1) * width]
-        product = jnp.dot(both, right, preferred_element_type=jnp.float32)
-        out_ref[...] = product[:rows] + product[rows:]
+        right = table_ref[:, k * width : (k + 1) * width]
+        out_ref[...] = jnp.dot(
+            jnp.concatenate(highs, axis=1), right, preferred_element_type=jnp.float32
+        ) + jnp.dot(jnp.concatenate(rests, axis=1), right, preferred_element_type=jnp.float32)
+        copies.append(pltpu.make_async_copy(out_ref, out, sems.at[k]))
+        copies[-1].start()
     pop = lax.axis_index("pop")
     mine = pop // 2
     lane, member = iota((128, 128), 0), iota((128, 128), 1)
@@ -264,6 +310,8 @@
         select = (at & (lax.rem(member, 2) == s)).astype(jnp.float32)
         total += jnp.dot(line, select, precision=lax.Precision.HIGHEST, preferred_element_type=jnp.float32)[:1]
     fit_ref[...] = total[:, : fit_ref.shape[1]]
+    for copy in copies:
+        copy.wait()
 
 
 def params(mib):
@@ -331,45 +379,60 @@
         held += list(fresh)
         blocks.update(fresh)
 
+    half = depth // 2
+    last = [blocks[place] for place in held]
+    pieces = [(place, 0) for place in held]
+    for k, (place, way) in enumerate(HALVES):
+        last.append(lax.ppermute(blocks[place][k * half : (k + 1) * half], "mp", pairs_of(way)))
+        pieces.append((moved(place, way), k * half))
     message = pl.pallas_call(
-        lambda *refs: last_kernel(held, *refs),
+        lambda *refs: last_kernel(pieces, *refs),
         out_shape=jax.ShapeDtypeStruct((device_total, 128), f32),
-        in_specs=[in_vmem] * (len(held) + 8),
+        in_specs=[in_vmem] * (len(last) + 8),
         out_specs=in_vmem,
-        scratch_shapes=[pltpu.VMEM((256, 2 * width), f32)] * 4 + [pltpu.VMEM((2, pairs_dev, width), f32)],
+        scratch_shapes=[pltpu.VMEM((256, 2 * width), f32)] * 4
+        + [
+            pltpu.VMEM((2, pairs_dev, width), f32),
+            pltpu.VMEM((256, sum(block.shape[0] for block in last)), bf16),
+            pltpu.VMEM((256, 256), bf16),
+        ],
         compiler_params=params(16),
-        cost_estimate=cost(2 * rows_dev * len(held) * depth * columns, 12_000_000),
+        cost_estimate=cost(2 * rows_dev * 3 * depth * columns, 12_000_000),
         name="last_round",
-    )(*[blocks[place] for place in held], *weights, acc, target, unit_weight, gate_out, up_out)
+    )(*last, *weights, acc, target, unit_weight, gate_out, up_out)
 
     received = lax.all_to_all(message, ("pop", "mp"), 0, 0, tiled=True)
 
     left_rows = model_width // lax.axis_size("pop")
-    factors = pl.pallas_call(
+    left, right = pl.pallas_call(
         factor_kernel,
-        out_shape=jax.ShapeDtypeStruct((4 * pair_total + 2 * left_rows, 2 * width), bf16),
+        out_shape=[
+            jax.ShapeDtypeStruct((2 * left_rows, 4 * pair_total), jnp.int8),
+            jax.ShapeDtypeStruct((4 * pair_total, 2 * width), bf16),
+        ],
         in_specs=[in_smem, any_space],
-        out_specs=in_vmem,
+        out_specs=[in_vmem] * 2,
         scratch_shapes=[pltpu.VMEM((8, 128), jnp.int32)],
         compiler_params=params(8),
         cost_estimate=cost(3_000_000_000, 4_000_000),
         name="factor_tables",
     )(seeds, message)
+    update = jax.ShapeDtypeStruct((left_rows, width), f32)
     update_gate, update_up, fitness = pl.pallas_call(
         update_kernel,
-        out_shape=[jax.ShapeDtypeStruct((left_rows, width), f32)] * 2
-        + [jax.ShapeDtypeStruct((1, 2 * pairs_dev), f32)],
-        in_specs=[in_vmem, any_space],
-        out_specs=[in_vmem] * 3,
+        out_shape=[update, update, jax.ShapeDtypeStruct((1, 2 * pairs_dev), f32)],
+        in_specs=[in_vmem] * 3,
+        out_specs=[any_space, any_space, in_vmem],
         scratch_shapes=[
             pltpu.VMEM((16, 128), f32),
-            pltpu.VMEM(factors.shape, bf16),
-            pltpu.SemaphoreType.DMA((4,)),
+            pltpu.VMEM(update.shape, f32),
+            pltpu.VMEM(update.shape, f32),
+            pltpu.SemaphoreType.DMA((2,)),
         ],
-        compiler_params=params(58),
+        compiler_params=params(16),
         cost_estimate=cost(1_200_000_000, 5_000_000),
         name="update",
-    )(received, factors)
+    )(received, left, right)
     return (update_gate, update_up, fitness.reshape(2 * pairs_dev))
 
 

time: 92.7 us -> 92.7 us (level)
  waiting for transfers between devices: 14.6 us -> 18.7 us
  Pallas kernels: 35.6 us -> 32.8 us
  local copies, waits for them, and re-layouts: 5.45 us -> 3.04 us
  starting transfers between devices: 35.9 us -> 37.1 us
    pallas_call x3, Pallas kernels: 18.1 us -> 15.2 us  [the longest x1 6.5 us: on_device(): pl.pallas_call(lambda *refs: last_kernel(pieces, *refs), out_shape=jax.Sh...]
    ppermute x0 -> x2, starting transfers between devices: none -> 2.82 us  [on_device(): lax.ppermute(blocks[place][k * half:(k + 1) * half], 'mp', pairs_of(way))]
    unnamed x22 -> x18, local copies, waits for them, and re-layouts: 5.45 us -> 3 us
    ppermute x15 -> x14, waiting for transfers between devices: 8.58 us -> 10.8 us  [on_device(): fresh[moved(place, way)] = lax.ppermute(block, 'mp', pairs_of(way))]
    all_to_all x1, waiting for transfers between devices: 5.97 us -> 7.88 us  [on_device(): received = lax.all_to_all(message, ('pop', 'mp'), 0, 0, tiled=True)]
    ppermute x15 -> x14, starting transfers between devices: 21.5 us -> 19.6 us  [on_device(): fresh[moved(place, way)] = lax.ppermute(block, 'mp', pairs_of(way))]
  transfers between devices with their start and end apart: 16 -> 17, of which waited for: 7 -> 4; matrix products, arithmetic and copies ran while one was open for 0% -> 0% of each run, Pallas kernels for 25% -> 24%
where the time goes in v4:
time: 92.7 us; the launch traced here: 92.6 us
  starting transfers between devices  37.1 us (40%)
  Pallas kernels  32.8 us (35%)
  waiting for transfers between devices  18.7 us (20%)
  local copies, waits for them, and re-layouts  3.04 us (3%)
  between operations  0.99 us (1%)
    ppermute x14, starting transfers between devices, on_device(): fresh[moved(place, way)] = lax.ppermute(block, 'mp', pairs_of(way))  19.6 us
    pallas_call x3, Pallas kernels, multiply(): pl.pallas_call(lambda *refs: round_kernel(places, acc is None, *refs), ou...  14.8 us
    all_to_all x1, starting transfers between devices, on_device(): received = lax.all_to_all(message, ('pop', 'mp'), 0, 0, tiled=True)  14.6 us
    ppermute x14, waiting for transfers between devices, on_device(): fresh[moved(place, way)] = lax.ppermute(block, 'mp', pairs_of(way))  10.8 us
    all_to_all x1, waiting for transfers between devices, on_device(): received = lax.all_to_all(message, ('pop', 'mp'), 0, 0, tiled=True)  7.88 us
    pallas_call x1, Pallas kernels, on_device(): pl.pallas_call(lambda *refs: last_kernel(pieces, *refs), out_shape=jax.Sh...  6.5 us
    pallas_call x1, Pallas kernels, on_device(): pl.pallas_call(factor_kernel, out_shape=[jax.ShapeDtypeStruct((2 * left_r...  5.11 us
    pallas_call x1, Pallas kernels, on_device(): pl.pallas_call(update_kernel, out_shape=[update, update, jax.ShapeDtypeSt...  3.61 us
  transfers between devices with their start and end apart: 17, of which 4 were waited for; matrix products, arithmetic and copies ran while one was open for 0% of the time, Pallas kernels for 24%

profile of v4, /device:TPU:1, one launch (start us, length us, event | category | flops | bytes accessed | tf_op | source)
XLA Modules:
  0.0 92.6 jit_solution(15836735593052055782)
XLA Ops:
  0.6 0.0 copy-start.3
  0.6 0.0 copy-start
  0.6 2.1 %collective-permute-start.4 = (bf16[224,1024]{1,0:T(8,128)(2,1)}, bf16[224,1024]{1,0:T(8,128)(2,1)S(1)}, u32[]{:S(2)}, u32[]{:S(2)}) collective-permute-start(bf16[224,1024]{1,0:T(8,128)(2,1)} %bitcast.8), channel_id=1, source_target_pairs={{0,1},{1,2},{2,3},{3,0},{4,5},{5,6},{6,7},{7,4},{8,9},{9,10},{10,1... | collective-permute-start | bytes 1376264 | tf_op jit(solution)/shard_map/ppermute | solution.py:375
  2.8 2.7 %collective-permute-start = (bf16[224,1024]{1,0:T(8,128)(2,1)}, bf16[224,1024]{1,0:T(8,128)(2,1)S(1)}, u32[]{:S(2)}, u32[]{:S(2)}) collective-permute-start(bf16[224,1024]{1,0:T(8,128)(2,1)} %bitcast.9), channel_id=1, source_target_pairs={{0,12},{1,13},{2,14},{3,15},{4,0},{5,1},{6,2},{7,3},{8,4},{9,5},{1... | collective-permute-start | bytes 1376264 | tf_op jit(solution)/shard_map/ppermute | solution.py:375
  5.5 0.0 collective-permute-start.7
  5.5 1.5 %collective-permute-start.6 = (bf16[224,1024]{1,0:T(8,128)(2,1)}, bf16[224,1024]{1,0:T(8,128)(2,1)S(1)}, u32[]{:S(2)}, u32[]{:S(2)}) collective-permute-start(bf16[224,1024]{1,0:T(8,128)(2,1)} %bitcast.11), channel_id=1, source_target_pairs={{0,3},{1,0},{2,1},{3,2},{4,7},{5,4},{6,5},{7,6},{8,11},{9,8},{10,9... | collective-permute-start | bytes 1376264 | tf_op jit(solution)/shard_map/ppermute | solution.py:375
  7.0 0.0 copy-start.5
  7.0 0.7 copy-done.5
  7.7 2.8 %prepare.1 = (bf16[3584,128]{1,0:T(8,128)(2,1)S(1)}, bf16[256,640]{1,0:T(8,128)(2,1)S(1)}, bf16[256,640]{1,0:T(8,128)(2,1)S(1)}) custom-call(s32[256]{0:T(256)S(1)} %copy-done.5), custom_call_target="tpu_custom_call" | custom-call | flops 2000000000 | bytes 2000000 | tf_op jit(solution)/shard_map/prepare/pallas_call | solution.py:342
  10.5 1.7 %collective-permute-done.4.refs_1_ = bf16[224,1024]{1,0:T(8,128)(2,1)S(1)} collective-permute-done((bf16[224,1024]{1,0:T(8,128)(2,1)}, bf16[224,1024]{1,0:T(8,128)(2,1)S(1)}, u32[]{:S(2)}, u32[]{:S(2)}) %collective-permute-start.4) | collective-permute-done | bytes 458784 | tf_op jit(solution)/shard_map/ppermute | solution.py:375
  12.2 1.9 %collective-permute-start.5 = (bf16[224,1024]{1,0:T(8,128)(2,1)S(1)}, bf16[224,1024]{1,0:T(8,128)(2,1)S(1)}, u32[]{:S(2)}, u32[]{:S(2)}) collective-permute-start(bf16[224,1024]{1,0:T(8,128)(2,1)S(1)} %collective-permute-done.4.refs_1_), channel_id=1, source_target_pairs={{0,1},{1,2},{2,3},{3,0},{4,5},{5,6},{6,7},{7,4},{8,9},{9,10},{10,1... | collective-permute-start | bytes 1376264 | tf_op jit(solution)/shard_map/ppermute | solution.py:375
  14.1 0.6 collective-permute-done.refs_2_
  14.7 3.3 %collective-permute-start.1 = (bf16[224,1024]{1,0:T(8,128)(2,1)S(1)}, bf16[224,1024]{1,0:T(8,128)(2,1)S(1)}, u32[]{:S(2)}, u32[]{:S(2)}) collective-permute-start(bf16[224,1024]{1,0:T(8,128)(2,1)S(1)} %collective-permute-done.refs_2_), channel_id=1, source_target_pairs={{0,12},{1,13},{2,14},{3,15},{4,0},{5,1},{6,2},{7,3},{8,4},{9,5},{1... | collective-permute-start | bytes 1376264 | tf_op jit(solution)/shard_map/ppermute | solution.py:375
  18.0 1.8 %collective-permute-start.14 = (bf16[224,1024]{1,0:T(8,128)(2,1)S(1)}, bf16[224,1024]{1,0:T(8,128)(2,1)S(1)}, u32[]{:S(2)}, u32[]{:S(2)}) collective-permute-start(bf16[224,1024]{1,0:T(8,128)(2,1)S(1)} %collective-permute-done.refs_2_), channel_id=1, source_target_pairs={{0,3},{1,0},{2,1},{3,2},{4,7},{5,4},{6,5},{7,6},{8,11},{9,8},{10,9... | collective-permute-start | bytes 1376264 | tf_op jit(solution)/shard_map/ppermute | solution.py:375
  19.8 0.0 collective-permute-done.7.refs_4_
  19.8 0.0 collective-permute-start.15
  19.8 0.0 collective-permute-done.6.refs_3_
  19.8 0.0 copy-done.3
  19.8 0.0 copy-done
  19.8 0.0 copy-start.1
  19.8 2.3 %copy-done.1 = bf16[3584,640]{1,0:T(8,128)(2,1)S(1)} copy-done((bf16[3584,640]{1,0:T(8,128)(2,1)S(1)}, bf16[3584,640]{1,0:T(8,128)(2,1)}, u32[]{:S(2)}) %copy-start.1) | copy-done | bytes 4587544
  22.1 5.1 %round_of_5.1 = (f32[1024,1408]{1,0:T(8,128)S(1)}, f32[8,128]{1,0:T(8,128)}) custom-call(bf16[224,1024]{1,0:T(8,128)(2,1)S(1)} %bitcast.12, bf16[224,1024]{1,0:T(8,128)(2,1)S(1)} %collective-permute-done.4.refs_1_, bf16[224,1024]{1,0:T(8,128)(2,1)S(1)} %collective-permute-done.refs_2_, bf16[224,1024]{1,0:T(8,128)(2,1)S(1)} %collective-permute-done.6.refs_3_, ...), custom_call_target="tpu_custom_call" | custom-call | flops 3229614080 | bytes 4000000 | tf_op jit(solution)/shard_map/round_of_5/pallas_call | solution.py:355
  27.2 0.0 collective-permute-done.5.refs_0_
  27.2 0.1 collective-permute-start.10
  27.3 2.6 %collective-permute-start.8 = (bf16[224,1024]{1,0:T(8,128)(2,1)S(1)}, bf16[224,1024]{1,0:T(8,128)(2,1)S(1)}, u32[]{:S(2)}, u32[]{:S(2)}) collective-permute-start(bf16[224,1024]{1,0:T(8,128)(2,1)S(1)} %collective-permute-done.5.refs_0_), channel_id=1, source_target_pairs={{0,12},{1,13},{2,14},{3,15},{4,0},{5,1},{6,2},{7,3},{8,4},{9,5},{1... | collective-permute-start | bytes 1376264 | tf_op jit(solution)/shard_map/ppermute | solution.py:375
  29.9 0.0 collective-permute-done.1.refs_1_
  29.9 0.0 collective-permute-start.12
  29.9 0.0 collective-permute-done.14.refs_2_
  29.9 2.7 %collective-permute-start.13 = (bf16[224,1024]{1,0:T(8,128)(2,1)S(1)}, bf16[224,1024]{1,0:T(8,128)(2,1)S(1)}, u32[]{:S(2)}, u32[]{:S(2)}) collective-permute-start(bf16[224,1024]{1,0:T(8,128)(2,1)S(1)} %collective-permute-done.7.refs_4_), channel_id=1, source_target_pairs={{0,3},{1,0},{2,1},{3,2},{4,7},{5,4},{6,5},{7,6},{8,11},{9,8},{10,9... | collective-permute-start | bytes 1376264 | tf_op jit(solution)/shard_map/ppermute | solution.py:375
  32.6 0.0 collective-permute-done.15.refs_3_
  32.6 0.0 collective-permute-start.2
  32.6 8.4 %collective-permute-done.10.refs_3_ = bf16[224,1024]{1,0:T(8,128)(2,1)S(1)} collective-permute-done((bf16[224,1024]{1,0:T(8,128)(2,1)S(1)}, bf16[224,1024]{1,0:T(8,128)(2,1)S(1)}, u32[]{:S(2)}, u32[]{:S(2)}) %collective-permute-start.10) | collective-permute-done | bytes 458784 | tf_op jit(solution)/shard_map/ppermute | solution.py:375
  41.1 1.0 %collective-permute-start.3 = (bf16[224,1024]{1,0:T(8,128)(2,1)S(1)}, bf16[224,1024]{1,0:T(8,128)(2,1)S(1)}, u32[]{:S(2)}, u32[]{:S(2)}) collective-permute-start(bf16[224,1024]{1,0:T(8,128)(2,1)S(1)} %collective-permute-done.1.refs_1_), channel_id=1, source_target_pairs={{0,3},{1,0},{2,1},{3,2},{4,7},{5,4},{6,5},{7,6},{8,11},{9,8},{10,9... | collective-permute-start | bytes 1376264 | tf_op jit(solution)/shard_map/ppermute | solution.py:375
  42.0 4.8 %round_of_4.2 = (f32[1024,1408]{1,0:T(8,128)S(1)}, f32[8,128]{1,0:T(8,128)}) custom-call(bf16[224,1024]{1,0:T(8,128)(2,1)S(1)} %collective-permute-done.5.refs_0_, bf16[224,1024]{1,0:T(8,128)(2,1)S(1)} %collective-permute-done.1.refs_1_, bf16[224,1024]{1,0:T(8,128)(2,1)S(1)} %collective-permute-done.14.refs_2_, ...), custom_call_target="tpu_custom_call", output_to_operand_aliasing={{0}: (7, {})} | custom-call | flops 2583691264 | bytes 4000000 | tf_op jit(solution)/shard_map/round_of_4/pallas_call | solution.py:355
  46.8 0.0 slice-start
  46.8 0.0 collective-permute-done.8.refs_1_
  46.8 0.1 collective-permute-start.11
  47.0 0.0 collective-permute-done.12.refs_0_
  47.0 2.7 %collective-permute-start.9 = (bf16[112,1024]{1,0:T(8,128)(2,1)S(1)}, bf16[112,1024]{1,0:T(8,128)(2,1)S(1)}, u32[]{:S(2)}, u32[]{:S(2)}) collective-permute-start(bf16[112,1024]{1,0:T(8,128)(2,1)S(1)} %slice.8), channel_id=1, source_target_pairs={{0,12},{1,13},{2,14},{3,15},{4,0},{5,1},{6,2},{7,3},{8,4},{9,5},{1... | collective-permute-start | bytes 688136 | tf_op jit(solution)/shard_map/ppermute | solution.py:386
  49.7 0.0 collective-permute-done.13.refs_2_
  49.7 0.0 slice-start.1
  49.7 0.0 copy-start.2
  49.7 0.0 copy-start.4
  49.7 4.8 %round_of_4.3 = (f32[1024,1408]{1,0:T(8,128)S(1)}, f32[8,128]{1,0:T(8,128)}) custom-call(bf16[224,1024]{1,0:T(8,128)(2,1)S(1)} %collective-permute-done.12.refs_0_, bf16[224,1024]{1,0:T(8,128)(2,1)S(1)} %collective-permute-done.8.refs_1_, bf16[224,1024]{1,0:T(8,128)(2,1)S(1)} %collective-permute-done.13.refs_2_, ...), custom_call_target="tpu_custom_call", output_to_operand_aliasing={{0}: (7, {})} | custom-call | flops 2583691264 | bytes 4000000 | tf_op jit(solution)/shard_map/round_of_4/pallas_call | solution.py:355
  54.6 0.0 collective-permute-done.2.refs_0_
  54.6 0.0 collective-permute-done.3.refs_1_
  54.6 0.0 collective-permute-done.11.refs_3_
  54.6 0.0 collective-permute-done.9.refs_2_
  54.6 0.0 slice-done
  54.6 0.0 slice-done.1
  54.6 0.0 copy-done.2
  54.6 0.0 copy-done.4
  54.6 0.0 copy-start.6
  54.6 6.5 %last_round.1.message_ref = f32[256,128]{1,0:T(8,128)} custom-call(bf16[224,1024]{1,0:T(8,128)(2,1)S(1)} %collective-permute-done.2.refs_0_, bf16[224,1024]{1,0:T(8,128)(2,1)S(1)} %collective-permute-done.3.refs_1_, bf16[112,1024]{1,0:T(8,128)(2,1)S(1)} %collective-permute-done.9.refs_2_, bf16[112,1024]{1,0:T(8,128)(2,1)S(1)} %collective-permute-done.11.refs_3_, ...), custom_call_target="tpu_custom_call" | custom-call | flops 1937768448 | bytes 12000000 | tf_op jit(solution)/shard_map/last_round/pallas_call | solution.py:388
  61.1 14.6 %all-to-all-start = ((f32[256,1,128]{2,1,0:T(1,128)}), f32[256,1,128]{2,1,0:T(1,128)S(1)}, u32[]{:S(2)}, u32[]{:S(2)}) async-start(f32[256,1,128]{2,1,0:T(1,128)} %bitcast.2), calls=%async_computation | async-start | bytes 262144 | tf_op jit(solution)/shard_map/all_to_all | solution.py:404
  75.8 0.0 copy-done.6
  75.8 5.1 %factor_tables.1 = (s8[448,1024]{1,0:T(32,128)(4,1)S(1)}, bf16[1024,1280]{1,0:T(8,128)(2,1)S(1)}) custom-call(s32[256]{0:T(256)S(1)} %copy-done.6, f32[256,128]{1,0:T(8,128)} %last_round.1.message_ref), custom_call_target="tpu_custom_call" | custom-call | flops 3000000000 | bytes 4000000 | tf_op jit(solution)/shard_map/factor_tables/pallas_call | solution.py:407
  80.9 7.9 %all-to-all-done = f32[256,1,128]{2,1,0:T(1,128)S(1)} async-done(((f32[256,1,128]{2,1,0:T(1,128)}), f32[256,1,128]{2,1,0:T(1,128)S(1)}, u32[]{:S(2)}, u32[]{:S(2)}) %all-to-all-start) | async-done | bytes 131104 | tf_op jit(solution)/shard_map/all_to_all | solution.py:404
  88.8 3.6 %update.1 = (f32[224,640]{1,0:T(8,128)}, f32[224,640]{1,0:T(8,128)}, f32[1,32]{1,0:T(1,128)}) custom-call(f32[256,128]{1,0:T(8,128)S(1)} %bitcast.13, s8[448,1024]{1,0:T(32,128)(4,1)S(1)} %get-tuple-element.32.left_ref, bf16[1024,1280]{1,0:T(8,128)(2,1)S(1)} %get-tuple-element.33.table_ref), custom_call_target="tpu_custom_call" | custom-call | flops 1200000000 | bytes 5000000 | tf_op jit(solution)/shard_map/update/pallas_call | solution.py:421
  (3 shorter events, 0.0 us)
Async XLA Ops:
  0.6 19.2 %copy-start.3 = (bf16[1024,224]{0,1:T(8,128)(2,1)S(1)}, bf16[1024,224]{0,1:T(8,128)(2,1)}, u32[]{:S(2)}) copy-start(bf16[1024,224]{0,1:T(8,128)(2,1)} %param.6) | copy-start | bytes 1376260
  0.6 19.2 %copy-start = (bf16[3584,640]{1,0:T(8,128)(2,1)S(1)}, bf16[3584,640]{1,0:T(8,128)(2,1)}, u32[]{:S(2)}) copy-start(bf16[3584,640]{1,0:T(8,128)(2,1)} %refs_4_.5) | copy-start | bytes 13762564
  0.6 11.5 %collective-permute-start.4 = (bf16[224,1024]{1,0:T(8,128)(2,1)}, bf16[224,1024]{1,0:T(8,128)(2,1)S(1)}, u32[]{:S(2)}, u32[]{:S(2)}) collective-permute-start(bf16[224,1024]{1,0:T(8,128)(2,1)} %bitcast.8), channel_id=1, source_target_pairs={{0,1},{1,2},{2,3},{3,0},{4,5},{5,6},{6,7},{7,4},{8,9},{9,10},{10,1... | collective-permute-start | bytes 1376264 | tf_op jit(solution)/shard_map/ppermute | solution.py:375
  2.8 11.9 %collective-permute-start = (bf16[224,1024]{1,0:T(8,128)(2,1)}, bf16[224,1024]{1,0:T(8,128)(2,1)S(1)}, u32[]{:S(2)}, u32[]{:S(2)}) collective-permute-start(bf16[224,1024]{1,0:T(8,128)(2,1)} %bitcast.9), channel_id=1, source_target_pairs={{0,12},{1,13},{2,14},{3,15},{4,0},{5,1},{6,2},{7,3},{8,4},{9,5},{1... | collective-permute-start | bytes 1376264 | tf_op jit(solution)/shard_map/ppermute | solution.py:375
  5.5 14.3 %collective-permute-start.7 = (bf16[224,1024]{1,0:T(8,128)(2,1)}, bf16[224,1024]{1,0:T(8,128)(2,1)S(1)}, u32[]{:S(2)}, u32[]{:S(2)}) collective-permute-start(bf16[224,1024]{1,0:T(8,128)(2,1)} %bitcast.10), channel_id=1, source_target_pairs={{0,4},{1,5},{2,6},{3,7},{4,8},{5,9},{6,10},{7,11},{8,12},{9,13},{1... | collective-permute-start | bytes 1376264 | tf_op jit(solution)/shard_map/ppermute | solution.py:375
  5.5 14.3 %collective-permute-start.6 = (bf16[224,1024]{1,0:T(8,128)(2,1)}, bf16[224,1024]{1,0:T(8,128)(2,1)S(1)}, u32[]{:S(2)}, u32[]{:S(2)}) collective-permute-start(bf16[224,1024]{1,0:T(8,128)(2,1)} %bitcast.11), channel_id=1, source_target_pairs={{0,3},{1,0},{2,1},{3,2},{4,7},{5,4},{6,5},{7,6},{8,11},{9,8},{10,9... | collective-permute-start | bytes 1376264 | tf_op jit(solution)/shard_map/ppermute | solution.py:375
  7.0 0.7 copy-start.5
  12.2 15.1 %collective-permute-start.5 = (bf16[224,1024]{1,0:T(8,128)(2,1)S(1)}, bf16[224,1024]{1,0:T(8,128)(2,1)S(1)}, u32[]{:S(2)}, u32[]{:S(2)}) collective-permute-start(bf16[224,1024]{1,0:T(8,128)(2,1)S(1)} %collective-permute-done.4.refs_1_), channel_id=1, source_target_pairs={{0,1},{1,2},{2,3},{3,0},{4,5},{5,6},{6,7},{7,4},{8,9},{9,10},{10,1... | collective-permute-start | bytes 1376264 | tf_op jit(solution)/shard_map/ppermute | solution.py:375
  14.7 15.2 %collective-permute-start.1 = (bf16[224,1024]{1,0:T(8,128)(2,1)S(1)}, bf16[224,1024]{1,0:T(8,128)(2,1)S(1)}, u32[]{:S(2)}, u32[]{:S(2)}) collective-permute-start(bf16[224,1024]{1,0:T(8,128)(2,1)S(1)} %collective-permute-done.refs_2_), channel_id=1, source_target_pairs={{0,12},{1,13},{2,14},{3,15},{4,0},{5,1},{6,2},{7,3},{8,4},{9,5},{1... | collective-permute-start | bytes 1376264 | tf_op jit(solution)/shard_map/ppermute | solution.py:375
  18.0 11.9 %collective-permute-start.14 = (bf16[224,1024]{1,0:T(8,128)(2,1)S(1)}, bf16[224,1024]{1,0:T(8,128)(2,1)S(1)}, u32[]{:S(2)}, u32[]{:S(2)}) collective-permute-start(bf16[224,1024]{1,0:T(8,128)(2,1)S(1)} %collective-permute-done.refs_2_), channel_id=1, source_target_pairs={{0,3},{1,0},{2,1},{3,2},{4,7},{5,4},{6,5},{7,6},{8,11},{9,8},{10,9... | collective-permute-start | bytes 1376264 | tf_op jit(solution)/shard_map/ppermute | solution.py:375
  19.8 12.8 %collective-permute-start.15 = (bf16[224,1024]{1,0:T(8,128)(2,1)S(1)}, bf16[224,1024]{1,0:T(8,128)(2,1)S(1)}, u32[]{:S(2)}, u32[]{:S(2)}) collective-permute-start(bf16[224,1024]{1,0:T(8,128)(2,1)S(1)} %collective-permute-done.4.refs_1_), channel_id=1, source_target_pairs={{0,4},{1,5},{2,6},{3,7},{4,8},{5,9},{6,10},{7,11},{8,12},{9,13},{1... | collective-permute-start | bytes 1376264 | tf_op jit(solution)/shard_map/ppermute | solution.py:375
  19.8 2.3 %copy-start.1 = (bf16[3584,640]{1,0:T(8,128)(2,1)S(1)}, bf16[3584,640]{1,0:T(8,128)(2,1)}, u32[]{:S(2)}) copy-start(bf16[3584,640]{1,0:T(8,128)(2,1)} %refs_5_.7) | copy-start | bytes 13762564
  27.2 13.8 %collective-permute-start.10 = (bf16[224,1024]{1,0:T(8,128)(2,1)S(1)}, bf16[224,1024]{1,0:T(8,128)(2,1)S(1)}, u32[]{:S(2)}, u32[]{:S(2)}) collective-permute-start(bf16[224,1024]{1,0:T(8,128)(2,1)S(1)} %collective-permute-done.5.refs_0_), channel_id=1, source_target_pairs={{0,4},{1,5},{2,6},{3,7},{4,8},{5,9},{6,10},{7,11},{8,12},{9,13},{1... | collective-permute-start | bytes 1376264 | tf_op jit(solution)/shard_map/ppermute | solution.py:375
  27.3 19.5 %collective-permute-start.8 = (bf16[224,1024]{1,0:T(8,128)(2,1)S(1)}, bf16[224,1024]{1,0:T(8,128)(2,1)S(1)}, u32[]{:S(2)}, u32[]{:S(2)}) collective-permute-start(bf16[224,1024]{1,0:T(8,128)(2,1)S(1)} %collective-permute-done.5.refs_0_), channel_id=1, source_target_pairs={{0,12},{1,13},{2,14},{3,15},{4,0},{5,1},{6,2},{7,3},{8,4},{9,5},{1... | collective-permute-start | bytes 1376264 | tf_op jit(solution)/shard_map/ppermute | solution.py:375
  29.9 17.0 %collective-permute-start.12 = (bf16[224,1024]{1,0:T(8,128)(2,1)S(1)}, bf16[224,1024]{1,0:T(8,128)(2,1)S(1)}, u32[]{:S(2)}, u32[]{:S(2)}) collective-permute-start(bf16[224,1024]{1,0:T(8,128)(2,1)S(1)} %collective-permute-done.refs_2_), channel_id=1, source_target_pairs={{0,1},{1,2},{2,3},{3,0},{4,5},{5,6},{6,7},{7,4},{8,9},{9,10},{10,1... | collective-permute-start | bytes 1376264 | tf_op jit(solution)/shard_map/ppermute | solution.py:375
  29.9 19.8 %collective-permute-start.13 = (bf16[224,1024]{1,0:T(8,128)(2,1)S(1)}, bf16[224,1024]{1,0:T(8,128)(2,1)S(1)}, u32[]{:S(2)}, u32[]{:S(2)}) collective-permute-start(bf16[224,1024]{1,0:T(8,128)(2,1)S(1)} %collective-permute-done.7.refs_4_), channel_id=1, source_target_pairs={{0,3},{1,0},{2,1},{3,2},{4,7},{5,4},{6,5},{7,6},{8,11},{9,8},{10,9... | collective-permute-start | bytes 1376264 | tf_op jit(solution)/shard_map/ppermute | solution.py:375
  32.6 22.0 %collective-permute-start.2 = (bf16[224,1024]{1,0:T(8,128)(2,1)S(1)}, bf16[224,1024]{1,0:T(8,128)(2,1)S(1)}, u32[]{:S(2)}, u32[]{:S(2)}) collective-permute-start(bf16[224,1024]{1,0:T(8,128)(2,1)S(1)} %collective-permute-done.1.refs_1_), channel_id=1, source_target_pairs={{0,1},{1,2},{2,3},{3,0},{4,5},{5,6},{6,7},{7,4},{8,9},{9,10},{10,1... | collective-permute-start | bytes 1376264 | tf_op jit(solution)/shard_map/ppermute | solution.py:375
  41.1 13.5 %collective-permute-start.3 = (bf16[224,1024]{1,0:T(8,128)(2,1)S(1)}, bf16[224,1024]{1,0:T(8,128)(2,1)S(1)}, u32[]{:S(2)}, u32[]{:S(2)}) collective-permute-start(bf16[224,1024]{1,0:T(8,128)(2,1)S(1)} %collective-permute-done.1.refs_1_), channel_id=1, source_target_pairs={{0,3},{1,0},{2,1},{3,2},{4,7},{5,4},{6,5},{7,6},{8,11},{9,8},{10,9... | collective-permute-start | bytes 1376264 | tf_op jit(solution)/shard_map/ppermute | solution.py:375
  46.8 7.8 %slice-start = ((s8[4587520]{0:T(1024)(128)(4,1)}), s8[4194304]{0:T(1024)(128)(4,1)S(1)}, s32[]{:S(2)}) async-start(s8[4587520]{0:T(1024)(128)(4,1)} %bitcast.6), calls=%async_computation.1 | async-start | bytes 8388608
  46.8 7.7 %collective-permute-start.11 = (bf16[112,1024]{1,0:T(8,128)(2,1)S(1)}, bf16[112,1024]{1,0:T(8,128)(2,1)S(1)}, u32[]{:S(2)}, u32[]{:S(2)}) collective-permute-start(bf16[112,1024]{1,0:T(8,128)(2,1)S(1)} %slice.9), channel_id=1, source_target_pairs={{0,4},{1,5},{2,6},{3,7},{4,8},{5,9},{6,10},{7,11},{8,12},{9,13},{1... | collective-permute-start | bytes 688136 | tf_op jit(solution)/shard_map/ppermute | solution.py:386
  47.0 7.6 %collective-permute-start.9 = (bf16[112,1024]{1,0:T(8,128)(2,1)S(1)}, bf16[112,1024]{1,0:T(8,128)(2,1)S(1)}, u32[]{:S(2)}, u32[]{:S(2)}) collective-permute-start(bf16[112,1024]{1,0:T(8,128)(2,1)S(1)} %slice.8), channel_id=1, source_target_pairs={{0,12},{1,13},{2,14},{3,15},{4,0},{5,1},{6,2},{7,3},{8,4},{9,5},{1... | collective-permute-start | bytes 688136 | tf_op jit(solution)/shard_map/ppermute | solution.py:386
  49.7 4.9 %slice-start.1 = ((s8[4587520]{0:T(1024)(128)(4,1)}), s8[393216]{0:T(1024)(128)(4,1)S(1)}, s32[]{:S(2)}) async-start(s8[4587520]{0:T(1024)(128)(4,1)} %bitcast.6), calls=%async_computation.2 | async-start | bytes 786432
  49.7 4.9 %copy-start.2 = (bf16[1024,640]{1,0:T(8,128)(2,1)S(1)}, bf16[1024,640]{1,0:T(8,128)(2,1)}, u32[]{:S(2)}) copy-start(bf16[1024,640]{1,0:T(8,128)(2,1)} %refs_8_.1) | copy-start | bytes 3932164
  49.7 4.9 %copy-start.4 = (f32[640]{0:T(1024)S(1)}, f32[640]{0:T(1024)}, u32[]{:S(2)}) copy-start(f32[640]{0:T(1024)} %refs_9_.1) | copy-start | bytes 7684
  54.6 21.1 %copy-start.6 = (s32[256]{0:T(256)S(1)}, s32[256]{0:T(256)}, u32[]{:S(2)}) copy-start(s32[256]{0:T(256)} %seed_ref.3) | copy-start | bytes 3076
  61.1 27.6 %all-to-all-start = ((f32[256,1,128]{2,1,0:T(1,128)}), f32[256,1,128]{2,1,0:T(1,128)S(1)}, u32[]{:S(2)}, u32[]{:S(2)}) async-start(f32[256,1,128]{2,1,0:T(1,128)} %bitcast.2), calls=%async_computation | async-start | bytes 262144 | tf_op jit(solution)/shard_map/all_to_all | solution.py:404

commit v5 on v4

--- a/solution.py
+++ b/solution.py
@@ -19,9 +19,8 @@
     (((0, 0), "+x"), ((0, 0), "-y"), ((0, 0), "-x"), ((0, 0), "+y")),
     (((1, 0), "+x"), ((0, 3), "-y"), ((0, 3), "-x"), ((1, 0), "+y")),
     (((0, 3), "+x"), ((2, 0), "-y"), ((0, 1), "-x"), ((2, 0), "+y")),
-    (((0, 2), "+x"), ((0, 2), "-x")),
+    (((0, 2), "+x"), ((0, 2), "-x"), ((2, 3), "-y")),
 )
-HALVES = (((2, 3), "-y"), ((2, 1), "+y"))
 
 
 def moved(place, way):
@@ -140,10 +139,11 @@
     n = len(places)
     acc_ref, mark_ref = refs[-2:]
     mark_ref[...] = jnp.zeros_like(mark_ref)
-
-    @pl.loop(0, acc_ref.shape[0] // 256)
+    tile = 512
+
+    @pl.loop(0, acc_ref.shape[0] // tile)
     def _(i):
-        rows = pl.ds(pl.multiple_of(i * 256, 256), 256)
+        rows = pl.ds(pl.multiple_of(i * tile, tile), tile)
         part = product_of(places, refs[:n], rows, *refs[n : n + 3])
         if fresh:
             acc_ref[rows, :] = part
@@ -379,12 +379,8 @@
         held += list(fresh)
         blocks.update(fresh)
 
-    half = depth // 2
     last = [blocks[place] for place in held]
     pieces = [(place, 0) for place in held]
-    for k, (place, way) in enumerate(HALVES):
-        last.append(lax.ppermute(blocks[place][k * half : (k + 1) * half], "mp", pairs_of(way)))
-        pieces.append((moved(place, way), k * half))
     message = pl.pallas_call(
         lambda *refs: last_kernel(pieces, *refs),
         out_shape=jax.ShapeDtypeStruct((device_total, 128), f32),

time: 92.7 us -> 89.1 us (0.961)
  Pallas kernels: 32.8 us -> 31 us
  starting transfers between devices: 37.1 us -> 35.6 us
    ppermute x2 -> x0, starting transfers between devices: 2.82 us -> none  [on_device(): lax.ppermute(blocks[place][k * half:(k + 1) * half], 'mp', pairs_of(way))]
    pallas_call x3, Pallas kernels: 14.8 us -> 12.9 us  [multiply(): pl.pallas_call(lambda *refs: round_kernel(places, acc is None, *refs), ou...]
    ppermute x14 -> x15, starting transfers between devices: 19.6 us -> 20.7 us  [on_device(): fresh[moved(place, way)] = lax.ppermute(block, 'mp', pairs_of(way))]
    ppermute x14 -> x15, waiting for transfers between devices: 10.8 us -> 10.5 us  [on_device(): fresh[moved(place, way)] = lax.ppermute(block, 'mp', pairs_of(way))]
  transfers between devices with their start and end apart: 17 -> 16, of which waited for: 4 -> 8; matrix products, arithmetic and copies ran while one was open for 0% -> 0% of each run, Pallas kernels for 24% -> 23%
where the time goes in v5:
time: 89.1 us; the launch traced here: 89 us
  starting transfers between devices  35.6 us (40%)
  Pallas kernels  31 us (35%)
  waiting for transfers between devices  18.4 us (21%)
  local copies, waits for them, and re-layouts  3.01 us (3%)
  between operations  0.95 us (1%)
    ppermute x15, starting transfers between devices, on_device(): fresh[moved(place, way)] = lax.ppermute(block, 'mp', pairs_of(way))  20.7 us
    all_to_all x1, starting transfers between devices, on_device(): received = lax.all_to_all(message, ('pop', 'mp'), 0, 0, tiled=True)  14.9 us
    pallas_call x3, Pallas kernels, multiply(): pl.pallas_call(lambda *refs: round_kernel(places, acc is None, *refs), ou...  12.9 us
    ppermute x15, waiting for transfers between devices, on_device(): fresh[moved(place, way)] = lax.ppermute(block, 'mp', pairs_of(way))  10.5 us
    all_to_all x1, waiting for transfers between devices, on_device(): received = lax.all_to_all(message, ('pop', 'mp'), 0, 0, tiled=True)  7.88 us
    pallas_call x1, Pallas kernels, on_device(): pl.pallas_call(lambda *refs: last_kernel(pieces, *refs), out_shape=jax.Sh...  6.52 us
    pallas_call x1, Pallas kernels, on_device(): pl.pallas_call(factor_kernel, out_shape=[jax.ShapeDtypeStruct((2 * left_r...  5.11 us
    pallas_call x1, Pallas kernels, on_device(): pl.pallas_call(update_kernel, out_shape=[update, update, jax.ShapeDtypeSt...  3.61 us
  transfers between devices with their start and end apart: 16, of which 8 were waited for; matrix products, arithmetic and copies ran while one was open for 0% of the time, Pallas kernels for 23%

profile of v5, /device:TPU:1, one launch (start us, length us, event | category | flops | bytes accessed | tf_op | source)
XLA Modules:
  0.0 89.0 jit_solution(11620163163496568189)
XLA Ops:
  0.6 0.0 copy-start.3
  0.6 0.0 copy-start
  0.6 2.1 %collective-permute-start.2 = (bf16[224,1024]{1,0:T(8,128)(2,1)}, bf16[224,1024]{1,0:T(8,128)(2,1)S(1)}, u32[]{:S(2)}, u32[]{:S(2)}) collective-permute-start(bf16[224,1024]{1,0:T(8,128)(2,1)} %bitcast.8), channel_id=1, source_target_pairs={{0,1},{1,2},{2,3},{3,0},{4,5},{5,6},{6,7},{7,4},{8,9},{9,10},{10,1... | collective-permute-start | bytes 1376264 | tf_op jit(solution)/shard_map/ppermute | solution.py:375
  2.8 2.7 %collective-permute-start = (bf16[224,1024]{1,0:T(8,128)(2,1)}, bf16[224,1024]{1,0:T(8,128)(2,1)S(1)}, u32[]{:S(2)}, u32[]{:S(2)}) collective-permute-start(bf16[224,1024]{1,0:T(8,128)(2,1)} %bitcast.9), channel_id=1, source_target_pairs={{0,12},{1,13},{2,14},{3,15},{4,0},{5,1},{6,2},{7,3},{8,4},{9,5},{1... | collective-permute-start | bytes 1376264 | tf_op jit(solution)/shard_map/ppermute | solution.py:375
  5.5 0.0 collective-permute-start.7
  5.5 1.5 %collective-permute-start.6 = (bf16[224,1024]{1,0:T(8,128)(2,1)}, bf16[224,1024]{1,0:T(8,128)(2,1)S(1)}, u32[]{:S(2)}, u32[]{:S(2)}) collective-permute-start(bf16[224,1024]{1,0:T(8,128)(2,1)} %bitcast.11), channel_id=1, source_target_pairs={{0,3},{1,0},{2,1},{3,2},{4,7},{5,4},{6,5},{7,6},{8,11},{9,8},{10,9... | collective-permute-start | bytes 1376264 | tf_op jit(solution)/shard_map/ppermute | solution.py:375
  7.0 0.0 copy-start.5
  7.0 0.7 copy-done.5
  7.7 2.8 %prepare.1 = (bf16[3584,128]{1,0:T(8,128)(2,1)S(1)}, bf16[256,640]{1,0:T(8,128)(2,1)S(1)}, bf16[256,640]{1,0:T(8,128)(2,1)S(1)}) custom-call(s32[256]{0:T(256)S(1)} %copy-done.5), custom_call_target="tpu_custom_call" | custom-call | flops 2000000000 | bytes 2000000 | tf_op jit(solution)/shard_map/prepare/pallas_call | solution.py:342
  10.5 1.7 %collective-permute-done.2.refs_1_ = bf16[224,1024]{1,0:T(8,128)(2,1)S(1)} collective-permute-done((bf16[224,1024]{1,0:T(8,128)(2,1)}, bf16[224,1024]{1,0:T(8,128)(2,1)S(1)}, u32[]{:S(2)}, u32[]{:S(2)}) %collective-permute-start.2) | collective-permute-done | bytes 458784 | tf_op jit(solution)/shard_map/ppermute | solution.py:375
  12.2 1.9 %collective-permute-start.3 = (bf16[224,1024]{1,0:T(8,128)(2,1)S(1)}, bf16[224,1024]{1,0:T(8,128)(2,1)S(1)}, u32[]{:S(2)}, u32[]{:S(2)}) collective-permute-start(bf16[224,1024]{1,0:T(8,128)(2,1)S(1)} %collective-permute-done.2.refs_1_), channel_id=1, source_target_pairs={{0,1},{1,2},{2,3},{3,0},{4,5},{5,6},{6,7},{7,4},{8,9},{9,10},{10,1... | collective-permute-start | bytes 1376264 | tf_op jit(solution)/shard_map/ppermute | solution.py:375
  14.1 0.6 collective-permute-done.refs_2_
  14.7 1.5 %collective-permute-start.4 = (bf16[224,1024]{1,0:T(8,128)(2,1)S(1)}, bf16[224,1024]{1,0:T(8,128)(2,1)S(1)}, u32[]{:S(2)}, u32[]{:S(2)}) collective-permute-start(bf16[224,1024]{1,0:T(8,128)(2,1)S(1)} %collective-permute-done.refs_2_), channel_id=1, source_target_pairs={{0,3},{1,0},{2,1},{3,2},{4,7},{5,4},{6,5},{7,6},{8,11},{9,8},{10,9... | collective-permute-start | bytes 1376264 | tf_op jit(solution)/shard_map/ppermute | solution.py:375
  16.2 3.6 %collective-permute-start.1 = (bf16[224,1024]{1,0:T(8,128)(2,1)S(1)}, bf16[224,1024]{1,0:T(8,128)(2,1)S(1)}, u32[]{:S(2)}, u32[]{:S(2)}) collective-permute-start(bf16[224,1024]{1,0:T(8,128)(2,1)S(1)} %collective-permute-done.refs_2_), channel_id=1, source_target_pairs={{0,12},{1,13},{2,14},{3,15},{4,0},{5,1},{6,2},{7,3},{8,4},{9,5},{1... | collective-permute-start | bytes 1376264 | tf_op jit(solution)/shard_map/ppermute | solution.py:375
  19.8 0.0 collective-permute-done.7.refs_4_
  19.8 0.0 collective-permute-start.5
  19.8 0.0 collective-permute-done.6.refs_3_
  19.8 0.0 copy-done.3
  19.8 0.0 copy-done
  19.8 0.0 copy-start.1
  19.8 2.3 %copy-done.1 = bf16[3584,640]{1,0:T(8,128)(2,1)S(1)} copy-done((bf16[3584,640]{1,0:T(8,128)(2,1)S(1)}, bf16[3584,640]{1,0:T(8,128)(2,1)}, u32[]{:S(2)}) %copy-start.1) | copy-done | bytes 4587544
  22.1 4.7 %round_of_5.1 = (f32[1024,1408]{1,0:T(8,128)S(1)}, f32[8,128]{1,0:T(8,128)}) custom-call(bf16[224,1024]{1,0:T(8,128)(2,1)S(1)} %bitcast.12, bf16[224,1024]{1,0:T(8,128)(2,1)S(1)} %collective-permute-done.2.refs_1_, bf16[224,1024]{1,0:T(8,128)(2,1)S(1)} %collective-permute-done.refs_2_, bf16[224,1024]{1,0:T(8,128)(2,1)S(1)} %collective-permute-done.6.refs_3_, ...), custom_call_target="tpu_custom_call" | custom-call | flops 3229614080 | bytes 4000000 | tf_op jit(solution)/shard_map/round_of_5/pallas_call | solution.py:355
  26.8 0.0 collective-permute-done.3.refs_0_
  26.8 2.7 %collective-permute-start.10 = (bf16[224,1024]{1,0:T(8,128)(2,1)S(1)}, bf16[224,1024]{1,0:T(8,128)(2,1)S(1)}, u32[]{:S(2)}, u32[]{:S(2)}) collective-permute-start(bf16[224,1024]{1,0:T(8,128)(2,1)S(1)} %collective-permute-done.3.refs_0_), channel_id=1, source_target_pairs={{0,12},{1,13},{2,14},{3,15},{4,0},{5,1},{6,2},{7,3},{8,4},{9,5},{1... | collective-permute-start | bytes 1376264 | tf_op jit(solution)/shard_map/ppermute | solution.py:375
  29.5 0.0 collective-permute-start.12
  29.5 0.0 collective-permute-done.4.refs_2_
  29.5 2.7 %collective-permute-start.13 = (bf16[224,1024]{1,0:T(8,128)(2,1)S(1)}, bf16[224,1024]{1,0:T(8,128)(2,1)S(1)}, u32[]{:S(2)}, u32[]{:S(2)}) collective-permute-start(bf16[224,1024]{1,0:T(8,128)(2,1)S(1)} %collective-permute-done.7.refs_4_), channel_id=1, source_target_pairs={{0,3},{1,0},{2,1},{3,2},{4,7},{5,4},{6,5},{7,6},{8,11},{9,8},{10,9... | collective-permute-start | bytes 1376264 | tf_op jit(solution)/shard_map/ppermute | solution.py:375
  32.2 0.0 collective-permute-done.1.refs_1_
  32.2 0.0 collective-permute-start.14
  32.2 0.0 collective-permute-done.5.refs_3_
  32.2 0.0 slice-start
  32.2 4.1 %round_of_4.2 = (f32[1024,1408]{1,0:T(8,128)S(1)}, f32[8,128]{1,0:T(8,128)}) custom-call(bf16[224,1024]{1,0:T(8,128)(2,1)S(1)} %collective-permute-done.3.refs_0_, bf16[224,1024]{1,0:T(8,128)(2,1)S(1)} %collective-permute-done.1.refs_1_, bf16[224,1024]{1,0:T(8,128)(2,1)S(1)} %collective-permute-done.4.refs_2_, ...), custom_call_target="tpu_custom_call", output_to_operand_aliasing={{0}: (7, {})} | custom-call | flops 2583691264 | bytes 4000000 | tf_op jit(solution)/shard_map/round_of_4/pallas_call | solution.py:355
  36.3 0.4 collective-permute-start.9
  36.7 0.2 collective-permute-done.10.refs_1_
  36.9 1.0 %collective-permute-start.8 = (bf16[224,1024]{1,0:T(8,128)(2,1)S(1)}, bf16[224,1024]{1,0:T(8,128)(2,1)S(1)}, u32[]{:S(2)}, u32[]{:S(2)}) collective-permute-start(bf16[224,1024]{1,0:T(8,128)(2,1)S(1)} %collective-permute-done.1.refs_1_), channel_id=1, source_target_pairs={{0,1},{1,2},{2,3},{3,0},{4,5},{5,6},{6,7},{7,4},{8,9},{9,10},{10,1... | collective-permute-start | bytes 1376264 | tf_op jit(solution)/shard_map/ppermute | solution.py:375
  37.9 1.9 %collective-permute-done.12.refs_0_ = bf16[224,1024]{1,0:T(8,128)(2,1)S(1)} collective-permute-done((bf16[224,1024]{1,0:T(8,128)(2,1)S(1)}, bf16[224,1024]{1,0:T(8,128)(2,1)S(1)}, u32[]{:S(2)}, u32[]{:S(2)}) %collective-permute-start.12) | collective-permute-done | bytes 458784 | tf_op jit(solution)/shard_map/ppermute | solution.py:375
  39.8 0.8 collective-permute-start.11
  40.5 0.0 collective-permute-done.13.refs_2_
  40.5 1.4 %collective-permute-done.14.refs_3_ = bf16[224,1024]{1,0:T(8,128)(2,1)S(1)} collective-permute-done((bf16[224,1024]{1,0:T(8,128)(2,1)S(1)}, bf16[224,1024]{1,0:T(8,128)(2,1)S(1)}, u32[]{:S(2)}, u32[]{:S(2)}) %collective-permute-start.14) | collective-permute-done | bytes 458784 | tf_op jit(solution)/shard_map/ppermute | solution.py:375
  41.9 0.0 slice-start.1
  41.9 0.0 copy-start.2
  41.9 0.0 copy-start.4
  41.9 4.1 %round_of_4.3 = (f32[1024,1408]{1,0:T(8,128)S(1)}, f32[8,128]{1,0:T(8,128)}) custom-call(bf16[224,1024]{1,0:T(8,128)(2,1)S(1)} %collective-permute-done.12.refs_0_, bf16[224,1024]{1,0:T(8,128)(2,1)S(1)} %collective-permute-done.10.refs_1_, bf16[224,1024]{1,0:T(8,128)(2,1)S(1)} %collective-permute-done.13.refs_2_, ...), custom_call_target="tpu_custom_call", output_to_operand_aliasing={{0}: (7, {})} | custom-call | flops 2583691264 | bytes 4000000 | tf_op jit(solution)/shard_map/round_of_4/pallas_call | solution.py:355
  46.0 3.0 %collective-permute-done.9.refs_1_ = bf16[224,1024]{1,0:T(8,128)(2,1)S(1)} collective-permute-done((bf16[224,1024]{1,0:T(8,128)(2,1)S(1)}, bf16[224,1024]{1,0:T(8,128)(2,1)S(1)}, u32[]{:S(2)}, u32[]{:S(2)}) %collective-permute-start.9) | collective-permute-done | bytes 458784 | tf_op jit(solution)/shard_map/ppermute | solution.py:375
  49.0 1.7 %collective-permute-done.8.refs_0_ = bf16[224,1024]{1,0:T(8,128)(2,1)S(1)} collective-permute-done((bf16[224,1024]{1,0:T(8,128)(2,1)S(1)}, bf16[224,1024]{1,0:T(8,128)(2,1)S(1)}, u32[]{:S(2)}, u32[]{:S(2)}) %collective-permute-start.8) | collective-permute-done | bytes 458784 | tf_op jit(solution)/shard_map/ppermute | solution.py:375
  50.7 0.0 collective-permute-done.11.refs_2_
  50.7 0.0 slice-done
  50.7 0.0 slice-done.1
  50.7 0.0 copy-done.2
  50.7 0.0 copy-done.4
  50.7 0.0 copy-start.6
  50.7 6.5 %last_round.1.message_ref = f32[256,128]{1,0:T(8,128)} custom-call(bf16[224,1024]{1,0:T(8,128)(2,1)S(1)} %collective-permute-done.8.refs_0_, bf16[224,1024]{1,0:T(8,128)(2,1)S(1)} %collective-permute-done.9.refs_1_, bf16[224,1024]{1,0:T(8,128)(2,1)S(1)} %collective-permute-done.11.refs_2_, bf16[3584,640]{1,0:T(8,128)(2,1)S(1)} %copy-done, ...), custom_call_target="tpu_custom_call" | custom-call | flops 1937768448 | bytes 12000000 | tf_op jit(solution)/shard_map/last_round/pallas_call | solution.py:384
  57.3 14.9 %all-to-all-start = ((f32[256,1,128]{2,1,0:T(1,128)}), f32[256,1,128]{2,1,0:T(1,128)S(1)}, u32[]{:S(2)}, u32[]{:S(2)}) async-start(f32[256,1,128]{2,1,0:T(1,128)} %bitcast.2), calls=%async_computation | async-start | bytes 262144 | tf_op jit(solution)/shard_map/all_to_all | solution.py:400
  72.2 0.0 copy-done.6
  72.2 5.1 %factor_tables.1 = (s8[448,1024]{1,0:T(32,128)(4,1)S(1)}, bf16[1024,1280]{1,0:T(8,128)(2,1)S(1)}) custom-call(s32[256]{0:T(256)S(1)} %copy-done.6, f32[256,128]{1,0:T(8,128)} %last_round.1.message_ref), custom_call_target="tpu_custom_call" | custom-call | flops 3000000000 | bytes 4000000 | tf_op jit(solution)/shard_map/factor_tables/pallas_call | solution.py:403
  77.3 7.9 %all-to-all-done = f32[256,1,128]{2,1,0:T(1,128)S(1)} async-done(((f32[256,1,128]{2,1,0:T(1,128)}), f32[256,1,128]{2,1,0:T(1,128)S(1)}, u32[]{:S(2)}, u32[]{:S(2)}) %all-to-all-start) | async-done | bytes 131104 | tf_op jit(solution)/shard_map/all_to_all | solution.py:400
  85.2 3.6 %update.1 = (f32[224,640]{1,0:T(8,128)}, f32[224,640]{1,0:T(8,128)}, f32[1,32]{1,0:T(1,128)}) custom-call(f32[256,128]{1,0:T(8,128)S(1)} %bitcast.13, s8[448,1024]{1,0:T(32,128)(4,1)S(1)} %get-tuple-element.38.left_ref, bf16[1024,1280]{1,0:T(8,128)(2,1)S(1)} %get-tuple-element.39.table_ref), custom_call_target="tpu_custom_call" | custom-call | flops 1200000000 | bytes 5000000 | tf_op jit(solution)/shard_map/update/pallas_call | solution.py:417
  (1 shorter events, 0.0 us)
Async XLA Ops:
  0.6 19.2 %copy-start.3 = (bf16[1024,224]{0,1:T(8,128)(2,1)S(1)}, bf16[1024,224]{0,1:T(8,128)(2,1)}, u32[]{:S(2)}) copy-start(bf16[1024,224]{0,1:T(8,128)(2,1)} %param.6) | copy-start | bytes 1376260
  0.6 19.2 %copy-start = (bf16[3584,640]{1,0:T(8,128)(2,1)S(1)}, bf16[3584,640]{1,0:T(8,128)(2,1)}, u32[]{:S(2)}) copy-start(bf16[3584,640]{1,0:T(8,128)(2,1)} %refs_3_.1) | copy-start | bytes 13762564
  0.6 11.5 %collective-permute-start.2 = (bf16[224,1024]{1,0:T(8,128)(2,1)}, bf16[224,1024]{1,0:T(8,128)(2,1)S(1)}, u32[]{:S(2)}, u32[]{:S(2)}) collective-permute-start(bf16[224,1024]{1,0:T(8,128)(2,1)} %bitcast.8), channel_id=1, source_target_pairs={{0,1},{1,2},{2,3},{3,0},{4,5},{5,6},{6,7},{7,4},{8,9},{9,10},{10,1... | collective-permute-start | bytes 1376264 | tf_op jit(solution)/shard_map/ppermute | solution.py:375
  2.8 11.9 %collective-permute-start = (bf16[224,1024]{1,0:T(8,128)(2,1)}, bf16[224,1024]{1,0:T(8,128)(2,1)S(1)}, u32[]{:S(2)}, u32[]{:S(2)}) collective-permute-start(bf16[224,1024]{1,0:T(8,128)(2,1)} %bitcast.9), channel_id=1, source_target_pairs={{0,12},{1,13},{2,14},{3,15},{4,0},{5,1},{6,2},{7,3},{8,4},{9,5},{1... | collective-permute-start | bytes 1376264 | tf_op jit(solution)/shard_map/ppermute | solution.py:375
  5.5 14.3 %collective-permute-start.7 = (bf16[224,1024]{1,0:T(8,128)(2,1)}, bf16[224,1024]{1,0:T(8,128)(2,1)S(1)}, u32[]{:S(2)}, u32[]{:S(2)}) collective-permute-start(bf16[224,1024]{1,0:T(8,128)(2,1)} %bitcast.10), channel_id=1, source_target_pairs={{0,4},{1,5},{2,6},{3,7},{4,8},{5,9},{6,10},{7,11},{8,12},{9,13},{1... | collective-permute-start | bytes 1376264 | tf_op jit(solution)/shard_map/ppermute | solution.py:375
  5.5 14.3 %collective-permute-start.6 = (bf16[224,1024]{1,0:T(8,128)(2,1)}, bf16[224,1024]{1,0:T(8,128)(2,1)S(1)}, u32[]{:S(2)}, u32[]{:S(2)}) collective-permute-start(bf16[224,1024]{1,0:T(8,128)(2,1)} %bitcast.11), channel_id=1, source_target_pairs={{0,3},{1,0},{2,1},{3,2},{4,7},{5,4},{6,5},{7,6},{8,11},{9,8},{10,9... | collective-permute-start | bytes 1376264 | tf_op jit(solution)/shard_map/ppermute | solution.py:375
  7.0 0.7 copy-start.5
  12.2 14.6 %collective-permute-start.3 = (bf16[224,1024]{1,0:T(8,128)(2,1)S(1)}, bf16[224,1024]{1,0:T(8,128)(2,1)S(1)}, u32[]{:S(2)}, u32[]{:S(2)}) collective-permute-start(bf16[224,1024]{1,0:T(8,128)(2,1)S(1)} %collective-permute-done.2.refs_1_), channel_id=1, source_target_pairs={{0,1},{1,2},{2,3},{3,0},{4,5},{5,6},{6,7},{7,4},{8,9},{9,10},{10,1... | collective-permute-start | bytes 1376264 | tf_op jit(solution)/shard_map/ppermute | solution.py:375
  14.7 14.8 %collective-permute-start.4 = (bf16[224,1024]{1,0:T(8,128)(2,1)S(1)}, bf16[224,1024]{1,0:T(8,128)(2,1)S(1)}, u32[]{:S(2)}, u32[]{:S(2)}) collective-permute-start(bf16[224,1024]{1,0:T(8,128)(2,1)S(1)} %collective-permute-done.refs_2_), channel_id=1, source_target_pairs={{0,3},{1,0},{2,1},{3,2},{4,7},{5,4},{6,5},{7,6},{8,11},{9,8},{10,9... | collective-permute-start | bytes 1376264 | tf_op jit(solution)/shard_map/ppermute | solution.py:375
  16.2 16.0 %collective-permute-start.1 = (bf16[224,1024]{1,0:T(8,128)(2,1)S(1)}, bf16[224,1024]{1,0:T(8,128)(2,1)S(1)}, u32[]{:S(2)}, u32[]{:S(2)}) collective-permute-start(bf16[224,1024]{1,0:T(8,128)(2,1)S(1)} %collective-permute-done.refs_2_), channel_id=1, source_target_pairs={{0,12},{1,13},{2,14},{3,15},{4,0},{5,1},{6,2},{7,3},{8,4},{9,5},{1... | collective-permute-start | bytes 1376264 | tf_op jit(solution)/shard_map/ppermute | solution.py:375
  19.8 12.4 %collective-permute-start.5 = (bf16[224,1024]{1,0:T(8,128)(2,1)S(1)}, bf16[224,1024]{1,0:T(8,128)(2,1)S(1)}, u32[]{:S(2)}, u32[]{:S(2)}) collective-permute-start(bf16[224,1024]{1,0:T(8,128)(2,1)S(1)} %collective-permute-done.2.refs_1_), channel_id=1, source_target_pairs={{0,4},{1,5},{2,6},{3,7},{4,8},{5,9},{6,10},{7,11},{8,12},{9,13},{1... | collective-permute-start | bytes 1376264 | tf_op jit(solution)/shard_map/ppermute | solution.py:375
  19.8 2.3 %copy-start.1 = (bf16[3584,640]{1,0:T(8,128)(2,1)S(1)}, bf16[3584,640]{1,0:T(8,128)(2,1)}, u32[]{:S(2)}) copy-start(bf16[3584,640]{1,0:T(8,128)(2,1)} %refs_4_.5) | copy-start | bytes 13762564
  26.8 10.1 %collective-permute-start.10 = (bf16[224,1024]{1,0:T(8,128)(2,1)S(1)}, bf16[224,1024]{1,0:T(8,128)(2,1)S(1)}, u32[]{:S(2)}, u32[]{:S(2)}) collective-permute-start(bf16[224,1024]{1,0:T(8,128)(2,1)S(1)} %collective-permute-done.3.refs_0_), channel_id=1, source_target_pairs={{0,12},{1,13},{2,14},{3,15},{4,0},{5,1},{6,2},{7,3},{8,4},{9,5},{1... | collective-permute-start | bytes 1376264 | tf_op jit(solution)/shard_map/ppermute | solution.py:375
  29.5 10.3 %collective-permute-start.12 = (bf16[224,1024]{1,0:T(8,128)(2,1)S(1)}, bf16[224,1024]{1,0:T(8,128)(2,1)S(1)}, u32[]{:S(2)}, u32[]{:S(2)}) collective-permute-start(bf16[224,1024]{1,0:T(8,128)(2,1)S(1)} %collective-permute-done.refs_2_), channel_id=1, source_target_pairs={{0,1},{1,2},{2,3},{3,0},{4,5},{5,6},{6,7},{7,4},{8,9},{9,10},{10,1... | collective-permute-start | bytes 1376264 | tf_op jit(solution)/shard_map/ppermute | solution.py:375
  29.5 11.0 %collective-permute-start.13 = (bf16[224,1024]{1,0:T(8,128)(2,1)S(1)}, bf16[224,1024]{1,0:T(8,128)(2,1)S(1)}, u32[]{:S(2)}, u32[]{:S(2)}) collective-permute-start(bf16[224,1024]{1,0:T(8,128)(2,1)S(1)} %collective-permute-done.7.refs_4_), channel_id=1, source_target_pairs={{0,3},{1,0},{2,1},{3,2},{4,7},{5,4},{6,5},{7,6},{8,11},{9,8},{10,9... | collective-permute-start | bytes 1376264 | tf_op jit(solution)/shard_map/ppermute | solution.py:375
  32.2 9.7 %collective-permute-start.14 = (bf16[224,1024]{1,0:T(8,128)(2,1)S(1)}, bf16[224,1024]{1,0:T(8,128)(2,1)S(1)}, u32[]{:S(2)}, u32[]{:S(2)}) collective-permute-start(bf16[224,1024]{1,0:T(8,128)(2,1)S(1)} %collective-permute-done.3.refs_0_), channel_id=1, source_target_pairs={{0,4},{1,5},{2,6},{3,7},{4,8},{5,9},{6,10},{7,11},{8,12},{9,13},{1... | collective-permute-start | bytes 1376264 | tf_op jit(solution)/shard_map/ppermute | solution.py:375
  32.2 18.5 %slice-start = ((s8[4587520]{0:T(1024)(128)(4,1)}), s8[4194304]{0:T(1024)(128)(4,1)S(1)}, s32[]{:S(2)}) async-start(s8[4587520]{0:T(1024)(128)(4,1)} %bitcast.6), calls=%async_computation.1 | async-start | bytes 8388608
  36.3 12.7 %collective-permute-start.9 = (bf16[224,1024]{1,0:T(8,128)(2,1)S(1)}, bf16[224,1024]{1,0:T(8,128)(2,1)S(1)}, u32[]{:S(2)}, u32[]{:S(2)}) collective-permute-start(bf16[224,1024]{1,0:T(8,128)(2,1)S(1)} %collective-permute-done.1.refs_1_), channel_id=1, source_target_pairs={{0,3},{1,0},{2,1},{3,2},{4,7},{5,4},{6,5},{7,6},{8,11},{9,8},{10,9... | collective-permute-start | bytes 1376264 | tf_op jit(solution)/shard_map/ppermute | solution.py:375
  36.9 13.8 %collective-permute-start.8 = (bf16[224,1024]{1,0:T(8,128)(2,1)S(1)}, bf16[224,1024]{1,0:T(8,128)(2,1)S(1)}, u32[]{:S(2)}, u32[]{:S(2)}) collective-permute-start(bf16[224,1024]{1,0:T(8,128)(2,1)S(1)} %collective-permute-done.1.refs_1_), channel_id=1, source_target_pairs={{0,1},{1,2},{2,3},{3,0},{4,5},{5,6},{6,7},{7,4},{8,9},{9,10},{10,1... | collective-permute-start | bytes 1376264 | tf_op jit(solution)/shard_map/ppermute | solution.py:375
  39.8 10.9 %collective-permute-start.11 = (bf16[224,1024]{1,0:T(8,128)(2,1)S(1)}, bf16[224,1024]{1,0:T(8,128)(2,1)S(1)}, u32[]{:S(2)}, u32[]{:S(2)}) collective-permute-start(bf16[224,1024]{1,0:T(8,128)(2,1)S(1)} %collective-permute-done.10.refs_1_), channel_id=1, source_target_pairs={{0,12},{1,13},{2,14},{3,15},{4,0},{5,1},{6,2},{7,3},{8,4},{9,5},{1... | collective-permute-start | bytes 1376264 | tf_op jit(solution)/shard_map/ppermute | solution.py:375
  41.9 8.8 %slice-start.1 = ((s8[4587520]{0:T(1024)(128)(4,1)}), s8[393216]{0:T(1024)(128)(4,1)S(1)}, s32[]{:S(2)}) async-start(s8[4587520]{0:T(1024)(128)(4,1)} %bitcast.6), calls=%async_computation.2 | async-start | bytes 786432
  41.9 8.8 %copy-start.2 = (bf16[1024,640]{1,0:T(8,128)(2,1)S(1)}, bf16[1024,640]{1,0:T(8,128)(2,1)}, u32[]{:S(2)}) copy-start(bf16[1024,640]{1,0:T(8,128)(2,1)} %refs_7_.1) | copy-start | bytes 3932164
  41.9 8.8 %copy-start.4 = (f32[640]{0:T(1024)S(1)}, f32[640]{0:T(1024)}, u32[]{:S(2)}) copy-start(f32[640]{0:T(1024)} %refs_8_.1) | copy-start | bytes 7684
  50.7 21.5 %copy-start.6 = (s32[256]{0:T(256)S(1)}, s32[256]{0:T(256)}, u32[]{:S(2)}) copy-start(s32[256]{0:T(256)} %seed_ref.3) | copy-start | bytes 3076
  57.3 27.9 %all-to-all-start = ((f32[256,1,128]{2,1,0:T(1,128)}), f32[256,1,128]{2,1,0:T(1,128)S(1)}, u32[]{:S(2)}, u32[]{:S(2)}) async-start(f32[256,1,128]{2,1,0:T(1,128)} %bitcast.2), calls=%async_computation | async-start | bytes 262144 | tf_op jit(solution)/shard_map/all_to_all | solution.py:400

commit v6 on v5

--- a/solution.py
+++ b/solution.py
@@ -14,13 +14,16 @@
 SEED_STEP = 747796405
 CELL_STEP = 277803737
 
+PASSED = (((0, 1),), ((0, 2), (3, 3), (1, 1)), ())
 WAYS = {"+x": (1, 0), "-x": (3, 0), "+y": (0, 1), "-y": (0, 3)}
 ROUNDS = (
     (((0, 0), "+x"), ((0, 0), "-y"), ((0, 0), "-x"), ((0, 0), "+y")),
     (((1, 0), "+x"), ((0, 3), "-y"), ((0, 3), "-x"), ((1, 0), "+y")),
     (((0, 3), "+x"), ((2, 0), "-y"), ((0, 1), "-x"), ((2, 0), "+y")),
-    (((0, 2), "+x"), ((0, 2), "-x"), ((2, 3), "-y")),
+    (((0, 2), "+x"), ((0, 2), "-x")),
 )
+HALVES = (((2, 3), (3, 3), "-y"), ((2, 1), (1, 1), "+y"))
+REST = 64
 
 
 def moved(place, way):
@@ -135,10 +138,13 @@
     return contract(tokens, jnp.concatenate(weights, axis=0))
 
 
-def round_kernel(places, fresh, *refs):
+def round_kernel(places, fresh, passed, *refs):
     n = len(places)
-    acc_ref, mark_ref = refs[-2:]
-    mark_ref[...] = jnp.zeros_like(mark_ref)
+    acc_ref, *handed = refs[len(refs) - 1 - len(passed) :]
+    for at, out_ref in zip(passed, handed):
+        count = out_ref.shape[0]
+        first = refs[at].shape[0] - REST if count == REST else 0
+        out_ref[...] = refs[at][first : first + count, :]
     tile = 512
 
     @pl.loop(0, acc_ref.shape[0] // tile)
@@ -151,19 +157,16 @@
             acc_ref[rows, :] = refs[n + 3][rows, :] + part
 
 
-def last_kernel(pieces, *refs):
-    n = len(pieces)
+def last_kernel(pieces, n, depth, *refs):
     blocks, weight_refs = refs[:n], refs[n : n + 3]
     acc_ref, target_ref, weight_ref, gate_out_ref, up_out_ref, message_ref = refs[n + 3 : n + 9]
     total_refs, side_refs, (parts_ref, turned_ref, low_ref) = refs[n + 9 : n + 11], refs[n + 11 : n + 13], refs[n + 13 :]
-    depth = blocks[0].shape[0]
     width = target_ref.shape[1]
     tile = 256
     tiles = acc_ref.shape[0] // tile
     scale = SIGMA / math.sqrt(16 * depth)
     features = [
-        pl.ds(pl.multiple_of(source_of(place) * depth + offset, 16), block.shape[0])
-        for (place, offset), block in zip(pieces, blocks)
+        pl.ds(pl.multiple_of(source_of(place) * depth + offset, 16), count) for place, offset, count in pieces
     ]
     lane_pair = lax.rem(iota((tile, 128), 1), 64) // 4
     row_pair = iota((tile, 128), 0) // ROWS
@@ -350,13 +353,17 @@
     )(seeds)
     weights = [gate_weight, up_weight, table]
 
-    def multiply(places, acc):
+    def multiply(places, acc, passed):
         given = [blocks[place] for place in places] + weights + ([] if acc is None else [acc])
+        outs = [jax.ShapeDtypeStruct((rows_dev, columns), f32)]
+        for place in passed:
+            whole = {ROUNDS[-1][0][0]: depth - REST, HALVES[0][1]: REST, HALVES[1][1]: REST}
+            outs.append(jax.ShapeDtypeStruct((whole.get(place, depth), rows_dev), bf16))
         return pl.pallas_call(
-            lambda *refs: round_kernel(places, acc is None, *refs),
-            out_shape=[jax.ShapeDtypeStruct((rows_dev, columns), f32), jax.ShapeDtypeStruct((8, 128), f32)],
+            lambda *refs: round_kernel(places, acc is None, [places.index(place) for place in passed], *refs),
+            out_shape=outs,
             in_specs=[in_vmem] * len(given),
-            out_specs=[in_vmem] * 2,
+            out_specs=[in_vmem] * len(outs),
             input_output_aliases={} if acc is None else {len(given) - 1: 0},
             compiler_params=params(12),
             cost_estimate=cost(2 * rows_dev * len(places) * depth * columns, 4_000_000),
@@ -364,25 +371,34 @@
         )(*given)
 
     blocks = {(0, 0): tokens.T}
-    acc, mark = None, gate_out
+    acc, given = None, {}
     held = [(0, 0)]
     for number, sends in enumerate(ROUNDS):
         fresh = {}
         for place, way in sends:
-            block = blocks[place]
-            if number > 0:
-                block = after(block, mark)
+            block = given.get(place, blocks[place])
+            if number == 1:
+                block = after(block, gate_out)
+            elif number == 2:
+                block = after(block, given[PASSED[0][0]])
             fresh[moved(place, way)] = lax.ppermute(block, "mp", pairs_of(way))
         if number > 0:
-            acc, mark = multiply(held, acc)
+            passed = PASSED[number - 1]
+            acc, *handed = multiply(held, acc, passed)
+            given.update(zip(passed, handed))
             held = []
         held += list(fresh)
         blocks.update(fresh)
 
+    half = depth // 2
     last = [blocks[place] for place in held]
-    pieces = [(place, 0) for place in held]
+    pieces = [(place, 0, depth - REST) for place in held]
+    for k, (place, other, way) in enumerate(HALVES):
+        both = [blocks[place][k * half : (k + 1) * half], given[other]]
+        last.append(lax.ppermute(jnp.concatenate(both, axis=0), "mp", pairs_of(way)))
+        pieces += [(moved(place, way), k * half, half), (moved(other, way), depth - REST, REST)]
     message = pl.pallas_call(
-        lambda *refs: last_kernel(pieces, *refs),
+        lambda *refs: last_kernel(pieces, len(last), depth, *refs),
         out_shape=jax.ShapeDtypeStruct((device_total, 128), f32),
         in_specs=[in_vmem] * (len(last) + 8),
         out_specs=in_vmem,

time: 89.1 us -> 86.5 us (0.971)
  waiting for transfers between devices: 18.4 us -> 14.4 us
  starting transfers between devices: 35.6 us -> 37.1 us
    ppermute x15 -> x14, waiting for transfers between devices: 10.5 us -> 6.54 us  [on_device(): fresh[moved(place, way)] = lax.ppermute(block, 'mp', pairs_of(way))]
    ppermute x0 -> x2, starting transfers between devices: none -> 2.29 us  [on_device(): lax.ppermute(jnp.concatenate(both, axis=0), 'mp', pairs_of(way))]
    all_to_all x1, starting transfers between devices: 14.9 us -> 14 us  [on_device(): received = lax.all_to_all(message, ('pop', 'mp'), 0, 0, tiled=True)]
    ppermute x15 -> x14, starting transfers between devices: 20.7 us -> 20.8 us  [on_device(): fresh[moved(place, way)] = lax.ppermute(block, 'mp', pairs_of(way))]
  transfers between devices with their start and end apart: 16 -> 17, of which waited for: 8 -> 6; matrix products, arithmetic and copies ran while one was open for 0% -> 0% of each run, Pallas kernels for 23% -> 24%
where the time goes in v6:
time: 86.5 us; the launch traced here: 86.3 us
  starting transfers between devices  37.1 us (43%)
  Pallas kernels  30.7 us (35%)
  waiting for transfers between devices  14.4 us (17%)
  local copies, waits for them, and re-layouts  3.04 us (4%)
  between operations  1.01 us (1%)
    ppermute x14, starting transfers between devices, on_device(): fresh[moved(place, way)] = lax.ppermute(block, 'mp', pairs_of(way))  20.8 us
    all_to_all x1, starting transfers between devices, on_device(): received = lax.all_to_all(message, ('pop', 'mp'), 0, 0, tiled=True)  14 us
    pallas_call x3, Pallas kernels, multiply(): pl.pallas_call(lambda *refs: round_kernel(places, acc is None, [places.in...  12.7 us
    all_to_all x1, waiting for transfers between devices, on_device(): received = lax.all_to_all(message, ('pop', 'mp'), 0, 0, tiled=True)  7.88 us
    ppermute x14, waiting for transfers between devices, on_device(): fresh[moved(place, way)] = lax.ppermute(block, 'mp', pairs_of(way))  6.54 us
    pallas_call x1, Pallas kernels, on_device(): pl.pallas_call(lambda *refs: last_kernel(pieces, len(last), depth, *refs)...  6.51 us
    pallas_call x1, Pallas kernels, on_device(): pl.pallas_call(factor_kernel, out_shape=[jax.ShapeDtypeStruct((2 * left_r...  5.11 us
    pallas_call x1, Pallas kernels, on_device(): pl.pallas_call(update_kernel, out_shape=[update, update, jax.ShapeDtypeSt...  3.62 us
  transfers between devices with their start and end apart: 17, of which 6 were waited for; matrix products, arithmetic and copies ran while one was open for 0% of the time, Pallas kernels for 24%

profile of v6, /device:TPU:1, one launch (start us, length us, event | category | flops | bytes accessed | tf_op | source)
XLA Modules:
  0.0 86.3 jit_solution(4166261932569601206)
XLA Ops:
  0.6 0.0 copy-start.3
  0.6 0.0 copy-start
  0.6 2.1 %collective-permute-start = (bf16[224,1024]{1,0:T(8,128)(2,1)}, bf16[224,1024]{1,0:T(8,128)(2,1)S(1)}, u32[]{:S(2)}, u32[]{:S(2)}) collective-permute-start(bf16[224,1024]{1,0:T(8,128)(2,1)} %bitcast.8), channel_id=1, source_target_pairs={{0,1},{1,2},{2,3},{3,0},{4,5},{5,6},{6,7},{7,4},{8,9},{9,10},{10,1... | collective-permute-start | bytes 1376264 | tf_op jit(solution)/shard_map/ppermute | solution.py:384
  2.8 2.7 %collective-permute-start.2 = (bf16[224,1024]{1,0:T(8,128)(2,1)}, bf16[224,1024]{1,0:T(8,128)(2,1)S(1)}, u32[]{:S(2)}, u32[]{:S(2)}) collective-permute-start(bf16[224,1024]{1,0:T(8,128)(2,1)} %bitcast.9), channel_id=1, source_target_pairs={{0,12},{1,13},{2,14},{3,15},{4,0},{5,1},{6,2},{7,3},{8,4},{9,5},{1... | collective-permute-start | bytes 1376264 | tf_op jit(solution)/shard_map/ppermute | solution.py:384
  5.5 0.0 collective-permute-start.7
  5.5 1.5 %collective-permute-start.6 = (bf16[224,1024]{1,0:T(8,128)(2,1)}, bf16[224,1024]{1,0:T(8,128)(2,1)S(1)}, u32[]{:S(2)}, u32[]{:S(2)}) collective-permute-start(bf16[224,1024]{1,0:T(8,128)(2,1)} %bitcast.11), channel_id=1, source_target_pairs={{0,3},{1,0},{2,1},{3,2},{4,7},{5,4},{6,5},{7,6},{8,11},{9,8},{10,9... | collective-permute-start | bytes 1376264 | tf_op jit(solution)/shard_map/ppermute | solution.py:384
  7.0 0.0 copy-start.5
  7.0 0.7 copy-done.5
  7.7 2.8 %prepare.1 = (bf16[3584,128]{1,0:T(8,128)(2,1)S(1)}, bf16[256,640]{1,0:T(8,128)(2,1)S(1)}, bf16[256,640]{1,0:T(8,128)(2,1)S(1)}) custom-call(s32[256]{0:T(256)S(1)} %copy-done.5), custom_call_target="tpu_custom_call" | custom-call | flops 2000000000 | bytes 2000000 | tf_op jit(solution)/shard_map/prepare/pallas_call | solution.py:345
  10.5 1.7 %collective-permute-done.refs_1_ = bf16[224,1024]{1,0:T(8,128)(2,1)S(1)} collective-permute-done((bf16[224,1024]{1,0:T(8,128)(2,1)}, bf16[224,1024]{1,0:T(8,128)(2,1)S(1)}, u32[]{:S(2)}, u32[]{:S(2)}) %collective-permute-start) | collective-permute-done | bytes 458784 | tf_op jit(solution)/shard_map/ppermute | solution.py:384
  12.2 1.9 %collective-permute-start.1 = (bf16[224,1024]{1,0:T(8,128)(2,1)S(1)}, bf16[224,1024]{1,0:T(8,128)(2,1)S(1)}, u32[]{:S(2)}, u32[]{:S(2)}) collective-permute-start(bf16[224,1024]{1,0:T(8,128)(2,1)S(1)} %collective-permute-done.refs_1_), channel_id=1, source_target_pairs={{0,1},{1,2},{2,3},{3,0},{4,5},{5,6},{6,7},{7,4},{8,9},{9,10},{10,1... | collective-permute-start | bytes 1376264 | tf_op jit(solution)/shard_map/ppermute | solution.py:384
  14.1 1.6 %collective-permute-start.5 = (bf16[224,1024]{1,0:T(8,128)(2,1)S(1)}, bf16[224,1024]{1,0:T(8,128)(2,1)S(1)}, u32[]{:S(2)}, u32[]{:S(2)}) collective-permute-start(bf16[224,1024]{1,0:T(8,128)(2,1)S(1)} %collective-permute-done.refs_1_), channel_id=1, source_target_pairs={{0,4},{1,5},{2,6},{3,7},{4,8},{5,9},{6,10},{7,11},{8,12},{9,13},{1... | collective-permute-start | bytes 1376264 | tf_op jit(solution)/shard_map/ppermute | solution.py:384
  15.7 0.0 collective-permute-done.2.refs_2_
  15.7 2.7 %collective-permute-start.4 = (bf16[224,1024]{1,0:T(8,128)(2,1)S(1)}, bf16[224,1024]{1,0:T(8,128)(2,1)S(1)}, u32[]{:S(2)}, u32[]{:S(2)}) collective-permute-start(bf16[224,1024]{1,0:T(8,128)(2,1)S(1)} %collective-permute-done.2.refs_2_), channel_id=1, source_target_pairs={{0,3},{1,0},{2,1},{3,2},{4,7},{5,4},{6,5},{7,6},{8,11},{9,8},{10,9... | collective-permute-start | bytes 1376264 | tf_op jit(solution)/shard_map/ppermute | solution.py:384
  18.3 0.0 collective-permute-done.7.refs_4_
  18.3 1.4 %collective-permute-start.3 = (bf16[224,1024]{1,0:T(8,128)(2,1)S(1)}, bf16[224,1024]{1,0:T(8,128)(2,1)S(1)}, u32[]{:S(2)}, u32[]{:S(2)}) collective-permute-start(bf16[224,1024]{1,0:T(8,128)(2,1)S(1)} %collective-permute-done.2.refs_2_), channel_id=1, source_target_pairs={{0,12},{1,13},{2,14},{3,15},{4,0},{5,1},{6,2},{7,3},{8,4},{9,5},{1... | collective-permute-start | bytes 1376264 | tf_op jit(solution)/shard_map/ppermute | solution.py:384
  19.8 0.0 collective-permute-done.6.refs_3_
  19.8 0.0 copy-done.3
  19.8 0.0 copy-done
  19.8 0.0 copy-start.1
  19.8 2.3 %copy-done.1 = bf16[3584,640]{1,0:T(8,128)(2,1)S(1)} copy-done((bf16[3584,640]{1,0:T(8,128)(2,1)S(1)}, bf16[3584,640]{1,0:T(8,128)(2,1)}, u32[]{:S(2)}) %copy-start.1) | copy-done | bytes 4587544
  22.1 4.5 %round_of_5.1 = (f32[1024,1408]{1,0:T(8,128)S(1)}, bf16[224,1024]{1,0:T(8,128)(2,1)S(1)}) custom-call(bf16[224,1024]{1,0:T(8,128)(2,1)S(1)} %bitcast.12, bf16[224,1024]{1,0:T(8,128)(2,1)S(1)} %collective-permute-done.refs_1_, bf16[224,1024]{1,0:T(8,128)(2,1)S(1)} %collective-permute-done.2.refs_2_, bf16[224,1024]{1,0:T(8,128)(2,1)S(1)} %collective-permute-done.6.refs_3_, ...), custom_call_target="tpu_custom_call" | custom-call | flops 3229614080 | bytes 4000000 | tf_op jit(solution)/shard_map/round_of_5/pallas_call | solution.py:362
  26.6 0.0 collective-permute-done.1.refs_0_
  26.6 0.7 collective-permute-start.12
  27.3 2.0 %collective-permute-start.10 = (bf16[224,1024]{1,0:T(8,128)(2,1)S(1)}, bf16[224,1024]{1,0:T(8,128)(2,1)S(1)}, u32[]{:S(2)}, u32[]{:S(2)}) collective-permute-start(bf16[224,1024]{1,0:T(8,128)(2,1)S(1)} %collective-permute-done.1.refs_0_), channel_id=1, source_target_pairs={{0,12},{1,13},{2,14},{3,15},{4,0},{5,1},{6,2},{7,3},{8,4},{9,5},{1... | collective-permute-start | bytes 1376264 | tf_op jit(solution)/shard_map/ppermute | solution.py:384
  29.4 0.0 collective-permute-done.5.refs_3_
  29.4 0.0 collective-permute-start.14
  29.4 0.0 collective-permute-done.4.refs_2_
  29.4 2.7 %collective-permute-start.15 = (bf16[224,1024]{1,0:T(8,128)(2,1)S(1)}, bf16[224,1024]{1,0:T(8,128)(2,1)S(1)}, u32[]{:S(2)}, u32[]{:S(2)}) collective-permute-start(bf16[224,1024]{1,0:T(8,128)(2,1)S(1)} %get-tuple-element.33), channel_id=1, source_target_pairs={{0,3},{1,0},{2,1},{3,2},{4,7},{5,4},{6,5},{7,6},{8,11},{9,8},{10,9... | collective-permute-start | bytes 1376264 | tf_op jit(solution)/shard_map/ppermute | solution.py:384
  32.0 0.0 collective-permute-done.3.refs_1_
  32.1 4.1 %round_of_4.2 = (f32[1024,1408]{1,0:T(8,128)S(1)}, bf16[160,1024]{1,0:T(8,128)(2,1)S(1)}, bf16[64,1024]{1,0:T(8,128)(2,1)S(1)}, bf16[64,1024]{1,0:T(8,128)(2,1)S(1)}) custom-call(bf16[224,1024]{1,0:T(8,128)(2,1)S(1)} %collective-permute-done.1.refs_0_, bf16[224,1024]{1,0:T(8,128)(2,1)S(1)} %collective-permute-done.3.refs_1_, ...), custom_call_target="tpu_custom_call", output_to_operand_aliasing={{0}: (7, {})} | custom-call | flops 2583691264 | bytes 4000000 | tf_op jit(solution)/shard_map/round_of_4/pallas_call | solution.py:362
  36.2 1.3 %collective-permute-done.12.refs_3_ = bf16[224,1024]{1,0:T(8,128)(2,1)S(1)} collective-permute-done((bf16[224,1024]{1,0:T(8,128)(2,1)S(1)}, bf16[224,1024]{1,0:T(8,128)(2,1)S(1)}, u32[]{:S(2)}, u32[]{:S(2)}) %collective-permute-start.12) | collective-permute-done | bytes 458784 | tf_op jit(solution)/shard_map/ppermute | solution.py:384
  37.6 0.1 collective-permute-start.13
  37.6 0.6 collective-permute-done.10.refs_1_
  38.3 0.0 slice-start
  38.3 2.2 %collective-permute-start.11 = (bf16[176,1024]{1,0:T(8,128)(2,1)S(1)}, bf16[176,1024]{1,0:T(8,128)(2,1)S(1)}, u32[]{:S(2)}, u32[]{:S(2)}) collective-permute-start(bf16[176,1024]{1,0:T(8,128)(2,1)S(1)} %pad_maximum_fusion), channel_id=1, source_target_pairs={{0,12},{1,13},{2,14},{3,15},{4,0},{5,1},{6,2},{7,3},{8,4},{9,5},{1... | collective-permute-start | bytes 1081352 | tf_op jit(solution)/shard_map/ppermute | solution.py:398
  40.6 0.9 %collective-permute-start.9 = (bf16[160,1024]{1,0:T(8,128)(2,1)S(1)}, bf16[160,1024]{1,0:T(8,128)(2,1)S(1)}, u32[]{:S(2)}, u32[]{:S(2)}) collective-permute-start(bf16[160,1024]{1,0:T(8,128)(2,1)S(1)} %get-tuple-element.27), channel_id=1, source_target_pairs={{0,3},{1,0},{2,1},{3,2},{4,7},{5,4},{6,5},{7,6},{8,11},{9,8},{10,9... | collective-permute-start | bytes 983048 | tf_op jit(solution)/shard_map/ppermute | solution.py:384
  41.5 0.0 collective-permute-done.14.refs_0_
  41.5 0.5 collective-permute-start.8
  42.0 0.0 collective-permute-done.15.refs_2_
  42.0 0.0 slice-start.1
  42.0 0.0 copy-start.2
  42.0 0.0 copy-start.4
  42.0 4.1 %round_of_4.3.refs_7_ = f32[1024,1408]{1,0:T(8,128)S(1)} custom-call(bf16[224,1024]{1,0:T(8,128)(2,1)S(1)} %collective-permute-done.14.refs_0_, bf16[224,1024]{1,0:T(8,128)(2,1)S(1)} %collective-permute-done.10.refs_1_, bf16[224,1024]{1,0:T(8,128)(2,1)S(1)} %collective-permute-done.15.refs_2_, ...), custom_call_target="tpu_custom_call", output_to_operand_aliasing={{}: (7, {})} | custom-call | flops 2583691264 | bytes 4000000 | tf_op jit(solution)/shard_map/round_of_4/pallas_call | solution.py:362
  46.1 0.7 collective-permute-done.9.refs_1_
  46.8 2.2 %collective-permute-done.8.refs_0_ = bf16[160,1024]{1,0:T(8,128)(2,1)S(1)} collective-permute-done((bf16[160,1024]{1,0:T(8,128)(2,1)S(1)}, bf16[160,1024]{1,0:T(8,128)(2,1)S(1)}, u32[]{:S(2)}, u32[]{:S(2)}) %collective-permute-start.8) | collective-permute-done | bytes 327712 | tf_op jit(solution)/shard_map/ppermute | solution.py:384
  48.9 0.0 collective-permute-done.13.refs_3_
  48.9 0.0 collective-permute-done.11.refs_2_
  48.9 0.0 slice-done
  48.9 0.0 slice-done.1
  49.0 0.0 copy-done.2
  49.0 0.0 copy-done.4
  49.0 0.0 copy-start.6
  49.0 6.5 %last_round.1.message_ref = f32[256,128]{1,0:T(8,128)} custom-call(bf16[160,1024]{1,0:T(8,128)(2,1)S(1)} %collective-permute-done.8.refs_0_, bf16[160,1024]{1,0:T(8,128)(2,1)S(1)} %collective-permute-done.9.refs_1_, bf16[176,1024]{1,0:T(8,128)(2,1)S(1)} %collective-permute-done.11.refs_2_, bf16[176,1024]{1,0:T(8,128)(2,1)S(1)} %collective-permute-done.13.refs_3_, ...), custom_call_target="tpu_custom_call" | custom-call | flops 1937768448 | bytes 12000000 | tf_op jit(solution)/shard_map/last_round/pallas_call | solution.py:400
  55.5 14.0 %all-to-all-start = ((f32[256,1,128]{2,1,0:T(1,128)}), f32[256,1,128]{2,1,0:T(1,128)S(1)}, u32[]{:S(2)}, u32[]{:S(2)}) async-start(f32[256,1,128]{2,1,0:T(1,128)} %bitcast.2), calls=%async_computation | async-start | bytes 262144 | tf_op jit(solution)/shard_map/all_to_all | solution.py:416
  69.5 0.0 copy-done.6
  69.5 5.1 %factor_tables.1 = (s8[448,1024]{1,0:T(32,128)(4,1)S(1)}, bf16[1024,1280]{1,0:T(8,128)(2,1)S(1)}) custom-call(s32[256]{0:T(256)S(1)} %copy-done.6, f32[256,128]{1,0:T(8,128)} %last_round.1.message_ref), custom_call_target="tpu_custom_call" | custom-call | flops 3000000000 | bytes 4000000 | tf_op jit(solution)/shard_map/factor_tables/pallas_call | solution.py:419
  74.6 7.9 %all-to-all-done = f32[256,1,128]{2,1,0:T(1,128)S(1)} async-done(((f32[256,1,128]{2,1,0:T(1,128)}), f32[256,1,128]{2,1,0:T(1,128)S(1)}, u32[]{:S(2)}, u32[]{:S(2)}) %all-to-all-start) | async-done | bytes 131104 | tf_op jit(solution)/shard_map/all_to_all | solution.py:416
  82.5 3.6 %update.1 = (f32[224,640]{1,0:T(8,128)}, f32[224,640]{1,0:T(8,128)}, f32[1,32]{1,0:T(1,128)}) custom-call(f32[256,128]{1,0:T(8,128)S(1)} %bitcast.13, s8[448,1024]{1,0:T(32,128)(4,1)S(1)} %get-tuple-element.36.left_ref, bf16[1024,1280]{1,0:T(8,128)(2,1)S(1)} %get-tuple-element.37.table_ref), custom_call_target="tpu_custom_call" | custom-call | flops 1200000000 | bytes 5000000 | tf_op jit(solution)/shard_map/update/pallas_call | solution.py:433
  (5 shorter events, 0.1 us)
Async XLA Ops:
  0.6 19.2 %copy-start.3 = (bf16[1024,224]{0,1:T(8,128)(2,1)S(1)}, bf16[1024,224]{0,1:T(8,128)(2,1)}, u32[]{:S(2)}) copy-start(bf16[1024,224]{0,1:T(8,128)(2,1)} %param.6) | copy-start | bytes 1376260
  0.6 19.2 %copy-start = (bf16[3584,640]{1,0:T(8,128)(2,1)S(1)}, bf16[3584,640]{1,0:T(8,128)(2,1)}, u32[]{:S(2)}) copy-start(bf16[3584,640]{1,0:T(8,128)(2,1)} %refs_4_.5) | copy-start | bytes 13762564
  0.6 11.5 %collective-permute-start = (bf16[224,1024]{1,0:T(8,128)(2,1)}, bf16[224,1024]{1,0:T(8,128)(2,1)S(1)}, u32[]{:S(2)}, u32[]{:S(2)}) collective-permute-start(bf16[224,1024]{1,0:T(8,128)(2,1)} %bitcast.8), channel_id=1, source_target_pairs={{0,1},{1,2},{2,3},{3,0},{4,5},{5,6},{6,7},{7,4},{8,9},{9,10},{10,1... | collective-permute-start | bytes 1376264 | tf_op jit(solution)/shard_map/ppermute | solution.py:384
  2.8 12.9 %collective-permute-start.2 = (bf16[224,1024]{1,0:T(8,128)(2,1)}, bf16[224,1024]{1,0:T(8,128)(2,1)S(1)}, u32[]{:S(2)}, u32[]{:S(2)}) collective-permute-start(bf16[224,1024]{1,0:T(8,128)(2,1)} %bitcast.9), channel_id=1, source_target_pairs={{0,12},{1,13},{2,14},{3,15},{4,0},{5,1},{6,2},{7,3},{8,4},{9,5},{1... | collective-permute-start | bytes 1376264 | tf_op jit(solution)/shard_map/ppermute | solution.py:384
  5.5 12.8 %collective-permute-start.7 = (bf16[224,1024]{1,0:T(8,128)(2,1)}, bf16[224,1024]{1,0:T(8,128)(2,1)S(1)}, u32[]{:S(2)}, u32[]{:S(2)}) collective-permute-start(bf16[224,1024]{1,0:T(8,128)(2,1)} %bitcast.10), channel_id=1, source_target_pairs={{0,4},{1,5},{2,6},{3,7},{4,8},{5,9},{6,10},{7,11},{8,12},{9,13},{1... | collective-permute-start | bytes 1376264 | tf_op jit(solution)/shard_map/ppermute | solution.py:384
  5.5 14.3 %collective-permute-start.6 = (bf16[224,1024]{1,0:T(8,128)(2,1)}, bf16[224,1024]{1,0:T(8,128)(2,1)S(1)}, u32[]{:S(2)}, u32[]{:S(2)}) collective-permute-start(bf16[224,1024]{1,0:T(8,128)(2,1)} %bitcast.11), channel_id=1, source_target_pairs={{0,3},{1,0},{2,1},{3,2},{4,7},{5,4},{6,5},{7,6},{8,11},{9,8},{10,9... | collective-permute-start | bytes 1376264 | tf_op jit(solution)/shard_map/ppermute | solution.py:384
  7.0 0.7 copy-start.5
  12.2 14.4 %collective-permute-start.1 = (bf16[224,1024]{1,0:T(8,128)(2,1)S(1)}, bf16[224,1024]{1,0:T(8,128)(2,1)S(1)}, u32[]{:S(2)}, u32[]{:S(2)}) collective-permute-start(bf16[224,1024]{1,0:T(8,128)(2,1)S(1)} %collective-permute-done.refs_1_), channel_id=1, source_target_pairs={{0,1},{1,2},{2,3},{3,0},{4,5},{5,6},{6,7},{7,4},{8,9},{9,10},{10,1... | collective-permute-start | bytes 1376264 | tf_op jit(solution)/shard_map/ppermute | solution.py:384
  14.1 15.3 %collective-permute-start.5 = (bf16[224,1024]{1,0:T(8,128)(2,1)S(1)}, bf16[224,1024]{1,0:T(8,128)(2,1)S(1)}, u32[]{:S(2)}, u32[]{:S(2)}) collective-permute-start(bf16[224,1024]{1,0:T(8,128)(2,1)S(1)} %collective-permute-done.refs_1_), channel_id=1, source_target_pairs={{0,4},{1,5},{2,6},{3,7},{4,8},{5,9},{6,10},{7,11},{8,12},{9,13},{1... | collective-permute-start | bytes 1376264 | tf_op jit(solution)/shard_map/ppermute | solution.py:384
  15.7 13.7 %collective-permute-start.4 = (bf16[224,1024]{1,0:T(8,128)(2,1)S(1)}, bf16[224,1024]{1,0:T(8,128)(2,1)S(1)}, u32[]{:S(2)}, u32[]{:S(2)}) collective-permute-start(bf16[224,1024]{1,0:T(8,128)(2,1)S(1)} %collective-permute-done.2.refs_2_), channel_id=1, source_target_pairs={{0,3},{1,0},{2,1},{3,2},{4,7},{5,4},{6,5},{7,6},{8,11},{9,8},{10,9... | collective-permute-start | bytes 1376264 | tf_op jit(solution)/shard_map/ppermute | solution.py:384
  18.3 13.7 %collective-permute-start.3 = (bf16[224,1024]{1,0:T(8,128)(2,1)S(1)}, bf16[224,1024]{1,0:T(8,128)(2,1)S(1)}, u32[]{:S(2)}, u32[]{:S(2)}) collective-permute-start(bf16[224,1024]{1,0:T(8,128)(2,1)S(1)} %collective-permute-done.2.refs_2_), channel_id=1, source_target_pairs={{0,12},{1,13},{2,14},{3,15},{4,0},{5,1},{6,2},{7,3},{8,4},{9,5},{1... | collective-permute-start | bytes 1376264 | tf_op jit(solution)/shard_map/ppermute | solution.py:384
  19.8 2.3 %copy-start.1 = (bf16[3584,640]{1,0:T(8,128)(2,1)S(1)}, bf16[3584,640]{1,0:T(8,128)(2,1)}, u32[]{:S(2)}) copy-start(bf16[3584,640]{1,0:T(8,128)(2,1)} %refs_5_.7) | copy-start | bytes 13762564
  26.6 10.9 %collective-permute-start.12 = (bf16[224,1024]{1,0:T(8,128)(2,1)S(1)}, bf16[224,1024]{1,0:T(8,128)(2,1)S(1)}, u32[]{:S(2)}, u32[]{:S(2)}) collective-permute-start(bf16[224,1024]{1,0:T(8,128)(2,1)S(1)} %collective-permute-done.1.refs_0_), channel_id=1, source_target_pairs={{0,4},{1,5},{2,6},{3,7},{4,8},{5,9},{6,10},{7,11},{8,12},{9,13},{1... | collective-permute-start | bytes 1376264 | tf_op jit(solution)/shard_map/ppermute | solution.py:384
  27.3 10.9 %collective-permute-start.10 = (bf16[224,1024]{1,0:T(8,128)(2,1)S(1)}, bf16[224,1024]{1,0:T(8,128)(2,1)S(1)}, u32[]{:S(2)}, u32[]{:S(2)}) collective-permute-start(bf16[224,1024]{1,0:T(8,128)(2,1)S(1)} %collective-permute-done.1.refs_0_), channel_id=1, source_target_pairs={{0,12},{1,13},{2,14},{3,15},{4,0},{5,1},{6,2},{7,3},{8,4},{9,5},{1... | collective-permute-start | bytes 1376264 | tf_op jit(solution)/shard_map/ppermute | solution.py:384
  29.4 12.1 %collective-permute-start.14 = (bf16[224,1024]{1,0:T(8,128)(2,1)S(1)}, bf16[224,1024]{1,0:T(8,128)(2,1)S(1)}, u32[]{:S(2)}, u32[]{:S(2)}) collective-permute-start(bf16[224,1024]{1,0:T(8,128)(2,1)S(1)} %collective-permute-done.2.refs_2_), channel_id=1, source_target_pairs={{0,1},{1,2},{2,3},{3,0},{4,5},{5,6},{6,7},{7,4},{8,9},{9,10},{10,1... | collective-permute-start | bytes 1376264 | tf_op jit(solution)/shard_map/ppermute | solution.py:384
  29.4 12.6 %collective-permute-start.15 = (bf16[224,1024]{1,0:T(8,128)(2,1)S(1)}, bf16[224,1024]{1,0:T(8,128)(2,1)S(1)}, u32[]{:S(2)}, u32[]{:S(2)}) collective-permute-start(bf16[224,1024]{1,0:T(8,128)(2,1)S(1)} %get-tuple-element.33), channel_id=1, source_target_pairs={{0,3},{1,0},{2,1},{3,2},{4,7},{5,4},{6,5},{7,6},{8,11},{9,8},{10,9... | collective-permute-start | bytes 1376264 | tf_op jit(solution)/shard_map/ppermute | solution.py:384
  37.6 11.4 %collective-permute-start.13 = (bf16[176,1024]{1,0:T(8,128)(2,1)S(1)}, bf16[176,1024]{1,0:T(8,128)(2,1)S(1)}, u32[]{:S(2)}, u32[]{:S(2)}) collective-permute-start(bf16[176,1024]{1,0:T(8,128)(2,1)S(1)} %pad_maximum_fusion.1), channel_id=1, source_target_pairs={{0,4},{1,5},{2,6},{3,7},{4,8},{5,9},{6,10},{7,11},{8,12},{9,13},{1... | collective-permute-start | bytes 1081352 | tf_op jit(solution)/shard_map/ppermute | solution.py:398
  38.3 10.6 %slice-start = ((s8[4587520]{0:T(1024)(128)(4,1)}), s8[4194304]{0:T(1024)(128)(4,1)S(1)}, s32[]{:S(2)}) async-start(s8[4587520]{0:T(1024)(128)(4,1)} %bitcast.6), calls=%async_computation.1 | async-start | bytes 8388608
  38.3 10.6 %collective-permute-start.11 = (bf16[176,1024]{1,0:T(8,128)(2,1)S(1)}, bf16[176,1024]{1,0:T(8,128)(2,1)S(1)}, u32[]{:S(2)}, u32[]{:S(2)}) collective-permute-start(bf16[176,1024]{1,0:T(8,128)(2,1)S(1)} %pad_maximum_fusion), channel_id=1, source_target_pairs={{0,12},{1,13},{2,14},{3,15},{4,0},{5,1},{6,2},{7,3},{8,4},{9,5},{1... | collective-permute-start | bytes 1081352 | tf_op jit(solution)/shard_map/ppermute | solution.py:398
  40.6 6.2 %collective-permute-start.9 = (bf16[160,1024]{1,0:T(8,128)(2,1)S(1)}, bf16[160,1024]{1,0:T(8,128)(2,1)S(1)}, u32[]{:S(2)}, u32[]{:S(2)}) collective-permute-start(bf16[160,1024]{1,0:T(8,128)(2,1)S(1)} %get-tuple-element.27), channel_id=1, source_target_pairs={{0,3},{1,0},{2,1},{3,2},{4,7},{5,4},{6,5},{7,6},{8,11},{9,8},{10,9... | collective-permute-start | bytes 983048 | tf_op jit(solution)/shard_map/ppermute | solution.py:384
  41.5 7.4 %collective-permute-start.8 = (bf16[160,1024]{1,0:T(8,128)(2,1)S(1)}, bf16[160,1024]{1,0:T(8,128)(2,1)S(1)}, u32[]{:S(2)}, u32[]{:S(2)}) collective-permute-start(bf16[160,1024]{1,0:T(8,128)(2,1)S(1)} %get-tuple-element.27), channel_id=1, source_target_pairs={{0,1},{1,2},{2,3},{3,0},{4,5},{5,6},{6,7},{7,4},{8,9},{9,10},{10,1... | collective-permute-start | bytes 983048 | tf_op jit(solution)/shard_map/ppermute | solution.py:384
  42.0 6.9 %slice-start.1 = ((s8[4587520]{0:T(1024)(128)(4,1)}), s8[393216]{0:T(1024)(128)(4,1)S(1)}, s32[]{:S(2)}) async-start(s8[4587520]{0:T(1024)(128)(4,1)} %bitcast.6), calls=%async_computation.2 | async-start | bytes 786432
  42.0 6.9 %copy-start.2 = (bf16[1024,640]{1,0:T(8,128)(2,1)S(1)}, bf16[1024,640]{1,0:T(8,128)(2,1)}, u32[]{:S(2)}) copy-start(bf16[1024,640]{1,0:T(8,128)(2,1)} %refs_8_.1) | copy-start | bytes 3932164
  42.0 6.9 %copy-start.4 = (f32[640]{0:T(1024)S(1)}, f32[640]{0:T(1024)}, u32[]{:S(2)}) copy-start(f32[640]{0:T(1024)} %refs_9_.1) | copy-start | bytes 7684
  49.0 20.5 %copy-start.6 = (s32[256]{0:T(256)S(1)}, s32[256]{0:T(256)}, u32[]{:S(2)}) copy-start(s32[256]{0:T(256)} %seed_ref.3) | copy-start | bytes 3076
  55.5 27.0 %all-to-all-start = ((f32[256,1,128]{2,1,0:T(1,128)}), f32[256,1,128]{2,1,0:T(1,128)S(1)}, u32[]{:S(2)}, u32[]{:S(2)}) async-start(f32[256,1,128]{2,1,0:T(1,128)} %bitcast.2), calls=%async_computation | async-start | bytes 262144 | tf_op jit(solution)/shard_map/all_to_all | solution.py:416

commit v7 on v6

--- a/solution.py
+++ b/solution.py
@@ -145,7 +145,7 @@
         count = out_ref.shape[0]
         first = refs[at].shape[0] - REST if count == REST else 0
         out_ref[...] = refs[at][first : first + count, :]
-    tile = 512
+    tile = 1024
 
     @pl.loop(0, acc_ref.shape[0] // tile)
     def _(i):
@@ -287,6 +287,16 @@
     fitness = (scores - center) / jnp.sqrt(jnp.full((16, 128), spread + EPSILON, jnp.float32))
     f_ref[...] = fitness
     factor = (fitness[:8] - fitness[8:]) * (0.5 / 16.0)
+    pop = lax.axis_index("pop")
+    mine = pop // 2
+    lane, member = iota((128, 128), 0), iota((128, 128), 1)
+    at = lane == lax.rem(pop, 2) * 64 + member // 2 * 4
+    total = jnp.zeros((1, 128), jnp.float32)
+    for s in range(2):
+        line = jnp.broadcast_to(f_ref[pl.ds(mine + 8 * s, 1), :], (8, 128))
+        select = (at & (lax.rem(member, 2) == s)).astype(jnp.float32)
+        total += jnp.dot(line, select, precision=lax.Precision.HIGHEST, preferred_element_type=jnp.float32)[:1]
+    fit_ref[...] = total[:, : fit_ref.shape[1]]
     copies = []
     for k, (out_ref, out) in enumerate(((out_gate_ref, out_gate), (out_up_ref, out_up))):
         highs, rests = [], []
@@ -303,16 +313,6 @@
         ) + jnp.dot(jnp.concatenate(rests, axis=1), right, preferred_element_type=jnp.float32)
         copies.append(pltpu.make_async_copy(out_ref, out, sems.at[k]))
         copies[-1].start()
-    pop = lax.axis_index("pop")
-    mine = pop // 2
-    lane, member = iota((128, 128), 0), iota((128, 128), 1)
-    at = lane == lax.rem(pop, 2) * 64 + member // 2 * 4
-    total = jnp.zeros((1, 128), jnp.float32)
-    for s in range(2):
-        line = jnp.broadcast_to(f_ref[pl.ds(mine + 8 * s, 1), :], (8, 128))
-        select = (at & (lax.rem(member, 2) == s)).astype(jnp.float32)
-        total += jnp.dot(line, select, precision=lax.Precision.HIGHEST, preferred_element_type=jnp.float32)[:1]
-    fit_ref[...] = total[:, : fit_ref.shape[1]]
     for copy in copies:
         copy.wait()
 

time: 86.5 us -> 86.3 us (level)
  Pallas kernels: 30.7 us -> 29.8 us
  transfers between devices with their start and end apart: 17 -> 17, of which waited for: 6 -> 6; matrix products, arithmetic and copies ran while one was open for 0% -> 0% of each run, Pallas kernels for 24% -> 23%
where the time goes in v7:
time: 86.3 us; the launch traced here: 86.1 us
  starting transfers between devices  37.1 us (43%)
  Pallas kernels  29.8 us (35%)
  waiting for transfers between devices  15 us (17%)
  local copies, waits for them, and re-layouts  3.04 us (4%)
  between operations  1.01 us (1%)
    ppermute x14, starting transfers between devices, on_device(): fresh[moved(place, way)] = lax.ppermute(block, 'mp', pairs_of(way))  20.8 us
    all_to_all x1, starting transfers between devices, on_device(): received = lax.all_to_all(message, ('pop', 'mp'), 0, 0, tiled=True)  13.8 us
    pallas_call x3, Pallas kernels, multiply(): pl.pallas_call(lambda *refs: round_kernel(places, acc is None, [places.in...  11.9 us
    all_to_all x1, waiting for transfers between devices, on_device(): received = lax.all_to_all(message, ('pop', 'mp'), 0, 0, tiled=True)  7.88 us
    ppermute x14, waiting for transfers between devices, on_device(): fresh[moved(place, way)] = lax.ppermute(block, 'mp', pairs_of(way))  7.16 us
    pallas_call x1, Pallas kernels, on_device(): pl.pallas_call(lambda *refs: last_kernel(pieces, len(last), depth, *refs)...  6.51 us
    pallas_call x1, Pallas kernels, on_device(): pl.pallas_call(factor_kernel, out_shape=[jax.ShapeDtypeStruct((2 * left_r...  5.11 us
    pallas_call x1, Pallas kernels, on_device(): pl.pallas_call(update_kernel, out_shape=[update, update, jax.ShapeDtypeSt...  3.56 us
  transfers between devices with their start and end apart: 17, of which 6 were waited for; matrix products, arithmetic and copies ran while one was open for 0% of the time, Pallas kernels for 23%

profile of v7, /device:TPU:1, one launch (start us, length us, event | category | flops | bytes accessed | tf_op | source)
XLA Modules:
  0.0 86.1 jit_solution(15950455655812649872)
XLA Ops:
  0.6 0.0 copy-start.3
  0.6 0.0 copy-start
  0.6 2.1 %collective-permute-start = (bf16[224,1024]{1,0:T(8,128)(2,1)}, bf16[224,1024]{1,0:T(8,128)(2,1)S(1)}, u32[]{:S(2)}, u32[]{:S(2)}) collective-permute-start(bf16[224,1024]{1,0:T(8,128)(2,1)} %bitcast.8), channel_id=1, source_target_pairs={{0,1},{1,2},{2,3},{3,0},{4,5},{5,6},{6,7},{7,4},{8,9},{9,10},{10,1... | collective-permute-start | bytes 1376264 | tf_op jit(solution)/shard_map/ppermute | solution.py:384
  2.8 2.7 %collective-permute-start.2 = (bf16[224,1024]{1,0:T(8,128)(2,1)}, bf16[224,1024]{1,0:T(8,128)(2,1)S(1)}, u32[]{:S(2)}, u32[]{:S(2)}) collective-permute-start(bf16[224,1024]{1,0:T(8,128)(2,1)} %bitcast.9), channel_id=1, source_target_pairs={{0,12},{1,13},{2,14},{3,15},{4,0},{5,1},{6,2},{7,3},{8,4},{9,5},{1... | collective-permute-start | bytes 1376264 | tf_op jit(solution)/shard_map/ppermute | solution.py:384
  5.5 0.0 collective-permute-start.7
  5.5 1.5 %collective-permute-start.6 = (bf16[224,1024]{1,0:T(8,128)(2,1)}, bf16[224,1024]{1,0:T(8,128)(2,1)S(1)}, u32[]{:S(2)}, u32[]{:S(2)}) collective-permute-start(bf16[224,1024]{1,0:T(8,128)(2,1)} %bitcast.11), channel_id=1, source_target_pairs={{0,3},{1,0},{2,1},{3,2},{4,7},{5,4},{6,5},{7,6},{8,11},{9,8},{10,9... | collective-permute-start | bytes 1376264 | tf_op jit(solution)/shard_map/ppermute | solution.py:384
  7.0 0.0 copy-start.5
  7.0 0.7 copy-done.5
  7.7 2.8 %prepare.1 = (bf16[3584,128]{1,0:T(8,128)(2,1)S(1)}, bf16[256,640]{1,0:T(8,128)(2,1)S(1)}, bf16[256,640]{1,0:T(8,128)(2,1)S(1)}) custom-call(s32[256]{0:T(256)S(1)} %copy-done.5), custom_call_target="tpu_custom_call" | custom-call | flops 2000000000 | bytes 2000000 | tf_op jit(solution)/shard_map/prepare/pallas_call | solution.py:345
  10.5 1.7 %collective-permute-done.refs_1_ = bf16[224,1024]{1,0:T(8,128)(2,1)S(1)} collective-permute-done((bf16[224,1024]{1,0:T(8,128)(2,1)}, bf16[224,1024]{1,0:T(8,128)(2,1)S(1)}, u32[]{:S(2)}, u32[]{:S(2)}) %collective-permute-start) | collective-permute-done | bytes 458784 | tf_op jit(solution)/shard_map/ppermute | solution.py:384
  12.2 1.9 %collective-permute-start.1 = (bf16[224,1024]{1,0:T(8,128)(2,1)S(1)}, bf16[224,1024]{1,0:T(8,128)(2,1)S(1)}, u32[]{:S(2)}, u32[]{:S(2)}) collective-permute-start(bf16[224,1024]{1,0:T(8,128)(2,1)S(1)} %collective-permute-done.refs_1_), channel_id=1, source_target_pairs={{0,1},{1,2},{2,3},{3,0},{4,5},{5,6},{6,7},{7,4},{8,9},{9,10},{10,1... | collective-permute-start | bytes 1376264 | tf_op jit(solution)/shard_map/ppermute | solution.py:384
  14.1 1.6 %collective-permute-start.5 = (bf16[224,1024]{1,0:T(8,128)(2,1)S(1)}, bf16[224,1024]{1,0:T(8,128)(2,1)S(1)}, u32[]{:S(2)}, u32[]{:S(2)}) collective-permute-start(bf16[224,1024]{1,0:T(8,128)(2,1)S(1)} %collective-permute-done.refs_1_), channel_id=1, source_target_pairs={{0,4},{1,5},{2,6},{3,7},{4,8},{5,9},{6,10},{7,11},{8,12},{9,13},{1... | collective-permute-start | bytes 1376264 | tf_op jit(solution)/shard_map/ppermute | solution.py:384
  15.7 0.0 collective-permute-done.2.refs_2_
  15.7 2.7 %collective-permute-start.4 = (bf16[224,1024]{1,0:T(8,128)(2,1)S(1)}, bf16[224,1024]{1,0:T(8,128)(2,1)S(1)}, u32[]{:S(2)}, u32[]{:S(2)}) collective-permute-start(bf16[224,1024]{1,0:T(8,128)(2,1)S(1)} %collective-permute-done.2.refs_2_), channel_id=1, source_target_pairs={{0,3},{1,0},{2,1},{3,2},{4,7},{5,4},{6,5},{7,6},{8,11},{9,8},{10,9... | collective-permute-start | bytes 1376264 | tf_op jit(solution)/shard_map/ppermute | solution.py:384
  18.3 0.0 collective-permute-done.7.refs_4_
  18.3 1.4 %collective-permute-start.3 = (bf16[224,1024]{1,0:T(8,128)(2,1)S(1)}, bf16[224,1024]{1,0:T(8,128)(2,1)S(1)}, u32[]{:S(2)}, u32[]{:S(2)}) collective-permute-start(bf16[224,1024]{1,0:T(8,128)(2,1)S(1)} %collective-permute-done.2.refs_2_), channel_id=1, source_target_pairs={{0,12},{1,13},{2,14},{3,15},{4,0},{5,1},{6,2},{7,3},{8,4},{9,5},{1... | collective-permute-start | bytes 1376264 | tf_op jit(solution)/shard_map/ppermute | solution.py:384
  19.8 0.0 collective-permute-done.6.refs_3_
  19.8 0.0 copy-done.3
  19.8 0.0 copy-done
  19.8 0.0 copy-start.1
  19.8 2.3 %copy-done.1 = bf16[3584,640]{1,0:T(8,128)(2,1)S(1)} copy-done((bf16[3584,640]{1,0:T(8,128)(2,1)S(1)}, bf16[3584,640]{1,0:T(8,128)(2,1)}, u32[]{:S(2)}) %copy-start.1) | copy-done | bytes 4587544
  22.1 4.2 %round_of_5.1 = (f32[1024,1408]{1,0:T(8,128)S(1)}, bf16[224,1024]{1,0:T(8,128)(2,1)S(1)}) custom-call(bf16[224,1024]{1,0:T(8,128)(2,1)S(1)} %bitcast.12, bf16[224,1024]{1,0:T(8,128)(2,1)S(1)} %collective-permute-done.refs_1_, bf16[224,1024]{1,0:T(8,128)(2,1)S(1)} %collective-permute-done.2.refs_2_, bf16[224,1024]{1,0:T(8,128)(2,1)S(1)} %collective-permute-done.6.refs_3_, ...), custom_call_target="tpu_custom_call" | custom-call | flops 3229614080 | bytes 4000000 | tf_op jit(solution)/shard_map/round_of_5/pallas_call | solution.py:362
  26.3 0.0 collective-permute-done.1.refs_0_
  26.3 1.0 %collective-permute-start.12 = (bf16[224,1024]{1,0:T(8,128)(2,1)S(1)}, bf16[224,1024]{1,0:T(8,128)(2,1)S(1)}, u32[]{:S(2)}, u32[]{:S(2)}) collective-permute-start(bf16[224,1024]{1,0:T(8,128)(2,1)S(1)} %collective-permute-done.1.refs_0_), channel_id=1, source_target_pairs={{0,4},{1,5},{2,6},{3,7},{4,8},{5,9},{6,10},{7,11},{8,12},{9,13},{1... | collective-permute-start | bytes 1376264 | tf_op jit(solution)/shard_map/ppermute | solution.py:384
  27.3 1.8 %collective-permute-start.10 = (bf16[224,1024]{1,0:T(8,128)(2,1)S(1)}, bf16[224,1024]{1,0:T(8,128)(2,1)S(1)}, u32[]{:S(2)}, u32[]{:S(2)}) collective-permute-start(bf16[224,1024]{1,0:T(8,128)(2,1)S(1)} %collective-permute-done.1.refs_0_), channel_id=1, source_target_pairs={{0,12},{1,13},{2,14},{3,15},{4,0},{5,1},{6,2},{7,3},{8,4},{9,5},{1... | collective-permute-start | bytes 1376264 | tf_op jit(solution)/shard_map/ppermute | solution.py:384
  29.1 0.0 collective-permute-done.5.refs_3_
  29.1 0.2 collective-permute-start.14
  29.3 0.0 collective-permute-done.4.refs_2_
  29.3 2.5 %collective-permute-start.15 = (bf16[224,1024]{1,0:T(8,128)(2,1)S(1)}, bf16[224,1024]{1,0:T(8,128)(2,1)S(1)}, u32[]{:S(2)}, u32[]{:S(2)}) collective-permute-start(bf16[224,1024]{1,0:T(8,128)(2,1)S(1)} %get-tuple-element.33), channel_id=1, source_target_pairs={{0,3},{1,0},{2,1},{3,2},{4,7},{5,4},{6,5},{7,6},{8,11},{9,8},{10,9... | collective-permute-start | bytes 1376264 | tf_op jit(solution)/shard_map/ppermute | solution.py:384
  31.8 0.0 collective-permute-done.3.refs_1_
  31.8 3.8 %round_of_4.2 = (f32[1024,1408]{1,0:T(8,128)S(1)}, bf16[160,1024]{1,0:T(8,128)(2,1)S(1)}, bf16[64,1024]{1,0:T(8,128)(2,1)S(1)}, bf16[64,1024]{1,0:T(8,128)(2,1)S(1)}) custom-call(bf16[224,1024]{1,0:T(8,128)(2,1)S(1)} %collective-permute-done.1.refs_0_, bf16[224,1024]{1,0:T(8,128)(2,1)S(1)} %collective-permute-done.3.refs_1_, ...), custom_call_target="tpu_custom_call", output_to_operand_aliasing={{0}: (7, {})} | custom-call | flops 2583691264 | bytes 4000000 | tf_op jit(solution)/shard_map/round_of_4/pallas_call | solution.py:362
  35.6 1.6 %collective-permute-done.12.refs_3_ = bf16[224,1024]{1,0:T(8,128)(2,1)S(1)} collective-permute-done((bf16[224,1024]{1,0:T(8,128)(2,1)S(1)}, bf16[224,1024]{1,0:T(8,128)(2,1)S(1)}, u32[]{:S(2)}, u32[]{:S(2)}) %collective-permute-start.12) | collective-permute-done | bytes 458784 | tf_op jit(solution)/shard_map/ppermute | solution.py:384
  37.3 0.1 collective-permute-start.13
  37.4 0.9 %collective-permute-done.10.refs_1_ = bf16[224,1024]{1,0:T(8,128)(2,1)S(1)} collective-permute-done((bf16[224,1024]{1,0:T(8,128)(2,1)S(1)}, bf16[224,1024]{1,0:T(8,128)(2,1)S(1)}, u32[]{:S(2)}, u32[]{:S(2)}) %collective-permute-start.10) | collective-permute-done | bytes 458784 | tf_op jit(solution)/shard_map/ppermute | solution.py:384
  38.3 0.0 slice-start
  38.3 2.5 %collective-permute-start.11 = (bf16[176,1024]{1,0:T(8,128)(2,1)S(1)}, bf16[176,1024]{1,0:T(8,128)(2,1)S(1)}, u32[]{:S(2)}, u32[]{:S(2)}) collective-permute-start(bf16[176,1024]{1,0:T(8,128)(2,1)S(1)} %pad_maximum_fusion), channel_id=1, source_target_pairs={{0,12},{1,13},{2,14},{3,15},{4,0},{5,1},{6,2},{7,3},{8,4},{9,5},{1... | collective-permute-start | bytes 1081352 | tf_op jit(solution)/shard_map/ppermute | solution.py:398
  40.8 0.9 %collective-permute-start.9 = (bf16[160,1024]{1,0:T(8,128)(2,1)S(1)}, bf16[160,1024]{1,0:T(8,128)(2,1)S(1)}, u32[]{:S(2)}, u32[]{:S(2)}) collective-permute-start(bf16[160,1024]{1,0:T(8,128)(2,1)S(1)} %get-tuple-element.27), channel_id=1, source_target_pairs={{0,3},{1,0},{2,1},{3,2},{4,7},{5,4},{6,5},{7,6},{8,11},{9,8},{10,9... | collective-permute-start | bytes 983048 | tf_op jit(solution)/shard_map/ppermute | solution.py:384
  41.7 0.0 collective-permute-done.14.refs_0_
  41.8 0.5 collective-permute-start.8
  42.3 0.0 collective-permute-done.15.refs_2_
  42.3 0.0 slice-start.1
  42.3 0.0 copy-start.2
  42.3 0.0 copy-start.4
  42.3 3.8 %round_of_4.3.refs_7_ = f32[1024,1408]{1,0:T(8,128)S(1)} custom-call(bf16[224,1024]{1,0:T(8,128)(2,1)S(1)} %collective-permute-done.14.refs_0_, bf16[224,1024]{1,0:T(8,128)(2,1)S(1)} %collective-permute-done.10.refs_1_, bf16[224,1024]{1,0:T(8,128)(2,1)S(1)} %collective-permute-done.15.refs_2_, ...), custom_call_target="tpu_custom_call", output_to_operand_aliasing={{}: (7, {})} | custom-call | flops 2583691264 | bytes 4000000 | tf_op jit(solution)/shard_map/round_of_4/pallas_call | solution.py:362
  46.1 0.9 %collective-permute-done.9.refs_1_ = bf16[160,1024]{1,0:T(8,128)(2,1)S(1)} collective-permute-done((bf16[160,1024]{1,0:T(8,128)(2,1)S(1)}, bf16[160,1024]{1,0:T(8,128)(2,1)S(1)}, u32[]{:S(2)}, u32[]{:S(2)}) %collective-permute-start.9) | collective-permute-done | bytes 327712 | tf_op jit(solution)/shard_map/ppermute | solution.py:384
  47.0 2.0 %collective-permute-done.8.refs_0_ = bf16[160,1024]{1,0:T(8,128)(2,1)S(1)} collective-permute-done((bf16[160,1024]{1,0:T(8,128)(2,1)S(1)}, bf16[160,1024]{1,0:T(8,128)(2,1)S(1)}, u32[]{:S(2)}, u32[]{:S(2)}) %collective-permute-start.8) | collective-permute-done | bytes 327712 | tf_op jit(solution)/shard_map/ppermute | solution.py:384
  49.0 0.0 collective-permute-done.13.refs_3_
  49.0 0.0 collective-permute-done.11.refs_2_
  49.0 0.0 slice-done
  49.0 0.0 slice-done.1
  49.0 0.0 copy-done.2
  49.0 0.0 copy-done.4
  49.1 0.0 copy-start.6
  49.1 6.5 %last_round.1.message_ref = f32[256,128]{1,0:T(8,128)} custom-call(bf16[160,1024]{1,0:T(8,128)(2,1)S(1)} %collective-permute-done.8.refs_0_, bf16[160,1024]{1,0:T(8,128)(2,1)S(1)} %collective-permute-done.9.refs_1_, bf16[176,1024]{1,0:T(8,128)(2,1)S(1)} %collective-permute-done.11.refs_2_, bf16[176,1024]{1,0:T(8,128)(2,1)S(1)} %collective-permute-done.13.refs_3_, ...), custom_call_target="tpu_custom_call" | custom-call | flops 1937768448 | bytes 12000000 | tf_op jit(solution)/shard_map/last_round/pallas_call | solution.py:400
  55.6 13.8 %all-to-all-start = ((f32[256,1,128]{2,1,0:T(1,128)}), f32[256,1,128]{2,1,0:T(1,128)S(1)}, u32[]{:S(2)}, u32[]{:S(2)}) async-start(f32[256,1,128]{2,1,0:T(1,128)} %bitcast.2), calls=%async_computation | async-start | bytes 262144 | tf_op jit(solution)/shard_map/all_to_all | solution.py:416
  69.4 0.0 copy-done.6
  69.4 5.1 %factor_tables.1 = (s8[448,1024]{1,0:T(32,128)(4,1)S(1)}, bf16[1024,1280]{1,0:T(8,128)(2,1)S(1)}) custom-call(s32[256]{0:T(256)S(1)} %copy-done.6, f32[256,128]{1,0:T(8,128)} %last_round.1.message_ref), custom_call_target="tpu_custom_call" | custom-call | flops 3000000000 | bytes 4000000 | tf_op jit(solution)/shard_map/factor_tables/pallas_call | solution.py:419
  74.5 7.9 %all-to-all-done = f32[256,1,128]{2,1,0:T(1,128)S(1)} async-done(((f32[256,1,128]{2,1,0:T(1,128)}), f32[256,1,128]{2,1,0:T(1,128)S(1)}, u32[]{:S(2)}, u32[]{:S(2)}) %all-to-all-start) | async-done | bytes 131104 | tf_op jit(solution)/shard_map/all_to_all | solution.py:416
  82.4 3.6 %update.1 = (f32[224,640]{1,0:T(8,128)}, f32[224,640]{1,0:T(8,128)}, f32[1,32]{1,0:T(1,128)}) custom-call(f32[256,128]{1,0:T(8,128)S(1)} %bitcast.13, s8[448,1024]{1,0:T(32,128)(4,1)S(1)} %get-tuple-element.36.left_ref, bf16[1024,1280]{1,0:T(8,128)(2,1)S(1)} %get-tuple-element.37.table_ref), custom_call_target="tpu_custom_call" | custom-call | flops 1200000000 | bytes 5000000 | tf_op jit(solution)/shard_map/update/pallas_call | solution.py:433
  (5 shorter events, 0.1 us)
Async XLA Ops:
  0.6 19.2 %copy-start.3 = (bf16[1024,224]{0,1:T(8,128)(2,1)S(1)}, bf16[1024,224]{0,1:T(8,128)(2,1)}, u32[]{:S(2)}) copy-start(bf16[1024,224]{0,1:T(8,128)(2,1)} %param.6) | copy-start | bytes 1376260
  0.6 19.2 %copy-start = (bf16[3584,640]{1,0:T(8,128)(2,1)S(1)}, bf16[3584,640]{1,0:T(8,128)(2,1)}, u32[]{:S(2)}) copy-start(bf16[3584,640]{1,0:T(8,128)(2,1)} %refs_4_.5) | copy-start | bytes 13762564
  0.6 11.5 %collective-permute-start = (bf16[224,1024]{1,0:T(8,128)(2,1)}, bf16[224,1024]{1,0:T(8,128)(2,1)S(1)}, u32[]{:S(2)}, u32[]{:S(2)}) collective-permute-start(bf16[224,1024]{1,0:T(8,128)(2,1)} %bitcast.8), channel_id=1, source_target_pairs={{0,1},{1,2},{2,3},{3,0},{4,5},{5,6},{6,7},{7,4},{8,9},{9,10},{10,1... | collective-permute-start | bytes 1376264 | tf_op jit(solution)/shard_map/ppermute | solution.py:384
  2.8 12.9 %collective-permute-start.2 = (bf16[224,1024]{1,0:T(8,128)(2,1)}, bf16[224,1024]{1,0:T(8,128)(2,1)S(1)}, u32[]{:S(2)}, u32[]{:S(2)}) collective-permute-start(bf16[224,1024]{1,0:T(8,128)(2,1)} %bitcast.9), channel_id=1, source_target_pairs={{0,12},{1,13},{2,14},{3,15},{4,0},{5,1},{6,2},{7,3},{8,4},{9,5},{1... | collective-permute-start | bytes 1376264 | tf_op jit(solution)/shard_map/ppermute | solution.py:384
  5.5 12.8 %collective-permute-start.7 = (bf16[224,1024]{1,0:T(8,128)(2,1)}, bf16[224,1024]{1,0:T(8,128)(2,1)S(1)}, u32[]{:S(2)}, u32[]{:S(2)}) collective-permute-start(bf16[224,1024]{1,0:T(8,128)(2,1)} %bitcast.10), channel_id=1, source_target_pairs={{0,4},{1,5},{2,6},{3,7},{4,8},{5,9},{6,10},{7,11},{8,12},{9,13},{1... | collective-permute-start | bytes 1376264 | tf_op jit(solution)/shard_map/ppermute | solution.py:384
  5.5 14.3 %collective-permute-start.6 = (bf16[224,1024]{1,0:T(8,128)(2,1)}, bf16[224,1024]{1,0:T(8,128)(2,1)S(1)}, u32[]{:S(2)}, u32[]{:S(2)}) collective-permute-start(bf16[224,1024]{1,0:T(8,128)(2,1)} %bitcast.11), channel_id=1, source_target_pairs={{0,3},{1,0},{2,1},{3,2},{4,7},{5,4},{6,5},{7,6},{8,11},{9,8},{10,9... | collective-permute-start | bytes 1376264 | tf_op jit(solution)/shard_map/ppermute | solution.py:384
  7.0 0.7 copy-start.5
  12.2 14.1 %collective-permute-start.1 = (bf16[224,1024]{1,0:T(8,128)(2,1)S(1)}, bf16[224,1024]{1,0:T(8,128)(2,1)S(1)}, u32[]{:S(2)}, u32[]{:S(2)}) collective-permute-start(bf16[224,1024]{1,0:T(8,128)(2,1)S(1)} %collective-permute-done.refs_1_), channel_id=1, source_target_pairs={{0,1},{1,2},{2,3},{3,0},{4,5},{5,6},{6,7},{7,4},{8,9},{9,10},{10,1... | collective-permute-start | bytes 1376264 | tf_op jit(solution)/shard_map/ppermute | solution.py:384
  14.1 15.0 %collective-permute-start.5 = (bf16[224,1024]{1,0:T(8,128)(2,1)S(1)}, bf16[224,1024]{1,0:T(8,128)(2,1)S(1)}, u32[]{:S(2)}, u32[]{:S(2)}) collective-permute-start(bf16[224,1024]{1,0:T(8,128)(2,1)S(1)} %collective-permute-done.refs_1_), channel_id=1, source_target_pairs={{0,4},{1,5},{2,6},{3,7},{4,8},{5,9},{6,10},{7,11},{8,12},{9,13},{1... | collective-permute-start | bytes 1376264 | tf_op jit(solution)/shard_map/ppermute | solution.py:384
  15.7 13.7 %collective-permute-start.4 = (bf16[224,1024]{1,0:T(8,128)(2,1)S(1)}, bf16[224,1024]{1,0:T(8,128)(2,1)S(1)}, u32[]{:S(2)}, u32[]{:S(2)}) collective-permute-start(bf16[224,1024]{1,0:T(8,128)(2,1)S(1)} %collective-permute-done.2.refs_2_), channel_id=1, source_target_pairs={{0,3},{1,0},{2,1},{3,2},{4,7},{5,4},{6,5},{7,6},{8,11},{9,8},{10,9... | collective-permute-start | bytes 1376264 | tf_op jit(solution)/shard_map/ppermute | solution.py:384
  18.3 13.4 %collective-permute-start.3 = (bf16[224,1024]{1,0:T(8,128)(2,1)S(1)}, bf16[224,1024]{1,0:T(8,128)(2,1)S(1)}, u32[]{:S(2)}, u32[]{:S(2)}) collective-permute-start(bf16[224,1024]{1,0:T(8,128)(2,1)S(1)} %collective-permute-done.2.refs_2_), channel_id=1, source_target_pairs={{0,12},{1,13},{2,14},{3,15},{4,0},{5,1},{6,2},{7,3},{8,4},{9,5},{1... | collective-permute-start | bytes 1376264 | tf_op jit(solution)/shard_map/ppermute | solution.py:384
  19.8 2.3 %copy-start.1 = (bf16[3584,640]{1,0:T(8,128)(2,1)S(1)}, bf16[3584,640]{1,0:T(8,128)(2,1)}, u32[]{:S(2)}) copy-start(bf16[3584,640]{1,0:T(8,128)(2,1)} %refs_5_.7) | copy-start | bytes 13762564
  26.3 10.9 %collective-permute-start.12 = (bf16[224,1024]{1,0:T(8,128)(2,1)S(1)}, bf16[224,1024]{1,0:T(8,128)(2,1)S(1)}, u32[]{:S(2)}, u32[]{:S(2)}) collective-permute-start(bf16[224,1024]{1,0:T(8,128)(2,1)S(1)} %collective-permute-done.1.refs_0_), channel_id=1, source_target_pairs={{0,4},{1,5},{2,6},{3,7},{4,8},{5,9},{6,10},{7,11},{8,12},{9,13},{1... | collective-permute-start | bytes 1376264 | tf_op jit(solution)/shard_map/ppermute | solution.py:384
  27.3 10.9 %collective-permute-start.10 = (bf16[224,1024]{1,0:T(8,128)(2,1)S(1)}, bf16[224,1024]{1,0:T(8,128)(2,1)S(1)}, u32[]{:S(2)}, u32[]{:S(2)}) collective-permute-start(bf16[224,1024]{1,0:T(8,128)(2,1)S(1)} %collective-permute-done.1.refs_0_), channel_id=1, source_target_pairs={{0,12},{1,13},{2,14},{3,15},{4,0},{5,1},{6,2},{7,3},{8,4},{9,5},{1... | collective-permute-start | bytes 1376264 | tf_op jit(solution)/shard_map/ppermute | solution.py:384
  29.1 12.7 %collective-permute-start.14 = (bf16[224,1024]{1,0:T(8,128)(2,1)S(1)}, bf16[224,1024]{1,0:T(8,128)(2,1)S(1)}, u32[]{:S(2)}, u32[]{:S(2)}) collective-permute-start(bf16[224,1024]{1,0:T(8,128)(2,1)S(1)} %collective-permute-done.2.refs_2_), channel_id=1, source_target_pairs={{0,1},{1,2},{2,3},{3,0},{4,5},{5,6},{6,7},{7,4},{8,9},{9,10},{10,1... | collective-permute-start | bytes 1376264 | tf_op jit(solution)/shard_map/ppermute | solution.py:384
  29.3 13.0 %collective-permute-start.15 = (bf16[224,1024]{1,0:T(8,128)(2,1)S(1)}, bf16[224,1024]{1,0:T(8,128)(2,1)S(1)}, u32[]{:S(2)}, u32[]{:S(2)}) collective-permute-start(bf16[224,1024]{1,0:T(8,128)(2,1)S(1)} %get-tuple-element.33), channel_id=1, source_target_pairs={{0,3},{1,0},{2,1},{3,2},{4,7},{5,4},{6,5},{7,6},{8,11},{9,8},{10,9... | collective-permute-start | bytes 1376264 | tf_op jit(solution)/shard_map/ppermute | solution.py:384
  37.3 11.7 %collective-permute-start.13 = (bf16[176,1024]{1,0:T(8,128)(2,1)S(1)}, bf16[176,1024]{1,0:T(8,128)(2,1)S(1)}, u32[]{:S(2)}, u32[]{:S(2)}) collective-permute-start(bf16[176,1024]{1,0:T(8,128)(2,1)S(1)} %pad_maximum_fusion.1), channel_id=1, source_target_pairs={{0,4},{1,5},{2,6},{3,7},{4,8},{5,9},{6,10},{7,11},{8,12},{9,13},{1... | collective-permute-start | bytes 1081352 | tf_op jit(solution)/shard_map/ppermute | solution.py:398
  38.3 10.7 %slice-start = ((s8[4587520]{0:T(1024)(128)(4,1)}), s8[4194304]{0:T(1024)(128)(4,1)S(1)}, s32[]{:S(2)}) async-start(s8[4587520]{0:T(1024)(128)(4,1)} %bitcast.6), calls=%async_computation.1 | async-start | bytes 8388608
  38.3 10.7 %collective-permute-start.11 = (bf16[176,1024]{1,0:T(8,128)(2,1)S(1)}, bf16[176,1024]{1,0:T(8,128)(2,1)S(1)}, u32[]{:S(2)}, u32[]{:S(2)}) collective-permute-start(bf16[176,1024]{1,0:T(8,128)(2,1)S(1)} %pad_maximum_fusion), channel_id=1, source_target_pairs={{0,12},{1,13},{2,14},{3,15},{4,0},{5,1},{6,2},{7,3},{8,4},{9,5},{1... | collective-permute-start | bytes 1081352 | tf_op jit(solution)/shard_map/ppermute | solution.py:398
  40.8 6.2 %collective-permute-start.9 = (bf16[160,1024]{1,0:T(8,128)(2,1)S(1)}, bf16[160,1024]{1,0:T(8,128)(2,1)S(1)}, u32[]{:S(2)}, u32[]{:S(2)}) collective-permute-start(bf16[160,1024]{1,0:T(8,128)(2,1)S(1)} %get-tuple-element.27), channel_id=1, source_target_pairs={{0,3},{1,0},{2,1},{3,2},{4,7},{5,4},{6,5},{7,6},{8,11},{9,8},{10,9... | collective-permute-start | bytes 983048 | tf_op jit(solution)/shard_map/ppermute | solution.py:384
  41.8 7.3 %collective-permute-start.8 = (bf16[160,1024]{1,0:T(8,128)(2,1)S(1)}, bf16[160,1024]{1,0:T(8,128)(2,1)S(1)}, u32[]{:S(2)}, u32[]{:S(2)}) collective-permute-start(bf16[160,1024]{1,0:T(8,128)(2,1)S(1)} %get-tuple-element.27), channel_id=1, source_target_pairs={{0,1},{1,2},{2,3},{3,0},{4,5},{5,6},{6,7},{7,4},{8,9},{9,10},{10,1... | collective-permute-start | bytes 983048 | tf_op jit(solution)/shard_map/ppermute | solution.py:384
  42.3 6.7 %slice-start.1 = ((s8[4587520]{0:T(1024)(128)(4,1)}), s8[393216]{0:T(1024)(128)(4,1)S(1)}, s32[]{:S(2)}) async-start(s8[4587520]{0:T(1024)(128)(4,1)} %bitcast.6), calls=%async_computation.2 | async-start | bytes 786432
  42.3 6.7 %copy-start.2 = (bf16[1024,640]{1,0:T(8,128)(2,1)S(1)}, bf16[1024,640]{1,0:T(8,128)(2,1)}, u32[]{:S(2)}) copy-start(bf16[1024,640]{1,0:T(8,128)(2,1)} %refs_8_.1) | copy-start | bytes 3932164
  42.3 6.7 %copy-start.4 = (f32[640]{0:T(1024)S(1)}, f32[640]{0:T(1024)}, u32[]{:S(2)}) copy-start(f32[640]{0:T(1024)} %refs_9_.1) | copy-start | bytes 7684
  49.1 20.3 %copy-start.6 = (s32[256]{0:T(256)S(1)}, s32[256]{0:T(256)}, u32[]{:S(2)}) copy-start(s32[256]{0:T(256)} %seed_ref.3) | copy-start | bytes 3076
  55.6 26.8 %all-to-all-start = ((f32[256,1,128]{2,1,0:T(1,128)}), f32[256,1,128]{2,1,0:T(1,128)S(1)}, u32[]{:S(2)}, u32[]{:S(2)}) async-start(f32[256,1,128]{2,1,0:T(1,128)} %bitcast.2), calls=%async_computation | async-start | bytes 262144 | tf_op jit(solution)/shard_map/all_to_all | solution.py:416
